TPU v7x, 256 devices: a whole 4x4x8 slice. The times are simulated.
256 devices in a mesh: row: 8 (over z), col: 16 (over y, x_lo, core), layer: 2 (over x_hi).
Axes of the slice: x: 4 (x_hi: 2, x_lo: 2; x = x_hi * 2 + x_lo), y: 4, z: 8, core: 2. Of those that a mesh axis runs over, the one named last changes fastest.
Arguments:
- slab_blocks: float32 [8, 16, 2, 16, 128, 128], P('row', 'col', 'layer'), may hold values from -0.5 to 0.5
- factor_blocks: float32 [8, 16, 2, 16, 1, 128, 128], P('row', 'col', 'layer'), may hold values from -6 to 6
- stack_left: int32 [8, 16, 2, 512], P('row', 'col', 'layer'), may hold values from 0 to 255
- stack_right: int32 [8, 16, 2, 512], P('row', 'col', 'layer'), may hold values from 0 to 127
- stack_target: int32 [8, 16, 2, 512], P('row', 'col', 'layer'), may hold values from 0 to 31
- stack_counts: int32 [8, 16, 2], P('row', 'col', 'layer'), may hold values from 1 to 512, as said below
Outputs:
- product_blocks: float32 [8, 16, 2, 16, 128, 128], P('row', 'col', 'layer')
Inputs may be any that keep to these rules, and one draw needn't show every extreme that they name: `stack_counts`: at most 512 listed products on one device; some device lists exactly 512 in every draw. Entries of a list beyond its count are not used.
All inputs are finite; a program needn't handle non-finite values.
Results may differ from a plain program's by a relative error of at most 0.0003.
Values sent between devices are 32-bit elements; how exact they have to be, the bound alone decides.
No kernel may reach another device: no remote copies, remote signals or barrier semaphores. Data moves between devices by JAX's collectives and lax.ppermute only.
A program may use at most 128 MiB of HBM per device.

v0:
```python
import jax
import jax.numpy as jnp
from jax import lax
from jax.sharding import PartitionSpec as P

SCH = 16
GROUP = 64


def body(slab_blocks, factor_blocks, stack_left, stack_right, stack_target, stack_counts):
    block_size = slab_blocks.shape[-1]
    panels = lax.all_gather(slab_blocks, "col", axis=1, tiled=True)
    left_store = panels.reshape(-1, block_size, block_size)
    arrived = lax.all_to_all(factor_blocks, "col", split_axis=3, concat_axis=1, tiled=True)
    owner_set = lax.all_gather(arrived, "row", axis=0, tiled=True)
    right_store = owner_set.reshape(-1, block_size, block_size)
    live_count = stack_counts.reshape(())
    left_index = stack_left.reshape(-1)
    right_index = stack_right.reshape(-1)
    target_index = stack_target.reshape(-1)
    layer_count = lax.axis_size("layer")
    n_target = layer_count * SCH

    def accumulate(turn, running):
        first_row = turn * GROUP
        take_left = lax.dynamic_slice_in_dim(left_index, first_row, GROUP)
        take_right = lax.dynamic_slice_in_dim(right_index, first_row, GROUP)
        take_target = lax.dynamic_slice_in_dim(target_index, first_row, GROUP)
        live_rows = first_row + jnp.arange(GROUP, dtype=jnp.int32) < live_count
        left_blocks = jnp.take(left_store, take_left, axis=0)
        right_blocks = jnp.take(right_store, take_right, axis=0)
        products = jnp.einsum(
            "pij,pkj->pik", left_blocks, right_blocks, precision=lax.Precision.HIGHEST
        )
        products = jnp.where(live_rows[:, None, None], products, jnp.zeros_like(products))
        return running + jax.ops.segment_sum(products, take_target, num_segments=n_target)

    groups = (live_count + GROUP - 1) // GROUP
    partial_value = lax.fori_loop(
        0, groups, accumulate, jnp.zeros((n_target, block_size, block_size), jnp.float32)
    )
    summed = lax.psum(partial_value, "layer")
    kept_blocks = lax.dynamic_slice_in_dim(summed, lax.axis_index("layer") * SCH, SCH, 0)
    return kept_blocks.reshape((1, 1, 1) + kept_blocks.shape)


def solution(mesh):
    return jax.shard_map(
        body,
        mesh=mesh,
        in_specs=(
            P("row", "col", "layer", None, None, None),
            P("row", "col", "layer", None, None, None, None),
            P("row", "col", "layer", None),
            P("row", "col", "layer", None),
            P("row", "col", "layer", None),
            P("row", "col", "layer"),
        ),
        out_specs=P("row", "col", "layer", None, None, None),
        check_vma=False,
    )
```

profile of v0, /device:TPU:34, one launch (start us, length us, event | category | flops | bytes accessed | tf_op | source)
XLA Modules:
  0.0 623.8 jit_solution(13709936136599101807)
XLA Ops:
  6.5 0.0 all-gather.6.cloned.1.call-start
  6.5 21.4 %all_to_all.12 = f32[1,1,1,16,1,128,128]{6,5,4,2,1,0,3:T(8,128)} all-to-all(f32[1,1,1,16,1,128,128]{6,5,4,2,1,0,3:T(8,128)} %bitcast.15), channel_id=1, replica_groups=mesh['row'=8,'col'=16,'layer'=2] {'col'}, dimensions={3} | all-to-all | bytes 2097152 | tf_op jit(solution)/shard_map/all_to_all | solution.py:14
  27.9 0.0 all-gather.6.cloned.1.call-update
  28.0 0.0 all-gather.4.cloned.1.call-start
  28.0 0.7 all-gather.4.cloned.1.call-update
  28.7 0.0 all-reduce.2.cloned.1.call-start
  29.4 91.7 %all-gather.6.cloned.1.call-done = f32[8,1,1,16,1,128,128]{6,5,4,3,2,1,0:T(8,128)} async-done(((f32[1,1,1,16,1,128,128]{6,5,4,3,2,1,0:T(8,128)}), f32[8,1,1,16,1,128,128]{6,5,4,3,2,1,0:T(8,128)}) %all-gather.6.cloned.1.call-update) | async-done | bytes 8388624 | tf_op jit(solution)/shard_map/all_gather | solution.py:15
  121.1 96.3 %all-gather.4.cloned.1.call-done = f32[1,16,1,16,128,128]{5,4,3,2,0,1:T(8,128)} async-done(((f32[1,1,1,16,128,128]{5,4,3,2,0,1:T(8,128)}), f32[1,16,1,16,128,128]{5,4,3,2,0,1:T(8,128)}) %all-gather.4.cloned.1.call-update) | async-done | bytes 16777232 | tf_op jit(solution)/shard_map/all_gather | solution.py:12
  217.4 0.2 broadcast.22
  217.6 80.2 %while.10 = (s32[]{:T(128)}, f32[32,128,128]{2,1,0:T(8,128)S(1)}, s32[]{:T(128)}, s32[512]{0:T(512)}, s32[]{:T(128)}, /*index=5*/s32[512]{0:T(512)}, f32[256,128...) while((s32[]{:T(128)}, f32[32,128,128]{2,1,0:T(8,128)S(1)}, ...), condition=%wide.region_2.3_spmd, body=%wide.region_0.2_spmd.sunk | while | flops 1614809984 | bytes 41954616 | solution.py:39
  217.6 0.8 compare_and_fusion.3
  218.4 6.2 gather_fusion
  224.6 8.5 %gather_fusion.1 = f32[64,128,128]{2,1,0:T(8,128)} fusion(f32[256,128,128]{2,1,0:T(8,128)} %get-tuple-element.174, s32[1024]{0:T(1024)S(1)} %pad_clamp_fusion.5), kind=kCustom, calls=%fused_computation.clone.1 | custom fusion | bytes 8388864 | tf_op jit(solution)/shard_map/while/body/jit(_take)/gather | solution.py:30
  233.1 0.7 add_compare_fusion.2
  233.8 14.4 %broadcast_select_fusion.2 = f32[64,128,128]{2,1,0:T(8,128)} fusion(f32[64,128,128]{2,1,0:T(8,128)} %gather_fusion, pred[64]{0:T(512)(128)(4,1)S(1)} %get-tuple-element.139, f32[64,128,128]{2,1,0:T(8,128)} %gather_fusion.1, pred[64]{0:T(512)(128)(4,1)S(1)} %get-tuple-element.141, pred[64]{0:T(512)(128)(4,1)S(1)} %add_compare_fusion.2), kind=kOutput, calls=%fused_computation.6.clone.1 | convolution fusion | flops 1613758464 | bytes 12583104 | tf_op jit(solution)/shard_map/while/body/pij,pkj->pik/dot_general | solution.py:32
  248.2 0.8 dynamic_slice.19
  248.9 8.8 %scatter_fusion = f32[32,128,128]{2,1,0:T(8,128)S(1)} fusion(f32[32,128,128]{2,1,0:T(8,128)S(1)} %get-tuple-element.156, s32[64]{0:T(128)S(1)} %dynamic_slice.19, f32[64,128,128]{2,1,0:T(8,128)} %broadcast_select_fusion.2), kind=kCustom, calls=%fused_computation.2.clone.1 | custom fusion | flops 1048576 | bytes 12583168 | tf_op jit(solution)/shard_map/while/body/scatter-add | solution.py:36
  257.7 0.8 compare_and_fusion.3
  258.5 6.2 gather_fusion
  264.7 8.5 %gather_fusion.1 = f32[64,128,128]{2,1,0:T(8,128)} fusion(f32[256,128,128]{2,1,0:T(8,128)} %get-tuple-element.174, s32[1024]{0:T(1024)S(1)} %pad_clamp_fusion.5), kind=kCustom, calls=%fused_computation.clone.1 | custom fusion | bytes 8388864 | tf_op jit(solution)/shard_map/while/body/jit(_take)/gather | solution.py:30
  273.2 0.7 add_compare_fusion.2
  273.9 14.4 %broadcast_select_fusion.2 = f32[64,128,128]{2,1,0:T(8,128)} fusion(f32[64,128,128]{2,1,0:T(8,128)} %gather_fusion, pred[64]{0:T(512)(128)(4,1)S(1)} %get-tuple-element.139, f32[64,128,128]{2,1,0:T(8,128)} %gather_fusion.1, pred[64]{0:T(512)(128)(4,1)S(1)} %get-tuple-element.141, pred[64]{0:T(512)(128)(4,1)S(1)} %add_compare_fusion.2), kind=kOutput, calls=%fused_computation.6.clone.1 | convolution fusion | flops 1613758464 | bytes 12583104 | tf_op jit(solution)/shard_map/while/body/pij,pkj->pik/dot_general | solution.py:32
  288.3 0.8 dynamic_slice.19
  289.0 8.8 %scatter_fusion = f32[32,128,128]{2,1,0:T(8,128)S(1)} fusion(f32[32,128,128]{2,1,0:T(8,128)S(1)} %get-tuple-element.156, s32[64]{0:T(128)S(1)} %dynamic_slice.19, f32[64,128,128]{2,1,0:T(8,128)} %broadcast_select_fusion.2), kind=kCustom, calls=%fused_computation.2.clone.1 | custom fusion | flops 1048576 | bytes 12583168 | tf_op jit(solution)/shard_map/while/body/scatter-add | solution.py:36
  297.8 0.0 copy-start
  297.8 1.3 copy-done
  299.1 0.0 all-reduce.2.cloned.1.call-update
  299.2 315.8 %all-reduce.2.cloned.1.call-done = f32[32,128,128]{2,1,0:T(8,128)} async-done(((f32[32,128,128]{2,1,0:T(8,128)}), f32[32,128,128]{2,1,0:T(8,128)}) %all-reduce.2.cloned.1.call-update) | async-done | bytes 2097168 | tf_op jit(solution)/shard_map/psum | solution.py:42
  615.0 2.3 dynamic-slice_bitcast_fusion
  (4 shorter events, 0.0 us)
Async XLA Ops:
  6.5 114.6 %all-gather.6.cloned.1.call-start = ((), (), s32[]{:S(2)}) async-start(), calls=%async_computation.3 | async-start | bytes 9437184 | tf_op jit(solution)/shard_map/all_gather | solution.py:15
  28.0 189.4 %all-gather.4.cloned.1.call-start = ((), (), s32[]{:S(2)}) async-start(), calls=%async_computation.1 | async-start | bytes 17825792 | tf_op jit(solution)/shard_map/all_gather | solution.py:12
  28.7 586.3 %all-reduce.2.cloned.1.call-start = ((), (), s32[]{:S(2)}) async-start(), calls=%async_computation.2 | async-start | bytes 4194304 | tf_op jit(solution)/shard_map/psum | solution.py:42
  297.8 1.3 copy-start
Sparse Core Ops, SparseCore 0:
  28.1 92.9 all-gather.5
  123.0 94.3 all-gather.3
  299.3 315.6 all-reduce.1
where the time goes:
time: 628 us; the launch traced here: 624 us
  waiting for transfers between devices  504 us (80%)
  local copies, waits for them, and re-layouts  34.7 us (6%)
  matrix products  28.8 us (5%)
  blocking collectives  21.4 us (3%)
  other arithmetic  20.5 us (3%)
  between operations  13.8 us (2%)
    psum x1, waiting for transfers between devices, body(): summed = lax.psum(partial_value, 'layer')  316 us
    all_gather x1, waiting for transfers between devices, body(): panels = lax.all_gather(slab_blocks, 'col', axis=1, tiled=True)  96.3 us
    all_gather x1, waiting for transfers between devices, body(): owner_set = lax.all_gather(arrived, 'row', axis=0, tiled=True)  91.7 us
    dot_general x2, matrix products, accumulate(): jnp.einsum('pij,pkj->pik', left_blocks, right_blocks, precision=lax.Preci...  28.8 us
    all_to_all x1, blocking collectives, body(): lax.all_to_all(factor_blocks, 'col', split_axis=3, concat_axis=1, tiled=T...  21.4 us
    scatter-add x2, other arithmetic, accumulate(): jax.ops.segment_sum(products, take_target, num_segments=n_target)  17.6 us
    gather x2, local copies, waits for them, and re-layouts, accumulate(): left_blocks = jnp.take(left_store, take_left, axis=0)  17 us
  transfers between devices with their start and end apart: 3, of which 3 were waited for; matrix products, arithmetic and copies ran while one was open for 0% of the time, Pallas kernels for 0%

commit v1 on v0

v1 whole, which is shorter than its diff:
```python
import jax
import jax.numpy as jnp
from jax import lax
from jax.experimental import pallas as pl
from jax.experimental.pallas import tpu as pltpu
from jax.sharding import Mesh
from jax.sharding import PartitionSpec as P

BS = 128
SA = 16
SCH = 16
N_ROW = 8
UNROLL = 4
TRANSPOSED = (((1,), (1,)), ((), ()))


def split(block):
    high = block.astype(jnp.bfloat16)
    low = (block - high.astype(jnp.float32)).astype(jnp.bfloat16)
    return high, low


def block_product(left, right):
    left_high, left_low = split(left)
    right_high, right_low = split(right)
    lhs = jnp.concatenate([left_high, left_high, left_low], axis=1)
    rhs = jnp.concatenate([right_high, right_low, right_high], axis=1)
    return lax.dot_general(lhs, rhs, TRANSPOSED, preferred_element_type=jnp.float32)


def multiply_kernel(where, left_index, right_index, target_index, left_own, left_other, *rest):
    pieces, (keep, send, left, right, total, load, store) = rest[:9], rest[9:]
    count, row, core, layer = where[0], where[1], where[2], where[3]
    half = left_own.shape[0]
    copies = [
        pltpu.make_async_copy(left_own, left.at[pl.ds(core * half, half)], load.at[0]),
        pltpu.make_async_copy(left_other, left.at[pl.ds((1 - core) * half, half)], load.at[1]),
    ]
    plan = [(0, 0, 16), (7, 0, 16), (1, 0, 16), (6, 0, 16), (2, 0, 16), (5, 0, 16), (3, 0, 16), (4, 0, 8), (4, 8, 8)]
    for position, (piece, (shift, first, length)) in enumerate(zip(pieces, plan)):
        start = lax.rem(row + shift, N_ROW) * SA + first
        copies.append(pltpu.make_async_copy(piece, right.at[pl.ds(start, length)], load.at[2 + position]))
    for copy in copies:
        copy.start()
    total[...] = jnp.zeros_like(total)
    for copy in copies:
        copy.wait()

    def accumulate(turn, carry):
        products, targets = [], []
        for step in range(UNROLL):
            p = turn * UNROLL + step
            live = p < count
            a = jnp.where(live, left_index[p], 0)
            b = jnp.where(live, right_index[p], 0)
            m = jnp.where(live, target_index[p], 0)
            column = a // SA
            place = lax.rem(column, 2) * half + (column // 2) * SA + lax.rem(a, SA)
            targets.append(jnp.where(live, lax.rem(m // SCH + layer, 2) * SCH + lax.rem(m, SCH), 2 * SCH))
            products.append(block_product(left[place], right[b]))
        for target, product in zip(targets, products):
            total[target] = total[target] + product
        return carry

    lax.fori_loop(0, (count + UNROLL - 1) // UNROLL, accumulate, 0)
    out_send = pltpu.make_async_copy(total.at[pl.ds(SCH, SCH)], send, store.at[0])
    out_keep = pltpu.make_async_copy(total.at[pl.ds(0, SCH)], keep, store.at[1])
    out_send.start()
    out_keep.start()
    out_send.wait()
    out_keep.wait()


def multiply(where, left_index, right_index, target_index, left_own, left_other, pieces):
    block = jax.ShapeDtypeStruct((SCH, BS, BS), jnp.float32)
    scalars = pl.BlockSpec(memory_space=pltpu.SMEM)
    whole = pl.BlockSpec(memory_space=pl.ANY)
    return pl.pallas_call(
        multiply_kernel,
        out_shape=(block, block),
        in_specs=[scalars] * 4 + [whole] * (2 + len(pieces)),
        out_specs=(whole, whole),
        scratch_shapes=[
            pltpu.VMEM((256, BS, BS), jnp.float32),
            pltpu.VMEM((128, BS, BS), jnp.float32),
            pltpu.VMEM((2 * SCH + 1, BS, BS), jnp.float32),
            pltpu.SemaphoreType.DMA((2 + len(pieces),)),
            pltpu.SemaphoreType.DMA((2,)),
        ],
        compiler_params=pltpu.CompilerParams(vmem_limit_bytes=40 << 20),
        cost_estimate=pl.CostEstimate(flops=512 * 6 * BS**3, bytes_accessed=26 << 20, transcendentals=0),
        name="multiply",
    )(where, left_index, right_index, target_index, left_own, left_other, *pieces)


def shift(value, axis, by):
    size = lax.axis_size(axis)
    return lax.ppermute(value, axis, [(i, (i + by) % size) for i in range(size)])


def body(slab_blocks, factor_blocks, stack_left, stack_right, stack_target, stack_counts):
    slab = slab_blocks.reshape(SA, BS, BS)
    left_own = lax.all_gather(slab, ("y", "x"), axis=0, tiled=True)
    left_other = shift(left_own, "core", 1)

    mine = lax.all_to_all(factor_blocks.reshape(SA, BS, BS), ("y", "x", "core"), split_axis=0, concat_axis=0, tiled=True)
    up = down = mine
    pieces = [mine]
    for _ in range(3):
        up, down = shift(up, "row", 1), shift(down, "row", -1)
        pieces += [up, down]
    pieces += [shift(up[:8], "row", 1), shift(down[8:], "row", -1)]

    where = jnp.stack(
        [stack_counts.reshape(()), lax.axis_index("row"), lax.axis_index("core"), lax.axis_index("layer")]
    ).astype(jnp.int32)
    keep, send = multiply(
        where,
        stack_left.reshape(-1),
        stack_right.reshape(-1),
        stack_target.reshape(-1),
        left_own,
        left_other,
        pieces,
    )
    summed = keep + shift(send, "layer", 1)
    return summed.reshape((1, 1, 1) + summed.shape)


def solution(mesh):
    fine = Mesh(mesh.devices.reshape(8, 4, 2, 2, 2), ("row", "y", "x", "core", "layer"))
    col = ("y", "x", "core")
    return jax.shard_map(
        body,
        mesh=fine,
        in_specs=(
            P("row", col, "layer", None, None, None),
            P("row", col, "layer", None, None, None, None),
            P("row", col, "layer", None),
            P("row", col, "layer", None),
            P("row", col, "layer", None),
            P("row", col, "layer"),
        ),
        out_specs=P("row", col, "layer", None, None, None),
        check_vma=False,
    )
```

time: 628 us -> 374 us (0.60)
  waiting for transfers between devices: 504 us -> 276 us
  starting transfers between devices: 0.08 us -> 39.1 us
  matrix products: 28.8 us -> 0 us
  local copies, waits for them, and re-layouts: 34.7 us -> 11.6 us
  other arithmetic: 20.5 us -> 1.18 us
  Pallas kernels: 0 us -> 7.92 us
    psum x1 -> x0, waiting for transfers between devices: 316 us -> none  [body(): summed = lax.psum(partial_value, 'layer')]
    ppermute x0 -> x10, waiting for transfers between devices: none -> 99.9 us  [shift(): lax.ppermute(value, axis, [(i, (i + by) % size) for i in range(size)])]
    ppermute x0 -> x10, starting transfers between devices: none -> 39.1 us  [shift(): lax.ppermute(value, axis, [(i, (i + by) % size) for i in range(size)])]
    gather x4 -> x0, local copies, waits for them, and re-layouts: 29.4 us -> none  [the longest x2 17 us: accumulate(): left_blocks = jnp.take(left_store, take_left, axis=0)]
    dot_general x2 -> x0, matrix products: 28.8 us -> none  [accumulate(): jnp.einsum('pij,pkj->pik', left_blocks, right_blocks, precision=lax.Preci...]
    scatter-add x2 -> x0, other arithmetic: 17.6 us -> none  [accumulate(): jax.ops.segment_sum(products, take_target, num_segments=n_target)]
    all_gather x2 -> x1, waiting for transfers between devices: 188 us -> 175 us  [body(): left_own = lax.all_gather(slab, ('y', 'x'), axis=0, tiled=True)]
    unnamed x2 -> x22, local copies, waits for them, and re-layouts: 1.31 us -> 9.91 us
  transfers between devices with their start and end apart: 3 -> 11, of which waited for: 3 -> 9; matrix products, arithmetic and copies ran while one was open for 0% -> 0% of each run, Pallas kernels for 0% -> 0%
where the time goes in v1:
time: 374 us; the launch traced here: 371 us
  waiting for transfers between devices  276 us (74%)
  starting transfers between devices  39.1 us (10%)
  blocking collectives  20.9 us (6%)
  between operations  14.1 us (4%)
  local copies, waits for them, and re-layouts  11.6 us (3%)
  Pallas kernels  7.92 us (2%)
    all_gather x1, waiting for transfers between devices, body(): left_own = lax.all_gather(slab, ('y', 'x'), axis=0, tiled=True)  175 us
    ppermute x10, waiting for transfers between devices, shift(): lax.ppermute(value, axis, [(i, (i + by) % size) for i in range(size)])  99.9 us
    ppermute x10, starting transfers between devices, shift(): lax.ppermute(value, axis, [(i, (i + by) % size) for i in range(size)])  39.1 us
    all_to_all x1, blocking collectives, body(): lax.all_to_all(factor_blocks.reshape(SA, BS, BS), ('y', 'x', 'core'), spl...  20.9 us
    unnamed x22, local copies, waits for them, and re-layouts  9.91 us
    pallas_call x1, Pallas kernels, multiply(): pl.pallas_call(multiply_kernel, out_shape=(block, block), in_specs=[scala...  7.92 us
  transfers between devices with their start and end apart: 11, of which 9 were waited for; matrix products, arithmetic and copies ran while one was open for 0% of the time, Pallas kernels for 0%

profile of v1, /device:TPU:34, one launch (start us, length us, event | category | flops | bytes accessed | tf_op | source)
XLA Modules:
  0.0 370.8 jit_solution(13643273556151112137)
XLA Ops:
  6.5 0.0 all-gather.3.cloned.1.call-start
  6.5 0.7 all-gather.3.cloned.1.call-update
  7.3 175.4 %all-gather.3.cloned.1.call-done = f32[1,1,1,128,128,128]{5,4,2,1,0,3:T(8,128)} async-done(((f32[1,1,1,16,128,128]{5,4,2,1,0,3:T(8,128)}), f32[1,1,1,128,128,128]{5,4,2,1,0,3:T(8,128)}) %all-gather.3.cloned.1.call-update) | async-done | bytes 8388624 | tf_op jit(solution)/shard_map/all_gather | solution.py:103
  182.7 0.0 collective-permute-start
  182.7 20.9 %all_to_all.5.rest_0_ = f32[16,128,128]{2,1,0:T(8,128)S(1)} all-to-all(f32[16,128,128]{2,1,0:T(8,128)} %bitcast.19), channel_id=1, replica_groups=mesh['row'=8,'y'=4,'x'=2,'core'=2,'layer'=2] {'y','x','core'}, dimensions={0} | all-to-all | bytes 2097152 | tf_op jit(solution)/shard_map/all_to_all | solution.py:106
  203.6 0.5 collective-permute-start.2
  204.1 1.6 collective-permute-start.1
  205.6 23.2 %collective-permute-done.2.rest_2_ = f32[16,128,128]{2,1,0:T(8,128)S(1)} collective-permute-done((f32[16,128,128]{2,1,0:T(8,128)S(1)}, f32[16,128,128]{2,1,0:T(8,128)S(1)}, u32[]{:S(2)}, u32[]{:S(2)}) %collective-permute-start.2) | collective-permute-done | bytes 1048608 | tf_op jit(solution)/shard_map/ppermute | solution.py:98
  228.8 1.3 collective-permute-start.4
  230.1 0.0 copy-start
  230.1 1.0 copy-done
  231.1 0.0 collective-permute-done.1.rest_1_
  231.1 0.7 collective-permute-start.3
  231.8 0.0 copy-start.2
  231.8 1.0 copy-done.2
  232.8 20.3 %collective-permute-done.4.rest_4_ = f32[16,128,128]{2,1,0:T(8,128)S(1)} collective-permute-done((f32[16,128,128]{2,1,0:T(8,128)S(1)}, f32[16,128,128]{2,1,0:T(8,128)S(1)}, u32[]{:S(2)}, u32[]{:S(2)}) %collective-permute-start.4) | collective-permute-done | bytes 1048608 | tf_op jit(solution)/shard_map/ppermute | solution.py:98
  253.1 2.5 collective-permute-start.6
  255.7 0.0 copy-start.4
  255.7 1.0 copy-done.4
  256.7 0.5 collective-permute-done.3.rest_3_
  257.1 0.0 copy-start.6
  257.1 0.0 collective-permute-start.5
  257.1 20.6 %collective-permute-done.6.rest_6_ = f32[16,128,128]{2,1,0:T(8,128)S(1)} collective-permute-done((f32[16,128,128]{2,1,0:T(8,128)S(1)}, f32[16,128,128]{2,1,0:T(8,128)S(1)}, u32[]{:S(2)}, u32[]{:S(2)}) %collective-permute-start.6) | collective-permute-done | bytes 1048608 | tf_op jit(solution)/shard_map/ppermute | solution.py:98
  277.7 0.8 slice.9
  278.5 2.6 collective-permute-start.8
  281.1 0.6 collective-permute-done.5.rest_5_
  281.8 0.0 copy-done.6
  281.8 0.8 slice.8
  282.6 0.0 collective-permute-start.7
  283.3 0.1 pad_add_fusion.where
  283.3 8.0 %collective-permute-done.8.rest_8_ = f32[8,128,128]{2,1,0:T(8,128)} collective-permute-done((f32[8,128,128]{2,1,0:T(8,128)}, f32[8,128,128]{2,1,0:T(8,128)}, u32[]{:S(2)}, u32[]{:S(2)}) %collective-permute-start.8) | collective-permute-done | bytes 524320 | tf_op jit(solution)/shard_map/ppermute | solution.py:98
  291.3 3.9 %collective-permute-done.7.rest_7_ = f32[8,128,128]{2,1,0:T(8,128)} collective-permute-done((f32[8,128,128]{2,1,0:T(8,128)}, f32[8,128,128]{2,1,0:T(8,128)}, u32[]{:S(2)}, u32[]{:S(2)}) %collective-permute-start.7) | collective-permute-done | bytes 524320 | tf_op jit(solution)/shard_map/ppermute | solution.py:98
  295.2 0.0 collective-permute-done.left_other
  295.2 0.0 copy-start.1
  295.2 1.2 copy-done.1
  296.5 0.0 copy-start.3
  296.5 1.2 copy-done.3
  297.7 0.0 copy-start.5
  297.7 1.2 copy-done.5
  298.9 0.0 copy-start.7
  298.9 1.2 copy-done.7
  300.1 0.0 copy-start.8
  300.1 0.7 copy-done.8
  300.8 0.0 copy-start.9
  300.8 0.7 copy-done.9
  301.5 0.0 copy-start.10
  301.5 0.7 copy-done.10
  302.2 7.9 %multiply.1 = (f32[16,128,128]{2,1,0:T(8,128)S(1)}, f32[16,128,128]{2,1,0:T(8,128)S(1)}) custom-call(s32[4]{0:T(128)S(1)} %pad_add_fusion.where, s32[512]{0:T(512)S(1)} %bitcast.13, s32[512]{0:T(512)S(1)} %bitcast.14, s32[512]{0:T(512)S(1)} %bitcast.15, f32[128,128,128]{2,1,0:T(8,128)} %bitcast.17, f32[128,128,128]{2,1,0:T(8,128)} %collective-permute-done.left_other, ...), custom_call_target="tpu_custom_call" | custom-call | flops 6442450944 | bytes 27262976 | tf_op jit(solution)/shard_map/multiply/pallas_call | solution.py:78
  310.1 29.9 %collective-permute-start.9 = (f32[16,128,128]{2,1,0:T(8,128)S(1)}, f32[16,128,128]{2,1,0:T(8,128)S(1)}, u32[]{:S(2)}, u32[]{:S(2)}) collective-permute-start(f32[16,128,128]{2,1,0:T(8,128)S(1)} %get-tuple-element.8), channel_id=1, source_target_pairs={{0,1},{1,0},{2,3},{3,2},{4,5},{5,4},{6,7},{7,6},{8,9},{9,8},{10,11... | collective-permute-start | bytes 3145736 | tf_op jit(solution)/shard_map/ppermute | solution.py:98
  340.0 22.9 %collective-permute-done.9 = f32[16,128,128]{2,1,0:T(8,128)S(1)} collective-permute-done((f32[16,128,128]{2,1,0:T(8,128)S(1)}, f32[16,128,128]{2,1,0:T(8,128)S(1)}, u32[]{:S(2)}, u32[]{:S(2)}) %collective-permute-start.9) | collective-permute-done | bytes 1048608 | tf_op jit(solution)/shard_map/ppermute | solution.py:98
  362.9 1.1 add_bitcast_fusion
Async XLA Ops:
  6.5 176.1 %all-gather.3.cloned.1.call-start = ((), (), s32[]{:S(2)}) async-start(), calls=%async_computation.1 | async-start | bytes 9437184 | tf_op jit(solution)/shard_map/all_gather | solution.py:103
  182.7 112.6 %collective-permute-start = (f32[128,128,128]{2,1,0:T(8,128)}, f32[128,128,128]{2,1,0:T(8,128)}, u32[]{:S(2)}, u32[]{:S(2)}) collective-permute-start(f32[128,128,128]{2,1,0:T(8,128)} %bitcast.16), channel_id=1, source_target_pairs={{0,2},{2,0},{1,3},{3,1},{4,6},{6,4},{5,7},{7,5},{8,10},{10,8},{9,1... | collective-permute-start | bytes 25165832 | tf_op jit(solution)/shard_map/ppermute | solution.py:98
  203.6 25.2 %collective-permute-start.2 = (f32[16,128,128]{2,1,0:T(8,128)S(1)}, f32[16,128,128]{2,1,0:T(8,128)S(1)}, u32[]{:S(2)}, u32[]{:S(2)}) collective-permute-start(f32[16,128,128]{2,1,0:T(8,128)S(1)} %all_to_all.5.rest_0_), channel_id=1, source_target_pairs={{0,224},{32,0},{64,32},{96,64},{128,96},{160,128},{192,160},{224,1... | collective-permute-start | bytes 3145736 | tf_op jit(solution)/shard_map/ppermute | solution.py:98
  204.1 27.0 %collective-permute-start.1 = (f32[16,128,128]{2,1,0:T(8,128)S(1)}, f32[16,128,128]{2,1,0:T(8,128)S(1)}, u32[]{:S(2)}, u32[]{:S(2)}) collective-permute-start(f32[16,128,128]{2,1,0:T(8,128)S(1)} %all_to_all.5.rest_0_), channel_id=1, source_target_pairs={{0,32},{32,64},{64,96},{96,128},{128,160},{160,192},{192,224},{224... | collective-permute-start | bytes 3145736 | tf_op jit(solution)/shard_map/ppermute | solution.py:98
  228.8 24.3 %collective-permute-start.4 = (f32[16,128,128]{2,1,0:T(8,128)S(1)}, f32[16,128,128]{2,1,0:T(8,128)S(1)}, u32[]{:S(2)}, u32[]{:S(2)}) collective-permute-start(f32[16,128,128]{2,1,0:T(8,128)S(1)} %collective-permute-done.2.rest_2_), channel_id=1, source_target_pairs={{0,224},{32,0},{64,32},{96,64},{128,96},{160,128},{192,160},{224,1... | collective-permute-start | bytes 3145736 | tf_op jit(solution)/shard_map/ppermute | solution.py:98
  230.1 1.0 copy-start
  231.1 26.0 %collective-permute-start.3 = (f32[16,128,128]{2,1,0:T(8,128)S(1)}, f32[16,128,128]{2,1,0:T(8,128)S(1)}, u32[]{:S(2)}, u32[]{:S(2)}) collective-permute-start(f32[16,128,128]{2,1,0:T(8,128)S(1)} %collective-permute-done.1.rest_1_), channel_id=1, source_target_pairs={{0,32},{32,64},{64,96},{96,128},{128,160},{160,192},{192,224},{224... | collective-permute-start | bytes 3145736 | tf_op jit(solution)/shard_map/ppermute | solution.py:98
  231.8 1.0 copy-start.2
  253.1 24.5 %collective-permute-start.6 = (f32[16,128,128]{2,1,0:T(8,128)S(1)}, f32[16,128,128]{2,1,0:T(8,128)S(1)}, u32[]{:S(2)}, u32[]{:S(2)}) collective-permute-start(f32[16,128,128]{2,1,0:T(8,128)S(1)} %collective-permute-done.4.rest_4_), channel_id=1, source_target_pairs={{0,224},{32,0},{64,32},{96,64},{128,96},{160,128},{192,160},{224,1... | collective-permute-start | bytes 3145736 | tf_op jit(solution)/shard_map/ppermute | solution.py:98
  255.7 1.0 copy-start.4
  257.1 24.6 %copy-start.6 = (f32[16,128,128]{2,1,0:T(8,128)}, f32[16,128,128]{2,1,0:T(8,128)S(1)}, u32[]{:S(2)}) copy-start(f32[16,128,128]{2,1,0:T(8,128)S(1)} %collective-permute-done.3.rest_3_) | copy-start | bytes 3145732
  257.1 24.6 %collective-permute-start.5 = (f32[16,128,128]{2,1,0:T(8,128)S(1)}, f32[16,128,128]{2,1,0:T(8,128)S(1)}, u32[]{:S(2)}, u32[]{:S(2)}) collective-permute-start(f32[16,128,128]{2,1,0:T(8,128)S(1)} %collective-permute-done.3.rest_3_), channel_id=1, source_target_pairs={{0,32},{32,64},{64,96},{96,128},{128,160},{160,192},{192,224},{224... | collective-permute-start | bytes 3145736 | tf_op jit(solution)/shard_map/ppermute | solution.py:98
  278.5 12.8 %collective-permute-start.8 = (f32[8,128,128]{2,1,0:T(8,128)}, f32[8,128,128]{2,1,0:T(8,128)}, u32[]{:S(2)}, u32[]{:S(2)}) collective-permute-start(f32[8,128,128]{2,1,0:T(8,128)} %slice.9), channel_id=1, source_target_pairs={{0,224},{32,0},{64,32},{96,64},{128,96},{160,128},{192,160},{224,1... | collective-permute-start | bytes 1572872 | tf_op jit(solution)/shard_map/ppermute | solution.py:98
  282.6 12.6 %collective-permute-start.7 = (f32[8,128,128]{2,1,0:T(8,128)}, f32[8,128,128]{2,1,0:T(8,128)}, u32[]{:S(2)}, u32[]{:S(2)}) collective-permute-start(f32[8,128,128]{2,1,0:T(8,128)} %slice.8), channel_id=1, source_target_pairs={{0,32},{32,64},{64,96},{96,128},{128,160},{160,192},{192,224},{224... | collective-permute-start | bytes 1572872 | tf_op jit(solution)/shard_map/ppermute | solution.py:98
  295.2 1.2 copy-start.1
  296.5 1.2 copy-start.3
  297.7 1.2 copy-start.5
  298.9 1.2 copy-start.7
  300.1 0.7 copy-start.8
  300.8 0.7 copy-start.9
  301.5 0.7 copy-start.10
  310.1 52.8 %collective-permute-start.9 = (f32[16,128,128]{2,1,0:T(8,128)S(1)}, f32[16,128,128]{2,1,0:T(8,128)S(1)}, u32[]{:S(2)}, u32[]{:S(2)}) collective-permute-start(f32[16,128,128]{2,1,0:T(8,128)S(1)} %get-tuple-element.8), channel_id=1, source_target_pairs={{0,1},{1,0},{2,3},{3,2},{4,5},{5,4},{6,7},{7,6},{8,9},{9,8},{10,11... | collective-permute-start | bytes 3145736 | tf_op jit(solution)/shard_map/ppermute | solution.py:98
Sparse Core Ops, SparseCore 0:
  9.1 173.4 all-gather.2

commit v2 on v1

v2 whole, which is shorter than its diff:
```python
import jax
import jax.numpy as jnp
from jax import lax
from jax.experimental import pallas as pl
from jax.experimental.pallas import tpu as pltpu
from jax.sharding import Mesh
from jax.sharding import PartitionSpec as P

BS = 128
SA = 16
SCH = 16
N_ROW = 8
N_LEFT = 256
N_RIGHT = 128
PCAP = 512
UNROLL = 16
BINS = 5
LISTED = PCAP + BINS * UNROLL
SPARE = 2 * SCH
TRANSPOSED = (((1,), (1,)), ((), ()))

SCALARS = pl.BlockSpec(memory_space=pltpu.SMEM)
IN_HBM = pl.BlockSpec(memory_space=pltpu.HBM)
VMEM = pl.BlockSpec(memory_space=pltpu.VMEM)
TOKEN = jax.ShapeDtypeStruct((1,), jnp.int32)
STATE = (
    pltpu.VMEM((N_LEFT, BS, BS), jnp.float32),
    pltpu.VMEM((N_RIGHT, BS, BS), jnp.float32),
    pltpu.VMEM((2 * SCH + 1, BS, BS), jnp.float32),
)


def hbm(*arrays):
    return [pltpu.with_memory_space_constraint(a, pltpu.HBM) for a in arrays]


def split(block):
    high = block.astype(jnp.bfloat16)
    low = (block - high.astype(jnp.float32)).astype(jnp.bfloat16)
    return high, low


def block_product(left, right):
    left_high, left_low = split(left)
    right_high, right_low = split(right)
    lhs = jnp.concatenate([left_high, left_high, left_low], axis=1)
    rhs = jnp.concatenate([right_high, right_low, right_high], axis=1)
    return lax.dot_general(lhs, rhs, TRANSPOSED, preferred_element_type=jnp.float32)


def stage_kernel(bins, sides, first, base, starts, bounds, listed, *refs):
    pieces, refs = refs[: len(sides)], refs[len(sides) :]
    if not first:
        refs = refs[3:]
    left, right, total, done = refs[:4]
    sems = refs[-1]
    copies = []
    for piece, (side, parts) in zip(pieces, sides):
        length = piece.shape[0] // parts
        for part in range(parts):
            i = len(copies)
            source = piece.at[pl.ds(part * length, length)]
            copies.append(pltpu.make_async_copy(source, (left, right)[side].at[pl.ds(starts[base + i], length)], sems.at[i]))
    for copy in copies:
        copy.start()
    if first:
        total[...] = jnp.zeros_like(total)
    for copy in copies:
        copy.wait()

    def accumulate(turn, carry):
        products, targets = [], []
        for step in range(UNROLL):
            code = listed[turn * UNROLL + step]
            targets.append(code & 255)
            products.append(block_product(left[code >> 16], right[(code >> 8) & 255]))
        for target, product in zip(targets, products):
            total[target] = total[target] + product
        return carry

    lax.fori_loop(bounds[bins[0]], bounds[bins[1]], accumulate, 0)
    done[0] = bounds[0]


def stage(bins, base, lefts, rights, bounds, listed, starts, state=None, flops=0):
    pieces = lefts + rights
    sides = [(int(i >= len(lefts)), n) for i, (n, _) in enumerate(pieces)]
    aliases = {} if state is None else {3 + len(pieces) + i: i for i in range(3)}
    *state, token = pl.pallas_call(
        lambda *refs: stage_kernel(bins, sides, not aliases, base, *refs),
        out_shape=[*STATE, TOKEN],
        in_specs=[SCALARS] * 3 + [IN_HBM] * len(pieces) + [VMEM] * len(aliases),
        out_specs=[VMEM] * 3 + [SCALARS],
        input_output_aliases=aliases,
        scratch_shapes=[pltpu.SemaphoreType.DMA((max(1, sum(n for _, n in sides)),))],
        compiler_params=pltpu.CompilerParams(vmem_limit_bytes=8 << 20),
        cost_estimate=pl.CostEstimate(flops=flops, bytes_accessed=0, transcendentals=0),
        name="stage_" + "_".join(map(str, bins)),
    )(starts, bounds, listed, *hbm(*[a for _, a in pieces]), *(state or ()))
    return state, token


def tie_kernel(*refs):
    token, scratch = refs[-2:]
    scratch[...] = jnp.zeros_like(scratch)
    token[0] = 0


def tie(arrays, tokens=()):
    *arrays, token = pl.pallas_call(
        tie_kernel,
        out_shape=[pltpu.HBM(a.shape, a.dtype) for a in arrays] + [TOKEN],
        in_specs=[IN_HBM] * len(arrays) + [SCALARS] * len(tokens),
        out_specs=[IN_HBM] * len(arrays) + [SCALARS],
        input_output_aliases={i: i for i in range(len(arrays))},
        scratch_shapes=[pltpu.VMEM((8, BS), jnp.float32)],
        compiler_params=pltpu.CompilerParams(vmem_limit_bytes=1 << 20),
        cost_estimate=pl.CostEstimate(flops=0, bytes_accessed=0, transcendentals=0),
        name="tie",
    )(*hbm(*arrays), *tokens)
    return arrays, token


def pack_kernel(n, *refs):
    pieces, (out, bounce, into, leave) = refs[:n], refs[-4:]
    slots = [pl.ds(i * SA, SA) for i in range(n)]
    fill = [pltpu.make_async_copy(piece, bounce.at[rows], into.at[i]) for i, (piece, rows) in enumerate(zip(pieces, slots))]
    drain = [pltpu.make_async_copy(bounce.at[rows], out.at[rows], leave.at[i]) for i, rows in enumerate(slots)]
    for copy in fill:
        copy.start()
    for first, second in zip(fill, drain):
        first.wait()
        second.start()
    for copy in drain:
        copy.wait()


def pack(*pieces, later_than=()):
    n = len(pieces)
    return pl.pallas_call(
        lambda *refs: pack_kernel(n, *refs),
        out_shape=pltpu.HBM((n * SA, BS, BS), jnp.float32),
        in_specs=[IN_HBM] * (n + len(later_than)),
        out_specs=IN_HBM,
        scratch_shapes=[
            pltpu.VMEM((n * SA, BS, BS), jnp.float32),
            pltpu.SemaphoreType.DMA((n,)),
            pltpu.SemaphoreType.DMA((n,)),
        ],
        compiler_params=pltpu.CompilerParams(vmem_limit_bytes=(n + 1) << 20),
        cost_estimate=pl.CostEstimate(flops=0, bytes_accessed=0, transcendentals=0),
        name="pack",
    )(*hbm(*pieces, *later_than))


def halves_kernel(up, down, up_half, down_half, sems):
    copies = [
        pltpu.make_async_copy(up.at[pl.ds(0, SA // 2)], up_half, sems.at[0]),
        pltpu.make_async_copy(down.at[pl.ds(SA // 2, SA // 2)], down_half, sems.at[1]),
    ]
    for copy in copies:
        copy.start()
    for copy in copies:
        copy.wait()


def halves(up, down):
    half = pltpu.VMEM((SA // 2, BS, BS), jnp.float32)
    return pl.pallas_call(
        halves_kernel,
        out_shape=(half, half),
        in_specs=[IN_HBM] * 2,
        out_specs=(VMEM, VMEM),
        scratch_shapes=[pltpu.SemaphoreType.DMA((2,))],
        compiler_params=pltpu.CompilerParams(vmem_limit_bytes=1 << 20),
        cost_estimate=pl.CostEstimate(flops=0, bytes_accessed=0, transcendentals=0),
        name="halves",
    )(*hbm(up, down))


def shift(value, axis, by):
    size = lax.axis_size(axis)
    return lax.ppermute(value, axis, [(i, (i + by) % size) for i in range(size)])


def order(left_index, right_index, target_index, count, row, layer, left_class):
    p = jnp.arange(PCAP, dtype=jnp.int32)
    away = (right_index // SA - row) % N_ROW
    kept = target_index // SCH == layer
    right_class = jnp.where((away <= 2) | (away >= 6), 0, jnp.where(away == 4, 2, 1))
    here = jnp.maximum(left_class, right_class)
    bins = jnp.where(here == 0, jnp.where(kept, 1, 0), jnp.where(kept, 4, 1 + here))
    bins = jnp.where(p < count, bins, BINS)
    target = jnp.where(kept, 0, SCH) + target_index % SCH
    code = (left_index << 16) | (right_index << 8) | target
    same = bins[:, None] == bins[None, :]
    rank = jnp.sum(same & (p[None, :] < p[:, None]), axis=1, dtype=jnp.int32)
    held = jnp.sum(bins[None, :] == jnp.arange(BINS, dtype=jnp.int32)[:, None], axis=1, dtype=jnp.int32)
    groups = (held + UNROLL - 1) // UNROLL
    b = jnp.arange(BINS + 1, dtype=jnp.int32)
    bounds = jnp.sum(jnp.where(b[None, :BINS] < b[:, None], groups[None, :], 0), axis=1, dtype=jnp.int32)
    start = jnp.sum(jnp.where(bins[:, None] == b[None, :BINS], bounds[None, :BINS] * UNROLL, 0), axis=1)
    place = jnp.where(bins < BINS, start + rank, -1)
    slot = jnp.arange(LISTED, dtype=jnp.int32)
    hit = place[None, :] == slot[:, None]
    listed = SPARE + jnp.sum(jnp.where(hit, code[None, :] - SPARE, 0), axis=1, dtype=jnp.int32)
    return bounds, listed


def body(slab_blocks, factor_blocks, stack_left, stack_right, stack_target, stack_counts):
    row, layer = lax.axis_index("row"), lax.axis_index("layer")
    y, x, core = lax.axis_index("y"), lax.axis_index("x"), lax.axis_index("core")

    left_index = stack_left.reshape(-1)
    across_y = (left_index // (4 * SA) - y) % 4
    across_x = (left_index // (2 * SA) - x) % 2
    left_class = jnp.where(across_y == 2, jnp.where(across_x == 0, 1, 2), jnp.where((across_y != 0) & (across_x == 1), 2, 0))
    bounds, listed = order(
        left_index,
        stack_right.reshape(-1),
        stack_target.reshape(-1),
        stack_counts.reshape(()),
        row,
        layer,
        left_class,
    )

    def left_at(dy, dx, dc, first=0):
        return (((y + dy) % 4 * 2 + (x + dx) % 2) * 2 + (core + dc) % 2) * SA + first

    def right_at(away, first=0):
        return (row + away) % N_ROW * SA + first

    own = slab_blocks.reshape(SA, BS, BS)
    mine = lax.all_to_all(factor_blocks.reshape(SA, BS, BS), ("y", "x", "core"), split_axis=0, concat_axis=0, tiled=True)

    first_places = [left_at(0, 0, 0), left_at(0, 0, 1), left_at(-1, 0, 0), left_at(1, 0, 0), left_at(0, 1, 0)]
    first_places += [left_at(-1, 0, 1), left_at(1, 0, 1), left_at(0, 1, 1)]
    first_places += [right_at(away) for away in (0, -1, 1, -2, 2)]
    second_places = [left_at(2, 0, 0), left_at(2, 0, 1), right_at(-3), right_at(3)]
    third_places = [left_at(dy, 1, dc) for dy in (1, -1, 2) for dc in range(2)] + [right_at(4), right_at(4, 8)]
    starts = jnp.stack(first_places + second_places + third_places)
    second, third = len(first_places), len(first_places) + len(second_places)

    up1, down1 = shift(mine, "row", 1), shift(mine, "row", -1)
    own_c = shift(own, "core", 1)
    sent = pack(own, later_than=(own_c,))
    own_up, own_down, across = shift(sent, "y", 1), shift(sent, "y", -1), shift(sent, "x", 1)
    packed = pack(own_up, own_down, across)
    (up1, down1, own_up, own_down, across, own_c, packed), t1 = tie((up1, down1, own_up, own_down, across, own_c, packed))

    up2, down2 = shift(up1, "row", 1), shift(down1, "row", -1)
    own_far, across_down = shift(own_up, "y", 1), shift(across, "y", -1)
    packed_c = shift(packed, "core", 1)
    (up2, down2, own_far, across_down, packed_c), t2 = tie((up2, down2, own_far, across_down, packed_c), (t1,))

    up3, down3 = shift(up2, "row", 1), shift(down2, "row", -1)
    far, across_up = shift(across_down, "y", -1), shift(own_up, "x", 1)
    own_far_c = shift(own_far, "core", 1)
    lefts = [(1, own), (1, own_c), (1, own_up), (1, own_down), (1, across), (3, packed_c)]
    rights = [(1, mine), (1, up1), (1, down1), (1, up2), (1, down2)]
    state, done = stage((0, 2), 0, lefts, rights, bounds, listed, starts, flops=8 * 10**9)
    (up3, down3, far, across_up, own_far_c), t3 = tie((up3, down3, far, across_up, own_far_c), (t2, done))

    up3_half, down3_half = halves(up3, down3)
    up4, down4 = shift(up3_half, "row", 1), shift(down3_half, "row", -1)
    across_down_c, across_up_c, far_c = shift(across_down, "core", 1), shift(across_up, "core", 1), shift(far, "core", 1)
    lefts, rights = [(1, own_far), (1, own_far_c)], [(1, up3), (1, down3)]
    state, done = stage((2, 3), second, lefts, rights, bounds, listed, starts, state, flops=4 * 10**9)
    (up4, down4, across_down_c, across_up_c, far_c), t4 = tie((up4, down4, across_down_c, across_up_c, far_c), (t3, done))

    lefts = [(1, a) for a in (across_down, across_down_c, across_up, across_up_c, far, far_c)]
    state, _ = stage((3, 4), third, lefts, [(1, up4), (1, down4)], bounds, listed, starts, state)
    arrived = shift(state[2][SCH : 2 * SCH], "layer", 1)
    state, _ = stage((4, 5), 0, [], [], bounds, listed, starts, state, flops=10**10)
    summed = state[2][:SCH] + arrived
    return summed.reshape((1, 1, 1) + summed.shape)


def solution(mesh):
    fine = Mesh(mesh.devices.reshape(8, 4, 2, 2, 2), ("row", "y", "x", "core", "layer"))
    col = ("y", "x", "core")
    return jax.shard_map(
        body,
        mesh=fine,
        in_specs=(
            P("row", col, "layer", None, None, None),
            P("row", col, "layer", None, None, None, None),
            P("row", col, "layer", None),
            P("row", col, "layer", None),
            P("row", col, "layer", None),
            P("row", col, "layer"),
        ),
        out_specs=P("row", col, "layer", None, None, None),
        check_vma=False,
    )
```

time: 374 us -> 175 us (0.47)
  waiting for transfers between devices: 276 us -> 98.1 us
  Pallas kernels: 7.92 us -> 31.1 us
  blocking collectives: 20.9 us -> 0 us
  between operations: 14.1 us -> 1 us
  starting transfers between devices: 39.1 us -> 30.1 us
    all_gather x1 -> x0, waiting for transfers between devices: 175 us -> none  [body(): left_own = lax.all_gather(slab, ('y', 'x'), axis=0, tiled=True)]
    pallas_call x1 -> x11, Pallas kernels: 7.92 us -> 31.1 us  [the longest x4 19.6 us: stage(): pl.pallas_call(lambda *refs: stage_kernel(bins, sides, not aliases, base,...]
    all_to_all x1 -> x0, blocking collectives: 20.9 us -> none  [body(): lax.all_to_all(factor_blocks.reshape(SA, BS, BS), ('y', 'x', 'core'), spl...]
    ppermute x10 -> x22, starting transfers between devices: 39.1 us -> 24 us  [shift(): lax.ppermute(value, axis, [(i, (i + by) % size) for i in range(size)])]
    ppermute x10 -> x22, waiting for transfers between devices: 99.9 us -> 89.2 us  [shift(): lax.ppermute(value, axis, [(i, (i + by) % size) for i in range(size)])]
    all_to_all x0 -> x1, waiting for transfers between devices: none -> 8.84 us  [body(): lax.all_to_all(factor_blocks.reshape(SA, BS, BS), ('y', 'x', 'core'), spl...]
    all_to_all x0 -> x1, starting transfers between devices: none -> 6.06 us  [body(): lax.all_to_all(factor_blocks.reshape(SA, BS, BS), ('y', 'x', 'core'), spl...]
    unnamed x22 -> x46, local copies, waits for them, and re-layouts: 9.91 us -> 9.11 us
  transfers between devices with their start and end apart: 11 -> 23, of which waited for: 9 -> 11; matrix products, arithmetic and copies ran while one was open for 0% -> 1% of each run, Pallas kernels for 0% -> 14%
where the time goes in v2:
time: 175 us; the launch traced here: 171 us
  waiting for transfers between devices  98.1 us (56%)
  Pallas kernels  31.1 us (18%)
  starting transfers between devices  30.1 us (17%)
  local copies, waits for them, and re-layouts  9.28 us (5%)
  other arithmetic  1.96 us (1%)
    ppermute x22, waiting for transfers between devices, shift(): lax.ppermute(value, axis, [(i, (i + by) % size) for i in range(size)])  89.2 us
    ppermute x22, starting transfers between devices, shift(): lax.ppermute(value, axis, [(i, (i + by) % size) for i in range(size)])  24 us
    pallas_call x4, Pallas kernels, stage(): pl.pallas_call(lambda *refs: stage_kernel(bins, sides, not aliases, base,...  19.6 us
    unnamed x46, local copies, waits for them, and re-layouts  9.11 us
    all_to_all x1, waiting for transfers between devices, body(): lax.all_to_all(factor_blocks.reshape(SA, BS, BS), ('y', 'x', 'core'), spl...  8.84 us
    all_to_all x1, starting transfers between devices, body(): lax.all_to_all(factor_blocks.reshape(SA, BS, BS), ('y', 'x', 'core'), spl...  6.06 us
    pallas_call x2, Pallas kernels, pack(): pl.pallas_call(lambda *refs: pack_kernel(n, *refs), out_shape=pltpu.HBM((...  5.17 us
    pallas_call x4, Pallas kernels, tie(): pl.pallas_call(tie_kernel, out_shape=[pltpu.HBM(a.shape, a.dtype) for a i...  5.13 us
  transfers between devices with their start and end apart: 23, of which 11 were waited for; matrix products, arithmetic and copies ran while one was open for 1% of the time, Pallas kernels for 14%

profile of v2, /device:TPU:34, one launch (start us, length us, event | category | flops | bytes accessed | tf_op | source)
XLA Modules:
  0.0 171.5 jit_solution(7255219246814957586)
XLA Ops:
  0.0 6.1 %all-to-all-start = ((f32[16,128,128]{2,1,0:T(8,128)}), f32[16,128,128]{2,1,0:T(8,128)}, u32[]{:S(2)}, u32[]{:S(2)}) async-start(f32[16,128,128]{2,1,0:T(8,128)} %bitcast.38), calls=%async_computation | async-start | bytes 2097152 | tf_op jit(solution)/shard_map/all_to_all | solution.py:235
  6.1 1.0 copy-done.3
  7.0 2.2 %pack.2 = f32[16,128,128]{2,1,0:T(8,128)} custom-call(f32[16,128,128]{2,1,0:T(8,128)} %bitcast.36, f32[16,128,128]{2,1,0:T(8,128)} %copy-done.3), custom_call_target="tpu_custom_call" | custom-call | tf_op jit(solution)/shard_map/pack/pallas_call | solution.py:140
  9.3 1.5 collective-permute-start.3
  10.8 1.8 %collective-permute-start.4 = (f32[16,128,128]{2,1,0:T(8,128)}, f32[16,128,128]{2,1,0:T(8,128)S(1)}, u32[]{:S(2)}, u32[]{:S(2)}) collective-permute-start(f32[16,128,128]{2,1,0:T(8,128)} %pack.2), channel_id=1, source_target_pairs={{0,24},{8,0},{16,8},{24,16},{1,25},{9,1},{17,9},{25,17},{2,26},{10... | collective-permute-start | bytes 3145736 | tf_op jit(solution)/shard_map/ppermute | solution.py:183
  12.6 0.2 collective-permute-start.5
  12.7 8.8 %all-to-all-done.refs_9_ = f32[16,128,128]{2,1,0:T(8,128)} async-done(((f32[16,128,128]{2,1,0:T(8,128)}), f32[16,128,128]{2,1,0:T(8,128)}, u32[]{:S(2)}, u32[]{:S(2)}) %all-to-all-start) | async-done | bytes 1048608 | tf_op jit(solution)/shard_map/all_to_all | solution.py:235
  21.6 1.9 %collective-permute-start = (f32[16,128,128]{2,1,0:T(8,128)}, f32[16,128,128]{2,1,0:T(8,128)S(1)}, u32[]{:S(2)}, u32[]{:S(2)}) collective-permute-start(f32[16,128,128]{2,1,0:T(8,128)} %all-to-all-done.refs_9_), channel_id=1, source_target_pairs={{0,32},{32,64},{64,96},{96,128},{128,160},{160,192},{192,224},{224... | collective-permute-start | bytes 3145736 | tf_op jit(solution)/shard_map/ppermute | solution.py:183
  23.5 0.1 collective-permute-start.1
  23.6 20.0 %collective-permute-done.3.refs_0_.refs_2_ = f32[16,128,128]{2,1,0:T(8,128)S(1)} collective-permute-done((f32[16,128,128]{2,1,0:T(8,128)}, f32[16,128,128]{2,1,0:T(8,128)S(1)}, u32[]{:S(2)}, u32[]{:S(2)}) %collective-permute-start.3) | collective-permute-done | bytes 1048608 | tf_op jit(solution)/shard_map/ppermute | solution.py:183
  43.7 1.0 copy-done.9
  44.6 0.4 copy-done.10
  45.0 1.0 copy-done.11
  46.0 3.0 %pack.3.refs_6_ = f32[48,128,128]{2,1,0:T(8,128)} custom-call(f32[16,128,128]{2,1,0:T(8,128)} %copy-done.9, f32[16,128,128]{2,1,0:T(8,128)} %copy-done.10, f32[16,128,128]{2,1,0:T(8,128)} %copy-done.11), custom_call_target="tpu_custom_call" | custom-call | tf_op jit(solution)/shard_map/pack/pallas_call | solution.py:140
  49.0 0.0 copy-start.20
  49.0 0.0 copy-start.22
  49.1 0.9 copy-done.17
  50.0 1.0 copy-done.18
  51.0 0.5 tie.4
  51.5 0.2 collective-permute-start.10
  52.4 0.1 convert_reduce_fusion.1
  52.5 0.1 collective-permute-start.8
  52.6 2.2 %collective-permute-start.6 = (f32[16,128,128]{2,1,0:T(8,128)}, f32[16,128,128]{2,1,0:T(8,128)S(1)}, u32[]{:S(2)}, u32[]{:S(2)}) collective-permute-start(f32[16,128,128]{2,1,0:T(8,128)} %get-tuple-element.44.refs_10_), channel_id=1, source_target_pairs={{0,32},{32,64},{64,96},{96,128},{128,160},{160,192},{192,224},{224... | collective-permute-start | bytes 3145736 | tf_op jit(solution)/shard_map/ppermute | solution.py:183
  54.8 0.0 collective-permute-start.7
  54.8 3.1 %collective-permute-start.9 = (f32[16,128,128]{2,1,0:T(8,128)}, f32[16,128,128]{2,1,0:T(8,128)S(1)}, u32[]{:S(2)}, u32[]{:S(2)}) collective-permute-start(f32[16,128,128]{2,1,0:T(8,128)} %get-tuple-element.47.refs_7_), channel_id=1, source_target_pairs={{0,24},{8,0},{16,8},{24,16},{1,25},{9,1},{17,9},{25,17},{2,26},{10... | collective-permute-start | bytes 3145736 | tf_op jit(solution)/shard_map/ppermute | solution.py:183
  57.9 0.1 stack.103.refs_0_
  58.0 0.1 select_reduce_fusion.2.refs_1_
  58.2 0.1 select_reduce_fusion.1
  58.2 0.3 convert_reduce_fusion
  58.5 21.0 %collective-permute-done.8.refs_2_ = f32[16,128,128]{2,1,0:T(8,128)S(1)} collective-permute-done((f32[16,128,128]{2,1,0:T(8,128)}, f32[16,128,128]{2,1,0:T(8,128)S(1)}, u32[]{:S(2)}, u32[]{:S(2)}) %collective-permute-start.8) | collective-permute-done | bytes 1048608 | tf_op jit(solution)/shard_map/ppermute | solution.py:183
  79.5 0.6 collective-permute-start.14
  80.1 1.2 collective-permute-done.7.refs_1_
  81.3 1.0 copy-done.13
  82.3 1.1 tie.5
  83.4 3.1 %collective-permute-start.13 = (f32[16,128,128]{2,1,0:T(8,128)}, f32[16,128,128]{2,1,0:T(8,128)S(1)}, u32[]{:S(2)}, u32[]{:S(2)}) collective-permute-start(f32[16,128,128]{2,1,0:T(8,128)} %get-tuple-element.50.refs_3_), channel_id=1, source_target_pairs={{0,24},{8,0},{16,8},{24,16},{1,25},{9,1},{17,9},{25,17},{2,26},{10... | collective-permute-start | bytes 3145736 | tf_op jit(solution)/shard_map/ppermute | solution.py:183
  86.5 2.7 %collective-permute-start.11 = (f32[16,128,128]{2,1,0:T(8,128)}, f32[16,128,128]{2,1,0:T(8,128)S(1)}, u32[]{:S(2)}, u32[]{:S(2)}) collective-permute-start(f32[16,128,128]{2,1,0:T(8,128)} %get-tuple-element.51.refs_12_), channel_id=1, source_target_pairs={{0,32},{32,64},{64,96},{96,128},{128,160},{160,192},{192,224},{224... | collective-permute-start | bytes 3145736 | tf_op jit(solution)/shard_map/ppermute | solution.py:183
  89.2 1.2 collective-permute-start.12
  90.3 0.2 select_reduce_fusion
  90.6 7.8 %stage_0_2.1 = (f32[256,128,128]{2,1,0:T(8,128)S(1)}, f32[128,128,128]{2,1,0:T(8,128)S(1)}, f32[33,128,128]{2,1,0:T(8,128)S(1)}, s32[1]{0:T(128)}) custom-call(s32[25]{0:T(128)S(1)} %stack.103.refs_0_, s32[6]{0:T(128)S(1)} %select_reduce_fusion.2.refs_1_, s32[592]{0:T(1024)S(1)} %broadcast_add_fusion.refs_2_, f32[16,128,128]{2,1,0:T(8,128)} %bitcast.37, ...), custom_call_target="tpu_custom_call" | custom-call | flops 8000000000 | tf_op jit(solution)/shard_map/stage_0_2/pallas_call | solution.py:89
  98.3 6.1 %collective-permute-done.14.refs_3_ = f32[16,128,128]{2,1,0:T(8,128)S(1)} collective-permute-done((f32[16,128,128]{2,1,0:T(8,128)}, f32[16,128,128]{2,1,0:T(8,128)S(1)}, u32[]{:S(2)}, u32[]{:S(2)}) %collective-permute-start.14) | collective-permute-done | bytes 1048608 | tf_op jit(solution)/shard_map/ppermute | solution.py:183
  104.4 4.1 %collective-permute-done.13.refs_2_ = f32[16,128,128]{2,1,0:T(8,128)S(1)} collective-permute-done((f32[16,128,128]{2,1,0:T(8,128)}, f32[16,128,128]{2,1,0:T(8,128)S(1)}, u32[]{:S(2)}, u32[]{:S(2)}) %collective-permute-start.13) | collective-permute-done | bytes 1048608 | tf_op jit(solution)/shard_map/ppermute | solution.py:183
  108.6 4.0 %collective-permute-done.11.refs_0_ = f32[16,128,128]{2,1,0:T(8,128)S(1)} collective-permute-done((f32[16,128,128]{2,1,0:T(8,128)}, f32[16,128,128]{2,1,0:T(8,128)S(1)}, u32[]{:S(2)}, u32[]{:S(2)}) %collective-permute-start.11) | collective-permute-done | bytes 1048608 | tf_op jit(solution)/shard_map/ppermute | solution.py:183
  112.6 0.8 collective-permute-done.12.refs_1_
  113.5 0.1 copy-done
  113.6 0.8 copy-done.1
  114.4 0.4 copy-done.8
  114.8 1.7 %tie.6 = (f32[16,128,128]{2,1,0:T(8,128)}, f32[16,128,128]{2,1,0:T(8,128)}, f32[16,128,128]{2,1,0:T(8,128)}, f32[16,128,128]{2,1,0:T(8,128)}, f32[16,128,128]{2,1,0:T(8,128)}, /*index=5*/s32[1]{0:T(128)}) custom-call(f32[16,128,128]{2,1,0:T(8,128)} %copy-done, ...), custom_call_target="tpu_custom_call", output_to_operand_aliasing={{0}: (0, {}), {1}: (1, {}), {2}: (2, {}), {3}: (3, {}), {4}... | custom-call | tf_op jit(solution)/shard_map/tie/pallas_call | solution.py:110
  116.5 0.1 collective-permute-start.19
  116.6 0.5 collective-permute-start.20
  117.1 1.2 halves.1
  118.3 2.6 %collective-permute-start.16 = (f32[8,128,128]{2,1,0:T(8,128)S(1)}, f32[8,128,128]{2,1,0:T(8,128)S(1)}, u32[]{:S(2)}, u32[]{:S(2)}) collective-permute-start(f32[8,128,128]{2,1,0:T(8,128)S(1)} %get-tuple-element.61), channel_id=1, source_target_pairs={{0,32},{32,64},{64,96},{96,128},{128,160},{160,192},{192,224},{224... | collective-permute-start | bytes 1572872 | tf_op jit(solution)/shard_map/ppermute | solution.py:183
  121.0 4.1 %stage_2_3.1 = (f32[256,128,128]{2,1,0:T(8,128)S(1)}, f32[128,128,128]{2,1,0:T(8,128)S(1)}, f32[33,128,128]{2,1,0:T(8,128)S(1)}, s32[1]{0:T(128)}) custom-call(s32[25]{0:T(128)S(1)} %stack.103.refs_0_, s32[6]{0:T(128)S(1)} %select_reduce_fusion.2.refs_1_, ...), custom_call_target="tpu_custom_call", output_to_operand_aliasing={{0}: (7, {}), {1}: (8, {}), {2}: (9, {})} | custom-call | flops 4000000000 | tf_op jit(solution)/shard_map/stage_2_3/pallas_call | solution.py:89
  125.1 8.0 %collective-permute-done.16.refs_0_ = f32[8,128,128]{2,1,0:T(8,128)S(1)} collective-permute-done((f32[8,128,128]{2,1,0:T(8,128)S(1)}, f32[8,128,128]{2,1,0:T(8,128)S(1)}, u32[]{:S(2)}, u32[]{:S(2)}) %collective-permute-start.16) | collective-permute-done | bytes 524320 | tf_op jit(solution)/shard_map/ppermute | solution.py:183
  133.1 2.8 %collective-permute-done.17.refs_1_ = f32[8,128,128]{2,1,0:T(8,128)S(1)} collective-permute-done((f32[8,128,128]{2,1,0:T(8,128)S(1)}, f32[8,128,128]{2,1,0:T(8,128)S(1)}, u32[]{:S(2)}, u32[]{:S(2)}) %collective-permute-start.17) | collective-permute-done | bytes 524320 | tf_op jit(solution)/shard_map/ppermute | solution.py:183
  135.9 0.8 copy-done.16
  136.7 0.3 copy-done.4
  137.0 0.4 copy-done.5
  137.4 1.8 %tie.7 = (f32[8,128,128]{2,1,0:T(8,128)}, f32[8,128,128]{2,1,0:T(8,128)}, f32[16,128,128]{2,1,0:T(8,128)}, f32[16,128,128]{2,1,0:T(8,128)}, f32[16,128,128]{2,1,0:T(8,128)}, /*index=5*/s32[1]{0:T(128)}) custom-call(f32[8,128,128]{2,1,0:T(8,128)} %copy-done.15, ...), custom_call_target="tpu_custom_call", output_to_operand_aliasing={{0}: (0, {}), {1}: (1, {}), {2}: (2, {}), {3}: (3, {}), {4}... | custom-call | tf_op jit(solution)/shard_map/tie/pallas_call | solution.py:110
  139.2 5.0 %stage_3_4.1 = (f32[256,128,128]{2,1,0:T(8,128)S(1)}, f32[128,128,128]{2,1,0:T(8,128)S(1)}, f32[33,128,128]{2,1,0:T(8,128)S(1)}, s32[1]{0:T(128)}) custom-call(s32[25]{0:T(128)S(1)} %stack.103.refs_0_, s32[6]{0:T(128)S(1)} %select_reduce_fusion.2.refs_1_, ...), custom_call_target="tpu_custom_call", output_to_operand_aliasing={{0}: (11, {}), {1}: (12, {}), {2}: (13, {})} | custom-call | tf_op jit(solution)/shard_map/stage_3_4/pallas_call | solution.py:89
  144.2 0.1 slice.18
  144.3 2.2 %collective-permute-start.21 = (f32[16,128,128]{2,1,0:T(8,128)S(1)}, f32[16,128,128]{2,1,0:T(8,128)S(1)}, u32[]{:S(2)}, u32[]{:S(2)}) collective-permute-start(f32[16,128,128]{2,1,0:T(8,128)S(1)} %slice.18), channel_id=1, source_target_pairs={{0,1},{1,0},{2,3},{3,2},{4,5},{5,4},{6,7},{7,6},{8,9},{9,8},{10,11... | collective-permute-start | bytes 3145736 | tf_op jit(solution)/shard_map/ppermute | solution.py:183
  146.5 2.7 %stage_4_5.1 = (f32[256,128,128]{2,1,0:T(8,128)S(1)}, f32[128,128,128]{2,1,0:T(8,128)S(1)}, f32[33,128,128]{2,1,0:T(8,128)S(1)}, s32[1]{0:T(128)}) custom-call(s32[25]{0:T(128)S(1)} %stack.103.refs_0_, s32[6]{0:T(128)S(1)} %select_reduce_fusion.2.refs_1_, ...), custom_call_target="tpu_custom_call", output_to_operand_aliasing={{0}: (3, {}), {1}: (4, {}), {2}: (5, {})} | custom-call | flops 10000000000 | tf_op jit(solution)/shard_map/stage_4_5/pallas_call | solution.py:89
  149.2 21.2 %collective-permute-done.21 = f32[16,128,128]{2,1,0:T(8,128)S(1)} collective-permute-done((f32[16,128,128]{2,1,0:T(8,128)S(1)}, f32[16,128,128]{2,1,0:T(8,128)S(1)}, u32[]{:S(2)}, u32[]{:S(2)}) %collective-permute-start.21) | collective-permute-done | bytes 1048608 | tf_op jit(solution)/shard_map/ppermute | solution.py:183
  170.4 1.1 add_bitcast_fusion
  (53 shorter events, 0.2 us)
Async XLA Ops:
  0.0 6.1 %collective-permute-start.2 = (f32[16,128,128]{2,1,0:T(8,128)}, f32[16,128,128]{2,1,0:T(8,128)S(1)}, u32[]{:S(2)}, u32[]{:S(2)}) collective-permute-start(f32[16,128,128]{2,1,0:T(8,128)} %bitcast.35), channel_id=1, source_target_pairs={{0,2},{2,0},{1,3},{3,1},{4,6},{6,4},{5,7},{7,5},{8,10},{10,8},{9,1... | collective-permute-start | bytes 3145736 | tf_op jit(solution)/shard_map/ppermute | solution.py:183
  0.0 21.6 %all-to-all-start = ((f32[16,128,128]{2,1,0:T(8,128)}), f32[16,128,128]{2,1,0:T(8,128)}, u32[]{:S(2)}, u32[]{:S(2)}) async-start(f32[16,128,128]{2,1,0:T(8,128)} %bitcast.38), calls=%async_computation | async-start | bytes 2097152 | tf_op jit(solution)/shard_map/all_to_all | solution.py:235
  6.1 1.0 copy-start.3
  9.3 34.4 %collective-permute-start.3 = (f32[16,128,128]{2,1,0:T(8,128)}, f32[16,128,128]{2,1,0:T(8,128)S(1)}, u32[]{:S(2)}, u32[]{:S(2)}) collective-permute-start(f32[16,128,128]{2,1,0:T(8,128)} %pack.2), channel_id=1, source_target_pairs={{0,8},{8,16},{16,24},{24,0},{1,9},{9,17},{17,25},{25,1},{2,10},{10... | collective-permute-start | bytes 3145736 | tf_op jit(solution)/shard_map/ppermute | solution.py:183
  10.8 32.8 %collective-permute-start.4 = (f32[16,128,128]{2,1,0:T(8,128)}, f32[16,128,128]{2,1,0:T(8,128)S(1)}, u32[]{:S(2)}, u32[]{:S(2)}) collective-permute-start(f32[16,128,128]{2,1,0:T(8,128)} %pack.2), channel_id=1, source_target_pairs={{0,24},{8,0},{16,8},{24,16},{1,25},{9,1},{17,9},{25,17},{2,26},{10... | collective-permute-start | bytes 3145736 | tf_op jit(solution)/shard_map/ppermute | solution.py:183
  12.6 31.1 %collective-permute-start.5 = (f32[16,128,128]{2,1,0:T(8,128)}, f32[16,128,128]{2,1,0:T(8,128)S(1)}, u32[]{:S(2)}, u32[]{:S(2)}) collective-permute-start(f32[16,128,128]{2,1,0:T(8,128)} %pack.2), channel_id=1, source_target_pairs={{0,4},{4,0},{1,5},{5,1},{2,6},{6,2},{3,7},{7,3},{8,12},{12,8},{9,1... | collective-permute-start | bytes 3145736 | tf_op jit(solution)/shard_map/ppermute | solution.py:183
  21.6 27.4 %collective-permute-start = (f32[16,128,128]{2,1,0:T(8,128)}, f32[16,128,128]{2,1,0:T(8,128)S(1)}, u32[]{:S(2)}, u32[]{:S(2)}) collective-permute-start(f32[16,128,128]{2,1,0:T(8,128)} %all-to-all-done.refs_9_), channel_id=1, source_target_pairs={{0,32},{32,64},{64,96},{96,128},{128,160},{160,192},{192,224},{224... | collective-permute-start | bytes 3145736 | tf_op jit(solution)/shard_map/ppermute | solution.py:183
  23.5 25.5 %collective-permute-start.1 = (f32[16,128,128]{2,1,0:T(8,128)}, f32[16,128,128]{2,1,0:T(8,128)S(1)}, u32[]{:S(2)}, u32[]{:S(2)}) collective-permute-start(f32[16,128,128]{2,1,0:T(8,128)} %all-to-all-done.refs_9_), channel_id=1, source_target_pairs={{0,224},{32,0},{64,32},{96,64},{128,96},{160,128},{192,160},{224,1... | collective-permute-start | bytes 3145736 | tf_op jit(solution)/shard_map/ppermute | solution.py:183
  43.6 1.0 copy-start.9
  43.7 1.4 copy-start.10
  45.0 1.0 copy-start.11
  49.0 3.3 %copy-start.20 = (s32[1,1,1,512]{3,2,1,0:T(1,128)S(1)}, s32[1,1,1,512]{3,2,1,0:T(1,128)}, u32[]{:S(2)}) copy-start(s32[1,1,1,512]{3,2,1,0:T(1,128)} %param.9) | copy-start | bytes 6148
  49.0 3.3 %copy-start.21 = (s32[1,1,1,512]{3,2,1,0:T(1,128)S(1)}, s32[1,1,1,512]{3,2,1,0:T(1,128)}, u32[]{:S(2)}) copy-start(s32[1,1,1,512]{3,2,1,0:T(1,128)} %param.8) | copy-start | bytes 6148
  49.0 3.3 %copy-start.22 = (s32[1,1,1,512]{3,2,1,0:T(1,128)S(1)}, s32[1,1,1,512]{3,2,1,0:T(1,128)}, u32[]{:S(2)}) copy-start(s32[1,1,1,512]{3,2,1,0:T(1,128)} %param.10) | copy-start | bytes 6148
  49.0 1.0 copy-start.17
  50.0 1.0 copy-start.18
  51.5 29.8 %collective-permute-start.10 = (f32[48,128,128]{2,1,0:T(8,128)}, f32[48,128,128]{2,1,0:T(8,128)}, u32[]{:S(2)}, u32[]{:S(2)}) collective-permute-start(f32[48,128,128]{2,1,0:T(8,128)} %get-tuple-element.48), channel_id=1, source_target_pairs={{0,2},{2,0},{1,3},{3,1},{4,6},{6,4},{5,7},{7,5},{8,10},{10,8},{9,1... | collective-permute-start | bytes 9437192 | tf_op jit(solution)/shard_map/ppermute | solution.py:183
  52.5 27.0 %collective-permute-start.8 = (f32[16,128,128]{2,1,0:T(8,128)}, f32[16,128,128]{2,1,0:T(8,128)S(1)}, u32[]{:S(2)}, u32[]{:S(2)}) collective-permute-start(f32[16,128,128]{2,1,0:T(8,128)} %get-tuple-element.46.refs_5_), channel_id=1, source_target_pairs={{0,8},{8,16},{16,24},{24,0},{1,9},{9,17},{17,25},{25,1},{2,10},{10... | collective-permute-start | bytes 3145736 | tf_op jit(solution)/shard_map/ppermute | solution.py:183
  52.6 27.5 %collective-permute-start.6 = (f32[16,128,128]{2,1,0:T(8,128)}, f32[16,128,128]{2,1,0:T(8,128)S(1)}, u32[]{:S(2)}, u32[]{:S(2)}) collective-permute-start(f32[16,128,128]{2,1,0:T(8,128)} %get-tuple-element.44.refs_10_), channel_id=1, source_target_pairs={{0,32},{32,64},{64,96},{96,128},{128,160},{160,192},{192,224},{224... | collective-permute-start | bytes 3145736 | tf_op jit(solution)/shard_map/ppermute | solution.py:183
  54.8 26.5 %collective-permute-start.7 = (f32[16,128,128]{2,1,0:T(8,128)}, f32[16,128,128]{2,1,0:T(8,128)}, u32[]{:S(2)}, u32[]{:S(2)}) collective-permute-start(f32[16,128,128]{2,1,0:T(8,128)} %get-tuple-element.45.refs_11_), channel_id=1, source_target_pairs={{0,224},{32,0},{64,32},{96,64},{128,96},{160,128},{192,160},{224,1... | collective-permute-start | bytes 3145736 | tf_op jit(solution)/shard_map/ppermute | solution.py:183
  54.8 26.4 %collective-permute-start.9 = (f32[16,128,128]{2,1,0:T(8,128)}, f32[16,128,128]{2,1,0:T(8,128)S(1)}, u32[]{:S(2)}, u32[]{:S(2)}) collective-permute-start(f32[16,128,128]{2,1,0:T(8,128)} %get-tuple-element.47.refs_7_), channel_id=1, source_target_pairs={{0,24},{8,0},{16,8},{24,16},{1,25},{9,1},{17,9},{25,17},{2,26},{10... | collective-permute-start | bytes 3145736 | tf_op jit(solution)/shard_map/ppermute | solution.py:183
  79.5 1.8 %copy-start.12 = (f32[16,128,128]{2,1,0:T(8,128)}, f32[16,128,128]{2,1,0:T(8,128)S(1)}, u32[]{:S(2)}) copy-start(f32[16,128,128]{2,1,0:T(8,128)S(1)} %collective-permute-done.8.refs_2_) | copy-start | bytes 3145732
  79.5 24.9 %collective-permute-start.14 = (f32[16,128,128]{2,1,0:T(8,128)}, f32[16,128,128]{2,1,0:T(8,128)S(1)}, u32[]{:S(2)}, u32[]{:S(2)}) collective-permute-start(f32[16,128,128]{2,1,0:T(8,128)} %get-tuple-element.46.refs_5_), channel_id=1, source_target_pairs={{0,4},{4,0},{1,5},{5,1},{2,6},{6,2},{3,7},{7,3},{8,12},{12,8},{9,1... | collective-permute-start | bytes 3145736 | tf_op jit(solution)/shard_map/ppermute | solution.py:183
  80.1 1.2 copy-start.19
  81.3 1.0 copy-start.13
  83.4 25.2 %collective-permute-start.13 = (f32[16,128,128]{2,1,0:T(8,128)}, f32[16,128,128]{2,1,0:T(8,128)S(1)}, u32[]{:S(2)}, u32[]{:S(2)}) collective-permute-start(f32[16,128,128]{2,1,0:T(8,128)} %get-tuple-element.50.refs_3_), channel_id=1, source_target_pairs={{0,24},{8,0},{16,8},{24,16},{1,25},{9,1},{17,9},{25,17},{2,26},{10... | collective-permute-start | bytes 3145736 | tf_op jit(solution)/shard_map/ppermute | solution.py:183
  86.5 26.1 %collective-permute-start.11 = (f32[16,128,128]{2,1,0:T(8,128)}, f32[16,128,128]{2,1,0:T(8,128)S(1)}, u32[]{:S(2)}, u32[]{:S(2)}) collective-permute-start(f32[16,128,128]{2,1,0:T(8,128)} %get-tuple-element.51.refs_12_), channel_id=1, source_target_pairs={{0,32},{32,64},{64,96},{96,128},{128,160},{160,192},{192,224},{224... | collective-permute-start | bytes 3145736 | tf_op jit(solution)/shard_map/ppermute | solution.py:183
  89.2 24.3 %collective-permute-start.12 = (f32[16,128,128]{2,1,0:T(8,128)}, f32[16,128,128]{2,1,0:T(8,128)S(1)}, u32[]{:S(2)}, u32[]{:S(2)}) collective-permute-start(f32[16,128,128]{2,1,0:T(8,128)} %get-tuple-element.52.refs_13_), channel_id=1, source_target_pairs={{0,224},{32,0},{64,32},{96,64},{128,96},{160,128},{192,160},{224,1... | collective-permute-start | bytes 3145736 | tf_op jit(solution)/shard_map/ppermute | solution.py:183
  90.3 23.1 %collective-permute-start.15 = (f32[16,128,128]{2,1,0:T(8,128)}, f32[16,128,128]{2,1,0:T(8,128)S(1)}, u32[]{:S(2)}, u32[]{:S(2)}) collective-permute-start(f32[16,128,128]{2,1,0:T(8,128)} %get-tuple-element.53.refs_3_), channel_id=1, source_target_pairs={{0,2},{2,0},{1,3},{3,1},{4,6},{6,4},{5,7},{7,5},{8,10},{10,8},{9,1... | collective-permute-start | bytes 3145736 | tf_op jit(solution)/shard_map/ppermute | solution.py:183
  90.6 13.9 %copy-start.14 = (f32[16,128,128]{2,1,0:T(8,128)S(1)}, f32[16,128,128]{2,1,0:T(8,128)}, u32[]{:S(2)}) copy-start(f32[16,128,128]{2,1,0:T(8,128)} %get-tuple-element.50.refs_3_) | copy-start | bytes 3145732
  104.4 9.0 %copy-start.6 = (f32[16,128,128]{2,1,0:T(8,128)}, f32[16,128,128]{2,1,0:T(8,128)S(1)}, u32[]{:S(2)}) copy-start(f32[16,128,128]{2,1,0:T(8,128)S(1)} %collective-permute-done.14.refs_3_) | copy-start | bytes 3145732
  104.4 20.7 %collective-permute-start.18 = (f32[16,128,128]{2,1,0:T(8,128)S(1)}, f32[16,128,128]{2,1,0:T(8,128)S(1)}, u32[]{:S(2)}, u32[]{:S(2)}) collective-permute-start(f32[16,128,128]{2,1,0:T(8,128)S(1)} %copy-done.14), channel_id=1, source_target_pairs={{0,2},{2,0},{1,3},{3,1},{4,6},{6,4},{5,7},{7,5},{8,10},{10,8},{9,1... | collective-permute-start | bytes 3145736 | tf_op jit(solution)/shard_map/ppermute | solution.py:183
  108.6 4.9 %copy-start.7 = (f32[16,128,128]{2,1,0:T(8,128)}, f32[16,128,128]{2,1,0:T(8,128)S(1)}, u32[]{:S(2)}) copy-start(f32[16,128,128]{2,1,0:T(8,128)S(1)} %collective-permute-done.13.refs_2_) | copy-start | bytes 3145732
  112.6 1.0 copy-start
  113.4 1.0 copy-start.1
  113.4 1.4 copy-start.8
  116.5 19.3 %collective-permute-start.19 = (f32[16,128,128]{2,1,0:T(8,128)}, f32[16,128,128]{2,1,0:T(8,128)S(1)}, u32[]{:S(2)}, u32[]{:S(2)}) collective-permute-start(f32[16,128,128]{2,1,0:T(8,128)} %get-tuple-element.63.refs_5_), channel_id=1, source_target_pairs={{0,2},{2,0},{1,3},{3,1},{4,6},{6,4},{5,7},{7,5},{8,10},{10,8},{9,1... | collective-permute-start | bytes 3145736 | tf_op jit(solution)/shard_map/ppermute | solution.py:183
  116.6 19.2 %collective-permute-start.20 = (f32[16,128,128]{2,1,0:T(8,128)}, f32[16,128,128]{2,1,0:T(8,128)S(1)}, u32[]{:S(2)}, u32[]{:S(2)}) collective-permute-start(f32[16,128,128]{2,1,0:T(8,128)} %get-tuple-element.64.refs_7_), channel_id=1, source_target_pairs={{0,2},{2,0},{1,3},{3,1},{4,6},{6,4},{5,7},{7,5},{8,10},{10,8},{9,1... | collective-permute-start | bytes 3145736 | tf_op jit(solution)/shard_map/ppermute | solution.py:183
  118.3 14.7 %collective-permute-start.16 = (f32[8,128,128]{2,1,0:T(8,128)S(1)}, f32[8,128,128]{2,1,0:T(8,128)S(1)}, u32[]{:S(2)}, u32[]{:S(2)}) collective-permute-start(f32[8,128,128]{2,1,0:T(8,128)S(1)} %get-tuple-element.61), channel_id=1, source_target_pairs={{0,32},{32,64},{64,96},{96,128},{128,160},{160,192},{192,224},{224... | collective-permute-start | bytes 1572872 | tf_op jit(solution)/shard_map/ppermute | solution.py:183
  121.0 14.9 %collective-permute-start.17 = (f32[8,128,128]{2,1,0:T(8,128)S(1)}, f32[8,128,128]{2,1,0:T(8,128)S(1)}, u32[]{:S(2)}, u32[]{:S(2)}) collective-permute-start(f32[8,128,128]{2,1,0:T(8,128)S(1)} %get-tuple-element.62), channel_id=1, source_target_pairs={{0,224},{32,0},{64,32},{96,64},{128,96},{160,128},{192,160},{224,1... | collective-permute-start | bytes 1572872 | tf_op jit(solution)/shard_map/ppermute | solution.py:183
  125.1 10.8 %copy-start.2 = (f32[16,128,128]{2,1,0:T(8,128)}, f32[16,128,128]{2,1,0:T(8,128)S(1)}, u32[]{:S(2)}) copy-start(f32[16,128,128]{2,1,0:T(8,128)S(1)} %collective-permute-done.18.refs_2_) | copy-start | bytes 3145732
  133.1 2.8 %copy-start.15 = (f32[8,128,128]{2,1,0:T(8,128)}, f32[8,128,128]{2,1,0:T(8,128)S(1)}, u32[]{:S(2)}) copy-start(f32[8,128,128]{2,1,0:T(8,128)S(1)} %collective-permute-done.16.refs_0_) | copy-start | bytes 1572868
  135.8 0.8 copy-start.16
  135.8 1.1 copy-start.4
  135.9 1.5 copy-start.5
  144.3 26.1 %collective-permute-start.21 = (f32[16,128,128]{2,1,0:T(8,128)S(1)}, f32[16,128,128]{2,1,0:T(8,128)S(1)}, u32[]{:S(2)}, u32[]{:S(2)}) collective-permute-start(f32[16,128,128]{2,1,0:T(8,128)S(1)} %slice.18), channel_id=1, source_target_pairs={{0,1},{1,0},{2,3},{3,2},{4,5},{5,4},{6,7},{7,6},{8,9},{9,8},{10,11... | collective-permute-start | bytes 3145736 | tf_op jit(solution)/shard_map/ppermute | solution.py:183

commit v3 on v2

v3 whole, which is shorter than its diff:
```python
import jax
import jax.numpy as jnp
from jax import lax
from jax.experimental import pallas as pl
from jax.experimental.pallas import tpu as pltpu
from jax.sharding import Mesh
from jax.sharding import PartitionSpec as P

BS = 128
SA = 16
SCH = 16
N_ROW = 8
N_LEFT = 256
N_RIGHT = 128
PCAP = 512
UNROLL = 16
BINS = 6
LISTED = PCAP + BINS * UNROLL
SPARE = 2 * SCH

SCALARS = pl.BlockSpec(memory_space=pltpu.SMEM)
IN_HBM = pl.BlockSpec(memory_space=pltpu.HBM)
ANYWHERE = pl.BlockSpec(memory_space=pl.ANY)
VMEM = pl.BlockSpec(memory_space=pltpu.VMEM)
TOKEN = jax.ShapeDtypeStruct((1,), jnp.int32)
STATE = (
    pltpu.VMEM((N_LEFT, BS, BS), jnp.float32),
    pltpu.VMEM((N_RIGHT, BS, 2 * BS), jnp.bfloat16),
    pltpu.VMEM((2 * SCH + 1, BS, BS), jnp.float32),
)


def hbm(*arrays):
    return [pltpu.with_memory_space_constraint(a, pltpu.HBM) for a in arrays]


def vmem(*arrays):
    return [pltpu.with_memory_space_constraint(a, pltpu.VMEM) for a in arrays]


def split(block):
    high = block.astype(jnp.bfloat16)
    low = (block - high.astype(jnp.float32)).astype(jnp.bfloat16)
    return high, low


def block_product(left, right):
    lhs = jnp.concatenate(split(left), axis=1)
    rhs = jnp.concatenate([right, right], axis=0)
    both = lax.dot_general(lhs, rhs, (((1,), (0,)), ((), ())), preferred_element_type=jnp.float32)
    return both[:, :BS] + both[:, BS:]


def stage_kernel(bins, parts, n_rights, first, base, starts, bounds, listed, *refs):
    lefts, rights, refs = refs[: len(parts)], refs[len(parts) : len(parts) + n_rights], refs[len(parts) + n_rights :]
    if not first:
        refs = refs[3:]
    left, right, total, done, sems = refs
    copies = []
    for piece, n in zip(lefts, parts):
        length = piece.shape[0] // n
        for part in range(n):
            i = len(copies)
            source = piece.at[pl.ds(part * length, length)]
            copies.append(pltpu.make_async_copy(source, left.at[pl.ds(starts[base + i], length)], sems.at[i]))
    for copy in copies:
        copy.start()
    if first:
        total[...] = jnp.zeros_like(total)
    for i, piece in enumerate(rights):
        place = starts[base + len(copies) + i]

        def prepare(turn, carry, piece=piece, place=place):
            for step in range(8):
                block = turn * 8 + step
                high, low = split(piece[block])
                right[place + block, :, :BS] = high.T
                right[place + block, :, BS:] = low.T
            return carry

        lax.fori_loop(0, piece.shape[0] // 8, prepare, 0)
    for copy in copies:
        copy.wait()

    def accumulate(turn, carry):
        products, targets = [], []
        for step in range(UNROLL):
            code = listed[turn * UNROLL + step]
            targets.append(code & 255)
            products.append(block_product(left[code >> 16], right[(code >> 8) & 255]))
        for target, product in zip(targets, products):
            total[target] = total[target] + product
        return carry

    lax.fori_loop(bounds[bins[0]], bounds[bins[1]], accumulate, 0)
    done[0] = bounds[0]


def stage(bins, base, lefts, rights, bounds, listed, starts, state=None, flops=0, place=IN_HBM, tokens=()):
    parts, pieces = [n for n, _ in lefts], [a for _, a in lefts]
    n = len(tokens) + 3 + len(lefts) + len(rights)
    aliases = {} if state is None else {n + i: i for i in range(3)}
    *state, token = pl.pallas_call(
        lambda *refs: stage_kernel(bins, parts, len(rights), not aliases, base, *refs[len(tokens) :]),
        out_shape=[*STATE, TOKEN],
        in_specs=[SCALARS] * (len(tokens) + 3) + [place] * len(lefts) + [VMEM] * (len(rights) + len(aliases)),
        out_specs=[VMEM] * 3 + [SCALARS],
        input_output_aliases=aliases,
        scratch_shapes=[pltpu.SemaphoreType.DMA((max(1, sum(parts)),))],
        compiler_params=pltpu.CompilerParams(vmem_limit_bytes=10 << 20),
        cost_estimate=pl.CostEstimate(flops=flops, bytes_accessed=0, transcendentals=0),
        name="stage_" + "_".join(map(str, bins)),
    )(*tokens, starts, bounds, listed, *(hbm(*pieces) if place is IN_HBM else pieces), *vmem(*rights), *(state or ()))
    return state, token


def tie_kernel(*refs):
    token, scratch = refs[-2:]
    scratch[...] = jnp.zeros_like(scratch)
    token[0] = 0


def tie(arrays, tokens=(), place=ANYWHERE):
    shape = jax.ShapeDtypeStruct if place is ANYWHERE else pltpu.HBM
    *arrays, token = pl.pallas_call(
        tie_kernel,
        out_shape=[shape(a.shape, a.dtype) for a in arrays] + [TOKEN],
        in_specs=[place] * len(arrays) + [SCALARS] * len(tokens),
        out_specs=[place] * len(arrays) + [SCALARS],
        input_output_aliases={i: i for i in range(len(arrays))},
        scratch_shapes=[pltpu.VMEM((8, BS), jnp.float32)],
        compiler_params=pltpu.CompilerParams(vmem_limit_bytes=1 << 20),
        cost_estimate=pl.CostEstimate(flops=0, bytes_accessed=0, transcendentals=0),
        name="tie",
    )(*(arrays if place is ANYWHERE else hbm(*arrays)), *tokens)
    return arrays, token


def witness(arrays, tokens=()):
    return pl.pallas_call(
        tie_kernel,
        out_shape=TOKEN,
        in_specs=[ANYWHERE] * len(arrays) + [SCALARS] * len(tokens),
        out_specs=SCALARS,
        scratch_shapes=[pltpu.VMEM((8, BS), jnp.float32)],
        compiler_params=pltpu.CompilerParams(vmem_limit_bytes=1 << 20),
        cost_estimate=pl.CostEstimate(flops=0, bytes_accessed=0, transcendentals=0),
        name="witness",
    )(*arrays, *tokens)


def pack_kernel(n, *refs):
    pieces, (out, bounce, into, leave) = refs[:n], refs[-4:]
    slots = [pl.ds(i * SA, SA) for i in range(n)]
    fill = [pltpu.make_async_copy(piece, bounce.at[rows], into.at[i]) for i, (piece, rows) in enumerate(zip(pieces, slots))]
    drain = [pltpu.make_async_copy(bounce.at[rows], out.at[rows], leave.at[i]) for i, rows in enumerate(slots)]
    for copy in fill:
        copy.start()
    for first, second in zip(fill, drain):
        first.wait()
        second.start()
    for copy in drain:
        copy.wait()


def pack(*pieces, later_than=()):
    n = len(pieces)
    return pl.pallas_call(
        lambda *refs: pack_kernel(n, *refs),
        out_shape=pltpu.HBM((n * SA, BS, BS), jnp.float32),
        in_specs=[IN_HBM] * (n + len(later_than)),
        out_specs=IN_HBM,
        scratch_shapes=[
            pltpu.VMEM((n * SA, BS, BS), jnp.float32),
            pltpu.SemaphoreType.DMA((n,)),
            pltpu.SemaphoreType.DMA((n,)),
        ],
        compiler_params=pltpu.CompilerParams(vmem_limit_bytes=(n + 1) << 20),
        cost_estimate=pl.CostEstimate(flops=0, bytes_accessed=0, transcendentals=0),
        name="pack",
    )(*hbm(*pieces, *later_than))


def shift(value, axis, by):
    size = lax.axis_size(axis)
    return lax.ppermute(value, axis, [(i, (i + by) % size) for i in range(size)])


def shift_apart(value, axis):
    size = lax.axis_size(axis)
    pairs = [(2 * i + core, (i + 1 - 2 * core) % size * 2 + core) for i in range(size) for core in range(2)]
    return lax.ppermute(value, (axis, "core"), pairs)


def order(left_index, right_index, target_index, count, row, layer, left_class):
    p = jnp.arange(PCAP, dtype=jnp.int32)
    away = (right_index // SA - row) % N_ROW
    kept = target_index // SCH == layer
    right_class = jnp.where((away <= 2) | (away >= 6), 0, jnp.where(away == 4, 2, 1))
    here = jnp.maximum(left_class, right_class)
    bins = jnp.where(here == 0, jnp.where(kept, 1, 0), jnp.where(kept, 5, 1 + here + (here == 2) * (target_index % SCH // (SCH // 2))))
    bins = jnp.where(p < count, bins, BINS)
    target = jnp.where(kept, 0, SCH) + target_index % SCH
    code = (left_index << 16) | (right_index << 8) | target
    same = bins[:, None] == bins[None, :]
    rank = jnp.sum(same & (p[None, :] < p[:, None]), axis=1, dtype=jnp.int32)
    held = jnp.sum(bins[None, :] == jnp.arange(BINS, dtype=jnp.int32)[:, None], axis=1, dtype=jnp.int32)
    groups = (held + UNROLL - 1) // UNROLL
    b = jnp.arange(BINS + 1, dtype=jnp.int32)
    bounds = jnp.sum(jnp.where(b[None, :BINS] < b[:, None], groups[None, :], 0), axis=1, dtype=jnp.int32)
    start = jnp.sum(jnp.where(bins[:, None] == b[None, :BINS], bounds[None, :BINS] * UNROLL, 0), axis=1)
    place = jnp.where(bins < BINS, start + rank, -1)
    slot = jnp.arange(LISTED, dtype=jnp.int32)
    hit = place[None, :] == slot[:, None]
    listed = SPARE + jnp.sum(jnp.where(hit, code[None, :] - SPARE, 0), axis=1, dtype=jnp.int32)
    return bounds, listed


def body(slab_blocks, factor_blocks, stack_left, stack_right, stack_target, stack_counts):
    row, layer = lax.axis_index("row"), lax.axis_index("layer")
    y, x, core = lax.axis_index("y"), lax.axis_index("x"), lax.axis_index("core")

    left_index = stack_left.reshape(-1)
    across_y = (left_index // (4 * SA) - y) % 4
    across_x = (left_index // (2 * SA) - x) % 2
    left_class = jnp.where(across_x == 0, jnp.where(across_y == 2, 1, 0), jnp.where(across_y < 2, across_y, 2))
    bounds, listed = order(
        left_index,
        stack_right.reshape(-1),
        stack_target.reshape(-1),
        stack_counts.reshape(()),
        row,
        layer,
        left_class,
    )

    def left_at(dy, dx, dc, first=0):
        return (((y + dy) % 4 * 2 + (x + dx) % 2) * 2 + (core + dc) % 2) * SA + first

    def right_at(away, first=0):
        return (row + away) % N_ROW * SA + first

    own = slab_blocks.reshape(SA, BS, BS)
    mine = lax.all_to_all(factor_blocks.reshape(SA, BS, BS), ("y", "x", "core"), split_axis=0, concat_axis=0, tiled=True)

    first_places = [left_at(0, 0, 0), left_at(0, 0, 1), left_at(-1, 0, 0), left_at(1, 0, 0), left_at(0, 1, 0)]
    first_places += [left_at(-1, 0, 1), left_at(1, 0, 1), left_at(0, 1, 1)]
    first_places += [right_at(away) for away in (0, -1, 1, -2, 2)]
    second_places = [left_at(dy, dx, dc) for dy, dx in ((2, 0), (1, 1)) for dc in range(2)] + [right_at(-3), right_at(3)]
    third_places = [left_at(dy, 1, dc) for dy in (-1, 2) for dc in range(2)] + [right_at(4)]
    starts = jnp.stack(first_places + second_places + third_places)
    second, third = len(first_places), len(first_places) + len(second_places)

    up1, down1 = shift(mine, "row", 1), shift(mine, "row", -1)
    own_c = shift(own, "core", 1)
    sent = pack(own, later_than=(shift(own[:1], "core", 1),))
    own_up, own_down, across = shift(sent, "y", 1), shift(sent, "y", -1), shift(sent, "x", 1)
    own_up_c, own_down_c, across_c = shift(own_up, "core", 1), shift(own_down, "core", 1), shift(across, "core", 1)
    z1 = witness((up1, down1))
    (own_up, own_down, across, own_c, own_up_c, own_down_c, across_c), _ = tie(
        (own_up, own_down, across, own_c, own_up_c, own_down_c, across_c), (z1,), IN_HBM
    )

    up2, down2 = shift(up1, "row", 1), shift(down1, "row", -1)
    own_far, across_down, across_up = shift(own_up, "y", 1), shift(across, "y", -1), shift(own_up, "x", 1)
    z2 = witness((up2, down2))
    (own_far, across_down, across_up), t2 = tie((own_far, across_down, across_up), (z2,), IN_HBM)

    up3, down3 = shift(up2, "row", 1), shift(down2, "row", -1)
    far = shift_apart(jnp.where(core == 0, across_up, across_down), "y")
    across_down_c = shift(across_down, "core", 1)
    lefts = [(1, a) for a in (own, own_c, own_up, own_down, across, own_up_c, own_down_c, across_c)]
    state, done = stage((0, 2), 0, lefts, [mine, up1, down1, up2, down2], bounds, listed, starts, flops=8 * 10**9, tokens=(t2,))

    (own_far,), _ = tie((own_far,), (done,), IN_HBM)
    own_far_c = shift(own_far, "core", 1)

    opposite = shift_apart(jnp.where(core == 0, up3, down3), "row")
    far_c, across_up_c = shift(far, "core", 1), shift(across_up, "core", 1)
    lefts = [(1, a) for a in (own_far, own_far_c, across_down, across_down_c)]
    state, done = stage((2, 3), second, lefts, [up3, down3], bounds, listed, starts, state, flops=10**9)

    lefts = [(1, a) for a in (across_up, across_up_c, far, far_c)]
    state, _ = stage((3, 4), third, lefts, [opposite], bounds, listed, starts, state, place=ANYWHERE)
    arrived_low = shift(state[2][SCH : SCH + SCH // 2], "layer", 1)
    state, _ = stage((4, 5), 0, [], [], bounds, listed, starts, state)
    arrived_high = shift(state[2][SCH + SCH // 2 : 2 * SCH], "layer", 1)
    state, _ = stage((5, 6), 0, [], [], bounds, listed, starts, state, flops=10**10)
    summed = state[2][:SCH] + jnp.concatenate([arrived_low, arrived_high])
    return summed.reshape((1, 1, 1) + summed.shape)


def solution(mesh):
    fine = Mesh(mesh.devices.reshape(8, 4, 2, 2, 2), ("row", "y", "x", "core", "layer"))
    col = ("y", "x", "core")
    return jax.shard_map(
        body,
        mesh=fine,
        in_specs=(
            P("row", col, "layer", None, None, None),
            P("row", col, "layer", None, None, None, None),
            P("row", col, "layer", None),
            P("row", col, "layer", None),
            P("row", col, "layer", None),
            P("row", col, "layer"),
        ),
        out_specs=P("row", col, "layer", None, None, None),
        check_vma=False,
    )
```

time: 175 us -> 150 us (0.86); the launches traced: 171 us -> 148 us
  waiting for transfers between devices: 98.1 us -> 84.3 us
  Pallas kernels: 31.1 us -> 24.2 us
  local copies, waits for them, and re-layouts: 9.28 us -> 5.42 us
    ppermute x22 -> x23, waiting for transfers between devices: 89.2 us -> 70.6 us  [shift(): lax.ppermute(value, axis, [(i, (i + by) % size) for i in range(size)])]
    ppermute x0 -> x2, waiting for transfers between devices: none -> 6.7 us  [shift_apart(): return lax.ppermute(value, (axis, 'core'), pairs)]
    unnamed x46 -> x20, local copies, waits for them, and re-layouts: 9.11 us -> 4.4 us
    pallas_call x9 -> x10, Pallas kernels: 26 us -> 22 us  [the longest x5 17.6 us: stage(): pl.pallas_call(lambda *refs: stage_kernel(bins, parts, len(rights), not a...]
    ppermute x22 -> x23, starting transfers between devices: 24 us -> 20.6 us  [shift(): lax.ppermute(value, axis, [(i, (i + by) % size) for i in range(size)])]
    ppermute x0 -> x2, starting transfers between devices: none -> 3.43 us  [shift_apart(): return lax.ppermute(value, (axis, 'core'), pairs)]
    pallas_call x2 -> x1, Pallas kernels: 5.17 us -> 2.21 us  [pack(): pl.pallas_call(lambda *refs: pack_kernel(n, *refs), out_shape=pltpu.HBM((...]
    all_to_all x1, waiting for transfers between devices: 8.84 us -> 7 us  [body(): lax.all_to_all(factor_blocks.reshape(SA, BS, BS), ('y', 'x', 'core'), spl...]
  transfers between devices with their start and end apart: 23 -> 26, of which waited for: 11 -> 12; matrix products, arithmetic and copies ran while one was open for 1% -> 2% of each run, Pallas kernels for 14% -> 15%
where the time goes in v3:
time: 150 us; the launch traced here: 148 us
  waiting for transfers between devices  84.3 us (56%)
  starting transfers between devices  30.1 us (20%)
  Pallas kernels  24.2 us (16%)
  local copies, waits for them, and re-layouts  5.42 us (4%)
  other arithmetic  3.41 us (2%)
    ppermute x23, waiting for transfers between devices, shift(): lax.ppermute(value, axis, [(i, (i + by) % size) for i in range(size)])  70.6 us
    ppermute x23, starting transfers between devices, shift(): lax.ppermute(value, axis, [(i, (i + by) % size) for i in range(size)])  20.6 us
    pallas_call x5, Pallas kernels, stage(): pl.pallas_call(lambda *refs: stage_kernel(bins, parts, len(rights), not a...  17.6 us
    all_to_all x1, waiting for transfers between devices, body(): lax.all_to_all(factor_blocks.reshape(SA, BS, BS), ('y', 'x', 'core'), spl...  7 us
    ppermute x2, waiting for transfers between devices, shift_apart(): return lax.ppermute(value, (axis, 'core'), pairs)  6.7 us
    all_to_all x1, starting transfers between devices, body(): lax.all_to_all(factor_blocks.reshape(SA, BS, BS), ('y', 'x', 'core'), spl...  6.09 us
    unnamed x20, local copies, waits for them, and re-layouts  4.4 us
    ppermute x2, starting transfers between devices, shift_apart(): return lax.ppermute(value, (axis, 'core'), pairs)  3.43 us
  transfers between devices with their start and end apart: 26, of which 12 were waited for; matrix products, arithmetic and copies ran while one was open for 2% of the time, Pallas kernels for 15%

profile of v3, /device:TPU:34, one launch (start us, length us, event | category | flops | bytes accessed | tf_op | source)
XLA Modules:
  0.0 148.4 jit_solution(3188849530768166994)
XLA Ops:
  0.0 6.1 %all-to-all-start = ((f32[16,128,128]{2,1,0:T(8,128)}), f32[16,128,128]{2,1,0:T(8,128)S(1)}, u32[]{:S(2)}, u32[]{:S(2)}) async-start(f32[16,128,128]{2,1,0:T(8,128)} %bitcast.39), calls=%async_computation | async-start | bytes 2097152 | tf_op jit(solution)/shard_map/all_to_all | solution.py:244
  6.1 0.8 slice_bitcast_fusion
  6.9 0.1 collective-permute-start
  7.1 1.1 collective-permute-done.refs_1_
  8.2 0.6 copy-done.6
  8.8 2.2 %pack.1 = f32[16,128,128]{2,1,0:T(8,128)} custom-call(f32[16,128,128]{2,1,0:T(8,128)} %bitcast.36, f32[1,128,128]{2,1,0:T(8,128)} %copy-done.6), custom_call_target="tpu_custom_call" | custom-call | tf_op jit(solution)/shard_map/pack/pallas_call | solution.py:168
  11.0 1.5 %collective-permute-start.1 = (f32[16,128,128]{2,1,0:T(8,128)}, f32[16,128,128]{2,1,0:T(8,128)}, u32[]{:S(2)}, u32[]{:S(2)}) collective-permute-start(f32[16,128,128]{2,1,0:T(8,128)} %pack.1), channel_id=1, source_target_pairs={{0,8},{8,16},{16,24},{24,0},{1,9},{9,17},{17,25},{25,1},{2,10},{10... | collective-permute-start | bytes 3145736 | tf_op jit(solution)/shard_map/ppermute | solution.py:186
  12.6 1.8 %collective-permute-start.2 = (f32[16,128,128]{2,1,0:T(8,128)}, f32[16,128,128]{2,1,0:T(8,128)}, u32[]{:S(2)}, u32[]{:S(2)}) collective-permute-start(f32[16,128,128]{2,1,0:T(8,128)} %pack.1), channel_id=1, source_target_pairs={{0,24},{8,0},{16,8},{24,16},{1,25},{9,1},{17,9},{25,17},{2,26},{10... | collective-permute-start | bytes 3145736 | tf_op jit(solution)/shard_map/ppermute | solution.py:186
  14.3 0.2 collective-permute-start.3
  14.5 7.0 %all-to-all-done.refs_12_ = f32[16,128,128]{2,1,0:T(8,128)S(1)} async-done(((f32[16,128,128]{2,1,0:T(8,128)}), f32[16,128,128]{2,1,0:T(8,128)S(1)}, u32[]{:S(2)}, u32[]{:S(2)}) %all-to-all-start) | async-done | bytes 1048608 | tf_op jit(solution)/shard_map/all_to_all | solution.py:244
  21.5 1.9 %collective-permute-start.8 = (f32[16,128,128]{2,1,0:T(8,128)S(1)}, f32[16,128,128]{2,1,0:T(8,128)S(1)}, u32[]{:S(2)}, u32[]{:S(2)}) collective-permute-start(f32[16,128,128]{2,1,0:T(8,128)S(1)} %all-to-all-done.refs_12_), channel_id=1, source_target_pairs={{0,32},{32,64},{64,96},{96,128},{128,160},{160,192},{192,224},{224... | collective-permute-start | bytes 3145736 | tf_op jit(solution)/shard_map/ppermute | solution.py:186
  23.4 0.1 collective-permute-start.9
  23.5 20.3 %collective-permute-done.1.refs_0_ = f32[16,128,128]{2,1,0:T(8,128)} collective-permute-done((f32[16,128,128]{2,1,0:T(8,128)}, f32[16,128,128]{2,1,0:T(8,128)}, u32[]{:S(2)}, u32[]{:S(2)}) %collective-permute-start.1) | collective-permute-done | bytes 1048608 | tf_op jit(solution)/shard_map/ppermute | solution.py:186
  43.8 0.1 collective-permute-start.4
  43.9 0.4 collective-permute-start.5
  44.3 0.1 collective-permute-start.6
  44.4 2.2 %collective-permute-done.8.refs_0_.refs_13_ = f32[16,128,128]{2,1,0:T(8,128)S(1)} collective-permute-done((f32[16,128,128]{2,1,0:T(8,128)S(1)}, f32[16,128,128]{2,1,0:T(8,128)S(1)}, u32[]{:S(2)}, u32[]{:S(2)}) %collective-permute-start.8) | collective-permute-done | bytes 1048608 | tf_op jit(solution)/shard_map/ppermute | solution.py:186
  47.3 0.1 stack.99.refs_1_.refs_0_
  47.5 0.1 convert_reduce_fusion.1
  47.6 0.1 select_reduce_fusion.2.refs_2_.refs_1_
  47.7 0.7 collective-permute-done.9.refs_1_.refs_14_
  48.4 3.1 %collective-permute-start.13 = (f32[16,128,128]{2,1,0:T(8,128)S(1)}, f32[16,128,128]{2,1,0:T(8,128)S(1)}, u32[]{:S(2)}, u32[]{:S(2)}) collective-permute-start(f32[16,128,128]{2,1,0:T(8,128)S(1)} %collective-permute-done.8.refs_0_.refs_13_), channel_id=1, source_target_pairs={{0,32},{32,64},{64,96},{96,128},{128,160},{160,192},{192,224},{224... | collective-permute-start | bytes 3145736 | tf_op jit(solution)/shard_map/ppermute | solution.py:186
  51.6 0.5 witness.2.refs_7_
  52.1 0.0 collective-permute-done.4.refs_3_
  52.1 0.6 collective-permute-start.14
  52.7 0.0 collective-permute-done.7.refs_6_
  52.7 1.2 tie.3
  53.8 0.1 collective-permute-start.10
  54.0 1.1 collective-permute-start.12
  55.1 3.0 %collective-permute-start.11 = (f32[16,128,128]{2,1,0:T(8,128)}, f32[16,128,128]{2,1,0:T(8,128)S(1)}, u32[]{:S(2)}, u32[]{:S(2)}) collective-permute-start(f32[16,128,128]{2,1,0:T(8,128)} %get-tuple-element.32.refs_8_), channel_id=1, source_target_pairs={{0,24},{8,0},{16,8},{24,16},{1,25},{9,1},{17,9},{25,17},{2,26},{10... | collective-permute-start | bytes 3145736 | tf_op jit(solution)/shard_map/ppermute | solution.py:186
  58.0 0.1 select_reduce_fusion.1
  58.1 0.2 convert_reduce_fusion
  58.4 0.2 select_reduce_fusion
  58.6 17.3 %collective-permute-done.13.refs_0_.refs_15_ = f32[16,128,128]{2,1,0:T(8,128)S(1)} collective-permute-done((f32[16,128,128]{2,1,0:T(8,128)S(1)}, f32[16,128,128]{2,1,0:T(8,128)S(1)}, u32[]{:S(2)}, u32[]{:S(2)}) %collective-permute-start.13) | collective-permute-done | bytes 1048608 | tf_op jit(solution)/shard_map/ppermute | solution.py:186
  75.9 0.2 collective-permute-start.18
  76.0 1.1 collective-permute-done.14.refs_1_.refs_16_
  77.1 0.5 witness.3.refs_3_
  77.6 2.0 %collective-permute-start.19 = (f32[16,128,128]{2,1,0:T(8,128)S(1)}, f32[16,128,128]{2,1,0:T(8,128)S(1)}, u32[]{:S(2)}, u32[]{:S(2)}) collective-permute-start(f32[16,128,128]{2,1,0:T(8,128)S(1)} %collective-permute-done.14.refs_1_.refs_16_), channel_id=1, source_target_pairs={{0,224},{32,0},{64,32},{96,64},{128,96},{160,128},{192,160},{224,1... | collective-permute-start | bytes 3145736 | tf_op jit(solution)/shard_map/ppermute | solution.py:186
  79.6 1.0 collective-permute-done.10.refs_0_
  80.6 1.0 copy-done.2
  81.6 0.4 copy-done
  82.0 1.1 copy-done.3
  83.1 1.1 tie.4
  84.2 0.1 collective-permute-start.22
  84.3 0.5 collective-permute-start.15
  84.8 1.3 broadcast_select_fusion.1
  86.1 0.1 collective-permute-start.16
  86.2 7.0 %stage_0_2.1 = (f32[256,128,128]{2,1,0:T(8,128)S(1)}, bf16[128,128,256]{2,1,0:T(8,128)(2,1)S(1)}, f32[33,128,128]{2,1,0:T(8,128)S(1)}, s32[1]{0:T(128)}) custom-call(s32[1]{0:T(128)} %get-tuple-element.36.refs_0_, s32[24]{0:T(128)S(1)} %stack.99.refs_1_.refs_0_, s32[7]{0:T(128)S(1)} %select_reduce_fusion.2.refs_2_.refs_1_, ...), custom_call_target="tpu_custom_call" | custom-call | flops 8000000000 | tf_op jit(solution)/shard_map/stage_0_2/pallas_call | solution.py:103
  93.2 1.1 tie.5
  94.3 7.5 %collective-permute-done.18.refs_7_ = f32[16,128,128]{2,1,0:T(8,128)S(1)} collective-permute-done((f32[16,128,128]{2,1,0:T(8,128)S(1)}, f32[16,128,128]{2,1,0:T(8,128)S(1)}, u32[]{:S(2)}, u32[]{:S(2)}) %collective-permute-start.18) | collective-permute-done | bytes 1048608 | tf_op jit(solution)/shard_map/ppermute | solution.py:186
  101.9 1.5 collective-permute-done.19.refs_8_
  103.3 0.1 broadcast_select_fusion
  103.5 3.4 %collective-permute-start.20 = (f32[16,128,128]{2,1,0:T(8,128)S(1)}, f32[16,128,128]{2,1,0:T(8,128)S(1)}, u32[]{:S(2)}, u32[]{:S(2)}) collective-permute-start(f32[16,128,128]{2,1,0:T(8,128)S(1)} %broadcast_select_fusion), channel_id=1, source_target_pairs={{0,32},{2,226},{32,64},{34,2},{64,96},{66,34},{96,128},{98,66},{12... | collective-permute-start | bytes 3145736 | tf_op jit(solution)/shard_map/ppermute | solution.py:192
  106.9 1.0 copy-done.5
  107.8 0.4 copy-done.4
  108.2 4.2 %stage_2_3.1 = (f32[256,128,128]{2,1,0:T(8,128)S(1)}, bf16[128,128,256]{2,1,0:T(8,128)(2,1)S(1)}, f32[33,128,128]{2,1,0:T(8,128)S(1)}, s32[1]{0:T(128)}) custom-call(s32[24]{0:T(128)S(1)} %stack.99.refs_1_.refs_0_, s32[7]{0:T(128)S(1)} %select_reduce_fusion.2.refs_2_.refs_1_, ...), custom_call_target="tpu_custom_call", output_to_operand_aliasing={{0}: (9, {}), {1}: (10, {}), {2}: (11, {})} | custom-call | flops 1000000000 | tf_op jit(solution)/shard_map/stage_2_3/pallas_call | solution.py:103
  112.4 6.7 %collective-permute-done.20.refs_7_ = f32[16,128,128]{2,1,0:T(8,128)S(1)} collective-permute-done((f32[16,128,128]{2,1,0:T(8,128)S(1)}, f32[16,128,128]{2,1,0:T(8,128)S(1)}, u32[]{:S(2)}, u32[]{:S(2)}) %collective-permute-start.20) | collective-permute-done | bytes 1048608 | tf_op jit(solution)/shard_map/ppermute | solution.py:192
  119.1 2.3 %stage_3_4.1 = (f32[256,128,128]{2,1,0:T(8,128)S(1)}, bf16[128,128,256]{2,1,0:T(8,128)(2,1)S(1)}, f32[33,128,128]{2,1,0:T(8,128)S(1)}, s32[1]{0:T(128)}) custom-call(s32[24]{0:T(128)S(1)} %stack.99.refs_1_.refs_0_, s32[7]{0:T(128)S(1)} %select_reduce_fusion.2.refs_2_.refs_1_, ...), custom_call_target="tpu_custom_call", output_to_operand_aliasing={{0}: (8, {}), {1}: (9, {}), {2}: (10, {})} | custom-call | tf_op jit(solution)/shard_map/stage_3_4/pallas_call | solution.py:103
  121.5 2.7 %collective-permute-start.23 = (f32[8,128,128]{2,1,0:T(8,128)S(1)}, f32[8,128,128]{2,1,0:T(8,128)S(1)}, u32[]{:S(2)}, u32[]{:S(2)}) collective-permute-start(f32[8,128,128]{2,1,0:T(8,128)S(1)} %slice.29), channel_id=1, source_target_pairs={{0,1},{1,0},{2,3},{3,2},{4,5},{5,4},{6,7},{7,6},{8,9},{9,8},{10,11... | collective-permute-start | bytes 1572872 | tf_op jit(solution)/shard_map/ppermute | solution.py:186
  124.1 1.6 %stage_4_5.1 = (f32[256,128,128]{2,1,0:T(8,128)S(1)}, bf16[128,128,256]{2,1,0:T(8,128)(2,1)S(1)}, f32[33,128,128]{2,1,0:T(8,128)S(1)}, s32[1]{0:T(128)}) custom-call(s32[24]{0:T(128)S(1)} %stack.99.refs_1_.refs_0_, s32[7]{0:T(128)S(1)} %select_reduce_fusion.2.refs_2_.refs_1_, ...), custom_call_target="tpu_custom_call", output_to_operand_aliasing={{0}: (3, {}), {1}: (4, {}), {2}: (5, {})} | custom-call | tf_op jit(solution)/shard_map/stage_4_5/pallas_call | solution.py:103
  125.8 1.0 collective-permute-start.24
  126.8 2.5 %stage_5_6.1 = (f32[256,128,128]{2,1,0:T(8,128)S(1)}, bf16[128,128,256]{2,1,0:T(8,128)(2,1)S(1)}, f32[33,128,128]{2,1,0:T(8,128)S(1)}, s32[1]{0:T(128)}) custom-call(s32[24]{0:T(128)S(1)} %stack.99.refs_1_.refs_0_, s32[7]{0:T(128)S(1)} %select_reduce_fusion.2.refs_2_.refs_1_, ...), custom_call_target="tpu_custom_call", output_to_operand_aliasing={{0}: (3, {}), {1}: (4, {}), {2}: (5, {})} | custom-call | flops 10000000000 | tf_op jit(solution)/shard_map/stage_5_6/pallas_call | solution.py:103
  129.3 17.9 %collective-permute-done.24 = f32[8,128,128]{2,1,0:T(8,128)S(1)} collective-permute-done((f32[8,128,128]{2,1,0:T(8,128)S(1)}, f32[8,128,128]{2,1,0:T(8,128)S(1)}, u32[]{:S(2)}, u32[]{:S(2)}) %collective-permute-start.24) | collective-permute-done | bytes 524320 | tf_op jit(solution)/shard_map/ppermute | solution.py:186
  147.3 1.1 fusion
  (37 shorter events, 0.2 us)
Async XLA Ops:
  0.0 47.4 %copy-start.7 = (s32[1,1,1,512]{3,2,1,0:T(1,128)S(1)}, s32[1,1,1,512]{3,2,1,0:T(1,128)}, u32[]{:S(2)}) copy-start(s32[1,1,1,512]{3,2,1,0:T(1,128)} %param.9) | copy-start | bytes 6148
  0.0 47.4 %copy-start.8 = (s32[1,1,1,512]{3,2,1,0:T(1,128)S(1)}, s32[1,1,1,512]{3,2,1,0:T(1,128)}, u32[]{:S(2)}) copy-start(s32[1,1,1,512]{3,2,1,0:T(1,128)} %param.8) | copy-start | bytes 6148
  0.0 47.4 %copy-start.9 = (s32[1,1,1,512]{3,2,1,0:T(1,128)S(1)}, s32[1,1,1,512]{3,2,1,0:T(1,128)}, u32[]{:S(2)}) copy-start(s32[1,1,1,512]{3,2,1,0:T(1,128)} %param.10) | copy-start | bytes 6148
  0.0 21.5 %all-to-all-start = ((f32[16,128,128]{2,1,0:T(8,128)}), f32[16,128,128]{2,1,0:T(8,128)S(1)}, u32[]{:S(2)}, u32[]{:S(2)}) async-start(f32[16,128,128]{2,1,0:T(8,128)} %bitcast.39), calls=%async_computation | async-start | bytes 2097152 | tf_op jit(solution)/shard_map/all_to_all | solution.py:244
  6.9 1.3 collective-permute-start
  8.2 0.6 copy-start.6
  11.0 32.8 %collective-permute-start.1 = (f32[16,128,128]{2,1,0:T(8,128)}, f32[16,128,128]{2,1,0:T(8,128)}, u32[]{:S(2)}, u32[]{:S(2)}) collective-permute-start(f32[16,128,128]{2,1,0:T(8,128)} %pack.1), channel_id=1, source_target_pairs={{0,8},{8,16},{16,24},{24,0},{1,9},{9,17},{17,25},{25,1},{2,10},{10... | collective-permute-start | bytes 3145736 | tf_op jit(solution)/shard_map/ppermute | solution.py:186
  12.6 31.3 %collective-permute-start.2 = (f32[16,128,128]{2,1,0:T(8,128)}, f32[16,128,128]{2,1,0:T(8,128)}, u32[]{:S(2)}, u32[]{:S(2)}) collective-permute-start(f32[16,128,128]{2,1,0:T(8,128)} %pack.1), channel_id=1, source_target_pairs={{0,24},{8,0},{16,8},{24,16},{1,25},{9,1},{17,9},{25,17},{2,26},{10... | collective-permute-start | bytes 3145736 | tf_op jit(solution)/shard_map/ppermute | solution.py:186
  14.3 30.0 %collective-permute-start.3 = (f32[16,128,128]{2,1,0:T(8,128)}, f32[16,128,128]{2,1,0:T(8,128)}, u32[]{:S(2)}, u32[]{:S(2)}) collective-permute-start(f32[16,128,128]{2,1,0:T(8,128)} %pack.1), channel_id=1, source_target_pairs={{0,4},{4,0},{1,5},{5,1},{2,6},{6,2},{3,7},{7,3},{8,12},{12,8},{9,1... | collective-permute-start | bytes 3145736 | tf_op jit(solution)/shard_map/ppermute | solution.py:186
  21.5 25.1 %collective-permute-start.8 = (f32[16,128,128]{2,1,0:T(8,128)S(1)}, f32[16,128,128]{2,1,0:T(8,128)S(1)}, u32[]{:S(2)}, u32[]{:S(2)}) collective-permute-start(f32[16,128,128]{2,1,0:T(8,128)S(1)} %all-to-all-done.refs_12_), channel_id=1, source_target_pairs={{0,32},{32,64},{64,96},{96,128},{128,160},{160,192},{192,224},{224... | collective-permute-start | bytes 3145736 | tf_op jit(solution)/shard_map/ppermute | solution.py:186
  23.4 25.0 %collective-permute-start.9 = (f32[16,128,128]{2,1,0:T(8,128)S(1)}, f32[16,128,128]{2,1,0:T(8,128)S(1)}, u32[]{:S(2)}, u32[]{:S(2)}) collective-permute-start(f32[16,128,128]{2,1,0:T(8,128)S(1)} %all-to-all-done.refs_12_), channel_id=1, source_target_pairs={{0,224},{32,0},{64,32},{96,64},{128,96},{160,128},{192,160},{224,1... | collective-permute-start | bytes 3145736 | tf_op jit(solution)/shard_map/ppermute | solution.py:186
  43.8 8.3 %collective-permute-start.4 = (f32[16,128,128]{2,1,0:T(8,128)}, f32[16,128,128]{2,1,0:T(8,128)}, u32[]{:S(2)}, u32[]{:S(2)}) collective-permute-start(f32[16,128,128]{2,1,0:T(8,128)} %bitcast.37), channel_id=1, source_target_pairs={{0,2},{2,0},{1,3},{3,1},{4,6},{6,4},{5,7},{7,5},{8,10},{10,8},{9,1... | collective-permute-start | bytes 3145736 | tf_op jit(solution)/shard_map/ppermute | solution.py:186
  43.9 8.8 %collective-permute-start.5 = (f32[16,128,128]{2,1,0:T(8,128)}, f32[16,128,128]{2,1,0:T(8,128)}, u32[]{:S(2)}, u32[]{:S(2)}) collective-permute-start(f32[16,128,128]{2,1,0:T(8,128)} %collective-permute-done.1.refs_0_), channel_id=1, source_target_pairs={{0,2},{2,0},{1,3},{3,1},{4,6},{6,4},{5,7},{7,5},{8,10},{10,8},{9,1... | collective-permute-start | bytes 3145736 | tf_op jit(solution)/shard_map/ppermute | solution.py:186
  44.3 8.4 %collective-permute-start.6 = (f32[16,128,128]{2,1,0:T(8,128)}, f32[16,128,128]{2,1,0:T(8,128)}, u32[]{:S(2)}, u32[]{:S(2)}) collective-permute-start(f32[16,128,128]{2,1,0:T(8,128)} %collective-permute-done.2.refs_1_), channel_id=1, source_target_pairs={{0,2},{2,0},{1,3},{3,1},{4,6},{6,4},{5,7},{7,5},{8,10},{10,8},{9,1... | collective-permute-start | bytes 3145736 | tf_op jit(solution)/shard_map/ppermute | solution.py:186
  46.6 6.0 %collective-permute-start.7 = (f32[16,128,128]{2,1,0:T(8,128)}, f32[16,128,128]{2,1,0:T(8,128)}, u32[]{:S(2)}, u32[]{:S(2)}) collective-permute-start(f32[16,128,128]{2,1,0:T(8,128)} %collective-permute-done.3.refs_2_), channel_id=1, source_target_pairs={{0,2},{2,0},{1,3},{3,1},{4,6},{6,4},{5,7},{7,5},{8,10},{10,8},{9,1... | collective-permute-start | bytes 3145736 | tf_op jit(solution)/shard_map/ppermute | solution.py:186
  48.4 27.4 %collective-permute-start.13 = (f32[16,128,128]{2,1,0:T(8,128)S(1)}, f32[16,128,128]{2,1,0:T(8,128)S(1)}, u32[]{:S(2)}, u32[]{:S(2)}) collective-permute-start(f32[16,128,128]{2,1,0:T(8,128)S(1)} %collective-permute-done.8.refs_0_.refs_13_), channel_id=1, source_target_pairs={{0,32},{32,64},{64,96},{96,128},{128,160},{160,192},{192,224},{224... | collective-permute-start | bytes 3145736 | tf_op jit(solution)/shard_map/ppermute | solution.py:186
  52.1 25.0 %collective-permute-start.14 = (f32[16,128,128]{2,1,0:T(8,128)S(1)}, f32[16,128,128]{2,1,0:T(8,128)S(1)}, u32[]{:S(2)}, u32[]{:S(2)}) collective-permute-start(f32[16,128,128]{2,1,0:T(8,128)S(1)} %collective-permute-done.9.refs_1_.refs_14_), channel_id=1, source_target_pairs={{0,224},{32,0},{64,32},{96,64},{128,96},{160,128},{192,160},{224,1... | collective-permute-start | bytes 3145736 | tf_op jit(solution)/shard_map/ppermute | solution.py:186
  53.8 26.8 %collective-permute-start.10 = (f32[16,128,128]{2,1,0:T(8,128)}, f32[16,128,128]{2,1,0:T(8,128)S(1)}, u32[]{:S(2)}, u32[]{:S(2)}) collective-permute-start(f32[16,128,128]{2,1,0:T(8,128)} %get-tuple-element.31.refs_6_), channel_id=1, source_target_pairs={{0,8},{8,16},{16,24},{24,0},{1,9},{9,17},{17,25},{25,1},{2,10},{10... | collective-permute-start | bytes 3145736 | tf_op jit(solution)/shard_map/ppermute | solution.py:186
  54.0 26.7 %collective-permute-start.12 = (f32[16,128,128]{2,1,0:T(8,128)}, f32[16,128,128]{2,1,0:T(8,128)S(1)}, u32[]{:S(2)}, u32[]{:S(2)}) collective-permute-start(f32[16,128,128]{2,1,0:T(8,128)} %get-tuple-element.31.refs_6_), channel_id=1, source_target_pairs={{0,4},{4,0},{1,5},{5,1},{2,6},{6,2},{3,7},{7,3},{8,12},{12,8},{9,1... | collective-permute-start | bytes 3145736 | tf_op jit(solution)/shard_map/ppermute | solution.py:186
  55.1 25.6 %collective-permute-start.11 = (f32[16,128,128]{2,1,0:T(8,128)}, f32[16,128,128]{2,1,0:T(8,128)S(1)}, u32[]{:S(2)}, u32[]{:S(2)}) collective-permute-start(f32[16,128,128]{2,1,0:T(8,128)} %get-tuple-element.32.refs_8_), channel_id=1, source_target_pairs={{0,24},{8,0},{16,8},{24,16},{1,25},{9,1},{17,9},{25,17},{2,26},{10... | collective-permute-start | bytes 3145736 | tf_op jit(solution)/shard_map/ppermute | solution.py:186
  75.9 26.0 %collective-permute-start.18 = (f32[16,128,128]{2,1,0:T(8,128)S(1)}, f32[16,128,128]{2,1,0:T(8,128)S(1)}, u32[]{:S(2)}, u32[]{:S(2)}) collective-permute-start(f32[16,128,128]{2,1,0:T(8,128)S(1)} %collective-permute-done.13.refs_0_.refs_15_), channel_id=1, source_target_pairs={{0,32},{32,64},{64,96},{96,128},{128,160},{160,192},{192,224},{224... | collective-permute-start | bytes 3145736 | tf_op jit(solution)/shard_map/ppermute | solution.py:186
  77.6 25.7 %collective-permute-start.19 = (f32[16,128,128]{2,1,0:T(8,128)S(1)}, f32[16,128,128]{2,1,0:T(8,128)S(1)}, u32[]{:S(2)}, u32[]{:S(2)}) collective-permute-start(f32[16,128,128]{2,1,0:T(8,128)S(1)} %collective-permute-done.14.refs_1_.refs_16_), channel_id=1, source_target_pairs={{0,224},{32,0},{64,32},{96,64},{128,96},{160,128},{192,160},{224,1... | collective-permute-start | bytes 3145736 | tf_op jit(solution)/shard_map/ppermute | solution.py:186
  80.6 1.0 copy-start.2
  80.6 1.4 copy-start
  82.0 1.1 copy-start.3
  84.2 22.6 %collective-permute-start.22 = (f32[16,128,128]{2,1,0:T(8,128)}, f32[16,128,128]{2,1,0:T(8,128)S(1)}, u32[]{:S(2)}, u32[]{:S(2)}) collective-permute-start(f32[16,128,128]{2,1,0:T(8,128)} %get-tuple-element.34.refs_5_), channel_id=1, source_target_pairs={{0,2},{2,0},{1,3},{3,1},{4,6},{6,4},{5,7},{7,5},{8,10},{10,8},{9,1... | collective-permute-start | bytes 3145736 | tf_op jit(solution)/shard_map/ppermute | solution.py:186
  84.3 28.1 %collective-permute-start.15 = (f32[16,128,128]{2,1,0:T(8,128)}, f32[16,128,128]{2,1,0:T(8,128)S(1)}, u32[]{:S(2)}, u32[]{:S(2)}) collective-permute-start(f32[16,128,128]{2,1,0:T(8,128)} %get-tuple-element.33.refs_3_), channel_id=1, source_target_pairs={{0,2},{2,0},{1,3},{3,1},{4,6},{6,4},{5,7},{7,5},{8,10},{10,8},{9,1... | collective-permute-start | bytes 3145736 | tf_op jit(solution)/shard_map/ppermute | solution.py:186
  86.1 20.7 %collective-permute-start.16 = (f32[16,128,128]{2,1,0:T(8,128)S(1)}, f32[16,128,128]{2,1,0:T(8,128)S(1)}, u32[]{:S(2)}, u32[]{:S(2)}) collective-permute-start(f32[16,128,128]{2,1,0:T(8,128)S(1)} %broadcast_select_fusion.1), channel_id=1, source_target_pairs={{0,8},{2,26},{8,16},{10,2},{16,24},{18,10},{24,0},{26,18},{1,9},{3... | collective-permute-start | bytes 3145736 | tf_op jit(solution)/shard_map/ppermute | solution.py:192
  101.9 5.0 %collective-permute-start.21 = (f32[16,128,128]{2,1,0:T(8,128)}, f32[16,128,128]{2,1,0:T(8,128)S(1)}, u32[]{:S(2)}, u32[]{:S(2)}) collective-permute-start(f32[16,128,128]{2,1,0:T(8,128)} %get-tuple-element.43.refs_3_), channel_id=1, source_target_pairs={{0,2},{2,0},{1,3},{3,1},{4,6},{6,4},{5,7},{7,5},{8,10},{10,8},{9,1... | collective-permute-start | bytes 3145736 | tf_op jit(solution)/shard_map/ppermute | solution.py:186
  103.5 15.7 %collective-permute-start.20 = (f32[16,128,128]{2,1,0:T(8,128)S(1)}, f32[16,128,128]{2,1,0:T(8,128)S(1)}, u32[]{:S(2)}, u32[]{:S(2)}) collective-permute-start(f32[16,128,128]{2,1,0:T(8,128)S(1)} %broadcast_select_fusion), channel_id=1, source_target_pairs={{0,32},{2,226},{32,64},{34,2},{64,96},{66,34},{96,128},{98,66},{12... | collective-permute-start | bytes 3145736 | tf_op jit(solution)/shard_map/ppermute | solution.py:192
  106.8 12.3 %collective-permute-start.17 = (f32[16,128,128]{2,1,0:T(8,128)S(1)}, f32[16,128,128]{2,1,0:T(8,128)S(1)}, u32[]{:S(2)}, u32[]{:S(2)}) collective-permute-start(f32[16,128,128]{2,1,0:T(8,128)S(1)} %collective-permute-done.16.refs_5_), channel_id=1, source_target_pairs={{0,2},{2,0},{1,3},{3,1},{4,6},{6,4},{5,7},{7,5},{8,10},{10,8},{9,1... | collective-permute-start | bytes 3145736 | tf_op jit(solution)/shard_map/ppermute | solution.py:186
  106.8 1.0 copy-start.5
  106.8 1.3 copy-start.4
  108.2 11.0 %copy-start.1 = (f32[16,128,128]{2,1,0:T(8,128)S(1)}, f32[16,128,128]{2,1,0:T(8,128)}, u32[]{:S(2)}) copy-start(f32[16,128,128]{2,1,0:T(8,128)} %get-tuple-element.33.refs_3_) | copy-start | bytes 3145732
  121.5 25.8 %collective-permute-start.23 = (f32[8,128,128]{2,1,0:T(8,128)S(1)}, f32[8,128,128]{2,1,0:T(8,128)S(1)}, u32[]{:S(2)}, u32[]{:S(2)}) collective-permute-start(f32[8,128,128]{2,1,0:T(8,128)S(1)} %slice.29), channel_id=1, source_target_pairs={{0,1},{1,0},{2,3},{3,2},{4,5},{5,4},{6,7},{7,6},{8,9},{9,8},{10,11... | collective-permute-start | bytes 1572872 | tf_op jit(solution)/shard_map/ppermute | solution.py:186
  125.8 21.5 %collective-permute-start.24 = (f32[8,128,128]{2,1,0:T(8,128)S(1)}, f32[8,128,128]{2,1,0:T(8,128)S(1)}, u32[]{:S(2)}, u32[]{:S(2)}) collective-permute-start(f32[8,128,128]{2,1,0:T(8,128)S(1)} %slice.30), channel_id=1, source_target_pairs={{0,1},{1,0},{2,3},{3,2},{4,5},{5,4},{6,7},{7,6},{8,9},{9,8},{10,11... | collective-permute-start | bytes 1572872 | tf_op jit(solution)/shard_map/ppermute | solution.py:186

commit v4 on v3

--- a/solution.py
+++ b/solution.py
@@ -223,7 +223,7 @@
     left_index = stack_left.reshape(-1)
     across_y = (left_index // (4 * SA) - y) % 4
     across_x = (left_index // (2 * SA) - x) % 2
-    left_class = jnp.where(across_x == 0, jnp.where(across_y == 2, 1, 0), jnp.where(across_y < 2, across_y, 2))
+    left_class = jnp.where((across_y == 2) | ((across_y != 0) & (across_x == 1)), 1, 0)
     bounds, listed = order(
         left_index,
         stack_right.reshape(-1),
@@ -246,8 +246,9 @@
     first_places = [left_at(0, 0, 0), left_at(0, 0, 1), left_at(-1, 0, 0), left_at(1, 0, 0), left_at(0, 1, 0)]
     first_places += [left_at(-1, 0, 1), left_at(1, 0, 1), left_at(0, 1, 1)]
     first_places += [right_at(away) for away in (0, -1, 1, -2, 2)]
-    second_places = [left_at(dy, dx, dc) for dy, dx in ((2, 0), (1, 1)) for dc in range(2)] + [right_at(-3), right_at(3)]
-    third_places = [left_at(dy, 1, dc) for dy in (-1, 2) for dc in range(2)] + [right_at(4)]
+    second_places = [left_at(dy, dx, dc) for dy, dx in ((2, 0), (1, 1), (-1, 1), (2, 1)) for dc in range(2)]
+    second_places += [right_at(-3), right_at(3)]
+    third_places = [right_at(4)]
     starts = jnp.stack(first_places + second_places + third_places)
     second, third = len(first_places), len(first_places) + len(second_places)
 
@@ -277,11 +278,10 @@
 
     opposite = shift_apart(jnp.where(core == 0, up3, down3), "row")
     far_c, across_up_c = shift(far, "core", 1), shift(across_up, "core", 1)
-    lefts = [(1, a) for a in (own_far, own_far_c, across_down, across_down_c)]
-    state, done = stage((2, 3), second, lefts, [up3, down3], bounds, listed, starts, state, flops=10**9)
-
-    lefts = [(1, a) for a in (across_up, across_up_c, far, far_c)]
-    state, _ = stage((3, 4), third, lefts, [opposite], bounds, listed, starts, state, place=ANYWHERE)
+    lefts = [(1, a) for a in (own_far, own_far_c, across_down, across_down_c, across_up, across_up_c, far, far_c)]
+    state, done = stage((2, 3), second, lefts, [up3, down3], bounds, listed, starts, state, flops=1 * 10**7)
+
+    state, _ = stage((3, 4), third, [], [opposite], bounds, listed, starts, state, place=ANYWHERE)
     arrived_low = shift(state[2][SCH : SCH + SCH // 2], "layer", 1)
     state, _ = stage((4, 5), 0, [], [], bounds, listed, starts, state)
     arrived_high = shift(state[2][SCH + SCH // 2 : 2 * SCH], "layer", 1)

time: 150 us -> 150 us (level)
  starting transfers between devices: 30.1 us -> 32.2 us
  local copies, waits for them, and re-layouts: 5.42 us -> 3.61 us
  waiting for transfers between devices: 84.3 us -> 82.7 us
    ppermute x2, waiting for transfers between devices: 6.7 us -> 4.81 us  [shift_apart(): return lax.ppermute(value, (axis, 'core'), pairs)]
    unnamed x20 -> x22, local copies, waits for them, and re-layouts: 4.4 us -> 2.59 us
where the time goes in v4:
time: 150 us; the launch traced here: 148 us
  waiting for transfers between devices  82.7 us (55%)
  starting transfers between devices  32.2 us (21%)
  Pallas kernels  24.6 us (16%)
  local copies, waits for them, and re-layouts  3.61 us (2%)
  other arithmetic  3.55 us (2%)
    ppermute x23, waiting for transfers between devices, shift(): lax.ppermute(value, axis, [(i, (i + by) % size) for i in range(size)])  70.9 us
    ppermute x23, starting transfers between devices, shift(): lax.ppermute(value, axis, [(i, (i + by) % size) for i in range(size)])  21.8 us
    pallas_call x5, Pallas kernels, stage(): pl.pallas_call(lambda *refs: stage_kernel(bins, parts, len(rights), not a...  17.9 us
    all_to_all x1, waiting for transfers between devices, body(): lax.all_to_all(factor_blocks.reshape(SA, BS, BS), ('y', 'x', 'core'), spl...  6.98 us
    all_to_all x1, starting transfers between devices, body(): lax.all_to_all(factor_blocks.reshape(SA, BS, BS), ('y', 'x', 'core'), spl...  6.09 us
    ppermute x2, waiting for transfers between devices, shift_apart(): return lax.ppermute(value, (axis, 'core'), pairs)  4.81 us
    ppermute x2, starting transfers between devices, shift_apart(): return lax.ppermute(value, (axis, 'core'), pairs)  4.29 us
    pallas_call x3, Pallas kernels, tie(): pl.pallas_call(tie_kernel, out_shape=[shape(a.shape, a.dtype) for a in ar...  3.49 us
  transfers between devices with their start and end apart: 26, of which 12 were waited for; matrix products, arithmetic and copies ran while one was open for 2% of the time, Pallas kernels for 15%

profile of v4, /device:TPU:34, one launch (start us, length us, event | category | flops | bytes accessed | tf_op | source)
XLA Modules:
  0.0 147.6 jit_solution(13842672516301559454)
XLA Ops:
  0.0 6.1 %all-to-all-start = ((f32[16,128,128]{2,1,0:T(8,128)}), f32[16,128,128]{2,1,0:T(8,128)S(1)}, u32[]{:S(2)}, u32[]{:S(2)}) async-start(f32[16,128,128]{2,1,0:T(8,128)} %bitcast.39), calls=%async_computation | async-start | bytes 2097152 | tf_op jit(solution)/shard_map/all_to_all | solution.py:244
  6.1 0.8 slice_bitcast_fusion
  6.9 0.1 collective-permute-start.7
  7.1 1.1 collective-permute-done.7.refs_1_
  8.2 0.6 copy-done.7
  8.8 2.2 %pack.1 = f32[16,128,128]{2,1,0:T(8,128)} custom-call(f32[16,128,128]{2,1,0:T(8,128)} %bitcast.36, f32[1,128,128]{2,1,0:T(8,128)} %copy-done.7), custom_call_target="tpu_custom_call" | custom-call | tf_op jit(solution)/shard_map/pack/pallas_call | solution.py:168
  11.1 1.5 %collective-permute-start.8 = (f32[16,128,128]{2,1,0:T(8,128)}, f32[16,128,128]{2,1,0:T(8,128)}, u32[]{:S(2)}, u32[]{:S(2)}) collective-permute-start(f32[16,128,128]{2,1,0:T(8,128)} %pack.1), channel_id=1, source_target_pairs={{0,8},{8,16},{16,24},{24,0},{1,9},{9,17},{17,25},{25,1},{2,10},{10... | collective-permute-start | bytes 3145736 | tf_op jit(solution)/shard_map/ppermute | solution.py:186
  12.6 1.8 %collective-permute-start.9 = (f32[16,128,128]{2,1,0:T(8,128)}, f32[16,128,128]{2,1,0:T(8,128)}, u32[]{:S(2)}, u32[]{:S(2)}) collective-permute-start(f32[16,128,128]{2,1,0:T(8,128)} %pack.1), channel_id=1, source_target_pairs={{0,24},{8,0},{16,8},{24,16},{1,25},{9,1},{17,9},{25,17},{2,26},{10... | collective-permute-start | bytes 3145736 | tf_op jit(solution)/shard_map/ppermute | solution.py:186
  14.4 0.2 collective-permute-start.10
  14.5 7.0 %all-to-all-done.refs_12_ = f32[16,128,128]{2,1,0:T(8,128)S(1)} async-done(((f32[16,128,128]{2,1,0:T(8,128)}), f32[16,128,128]{2,1,0:T(8,128)S(1)}, u32[]{:S(2)}, u32[]{:S(2)}) %all-to-all-start) | async-done | bytes 1048608 | tf_op jit(solution)/shard_map/all_to_all | solution.py:244
  21.5 1.9 %collective-permute-start = (f32[16,128,128]{2,1,0:T(8,128)S(1)}, f32[16,128,128]{2,1,0:T(8,128)S(1)}, u32[]{:S(2)}, u32[]{:S(2)}) collective-permute-start(f32[16,128,128]{2,1,0:T(8,128)S(1)} %all-to-all-done.refs_12_), channel_id=1, source_target_pairs={{0,32},{32,64},{64,96},{96,128},{128,160},{160,192},{192,224},{224... | collective-permute-start | bytes 3145736 | tf_op jit(solution)/shard_map/ppermute | solution.py:186
  23.4 0.1 collective-permute-start.3
  23.5 20.2 %collective-permute-done.8.refs_0_ = f32[16,128,128]{2,1,0:T(8,128)} collective-permute-done((f32[16,128,128]{2,1,0:T(8,128)}, f32[16,128,128]{2,1,0:T(8,128)}, u32[]{:S(2)}, u32[]{:S(2)}) %collective-permute-start.8) | collective-permute-done | bytes 1048608 | tf_op jit(solution)/shard_map/ppermute | solution.py:186
  43.8 0.1 collective-permute-start.11
  43.9 0.0 collective-permute-done.9.refs_1_
  43.9 0.4 collective-permute-start.12
  44.3 0.0 collective-permute-done.10.refs_2_
  44.3 0.1 collective-permute-start.13
  44.4 2.2 %collective-permute-done.refs_0_.refs_13_ = f32[16,128,128]{2,1,0:T(8,128)S(1)} collective-permute-done((f32[16,128,128]{2,1,0:T(8,128)S(1)}, f32[16,128,128]{2,1,0:T(8,128)S(1)}, u32[]{:S(2)}, u32[]{:S(2)}) %collective-permute-start) | collective-permute-done | bytes 1048608 | tf_op jit(solution)/shard_map/ppermute | solution.py:186
  47.4 0.1 convert_reduce_fusion.1
  47.5 1.0 collective-permute-done.3.refs_1_.refs_14_
  48.4 3.1 %collective-permute-start.1 = (f32[16,128,128]{2,1,0:T(8,128)S(1)}, f32[16,128,128]{2,1,0:T(8,128)}, u32[]{:S(2)}, u32[]{:S(2)}) collective-permute-start(f32[16,128,128]{2,1,0:T(8,128)S(1)} %collective-permute-done.refs_0_.refs_13_), channel_id=1, source_target_pairs={{0,32},{32,64},{64,96},{96,128},{128,160},{160,192},{192,224},{224... | collective-permute-start | bytes 3145736 | tf_op jit(solution)/shard_map/ppermute | solution.py:186
  51.6 0.5 witness.2.refs_7_
  52.1 0.3 collective-permute-start.4
  52.4 1.2 tie.3
  53.6 0.2 collective-permute-start.15
  53.9 1.0 collective-permute-start.17
  54.8 3.0 %collective-permute-start.16 = (f32[16,128,128]{2,1,0:T(8,128)}, f32[16,128,128]{2,1,0:T(8,128)}, u32[]{:S(2)}, u32[]{:S(2)}) collective-permute-start(f32[16,128,128]{2,1,0:T(8,128)} %get-tuple-element.32.refs_8_), channel_id=1, source_target_pairs={{0,24},{8,0},{16,8},{24,16},{1,25},{9,1},{17,9},{25,17},{2,26},{10... | collective-permute-start | bytes 3145736 | tf_op jit(solution)/shard_map/ppermute | solution.py:186
  57.8 0.1 stack.99.refs_1_.refs_0_
  57.9 0.1 select_reduce_fusion.2.refs_2_.refs_1_
  58.0 0.1 select_reduce_fusion.1
  58.1 0.3 convert_reduce_fusion
  58.4 17.3 %collective-permute-done.1.refs_0_.refs_15_ = f32[16,128,128]{2,1,0:T(8,128)} collective-permute-done((f32[16,128,128]{2,1,0:T(8,128)S(1)}, f32[16,128,128]{2,1,0:T(8,128)}, u32[]{:S(2)}, u32[]{:S(2)}) %collective-permute-start.1) | collective-permute-done | bytes 1048608 | tf_op jit(solution)/shard_map/ppermute | solution.py:186
  75.7 0.3 collective-permute-start.2
  76.0 1.1 collective-permute-done.4.refs_1_.refs_16_
  77.1 0.5 witness.3.refs_3_
  77.6 1.8 %collective-permute-start.5 = (f32[16,128,128]{2,1,0:T(8,128)S(1)}, f32[16,128,128]{2,1,0:T(8,128)S(1)}, u32[]{:S(2)}, u32[]{:S(2)}) collective-permute-start(f32[16,128,128]{2,1,0:T(8,128)S(1)} %collective-permute-done.4.refs_1_.refs_16_), channel_id=1, source_target_pairs={{0,224},{32,0},{64,32},{96,64},{128,96},{160,128},{192,160},{224,1... | collective-permute-start | bytes 3145736 | tf_op jit(solution)/shard_map/ppermute | solution.py:186
  79.5 1.0 collective-permute-done.15.refs_0_
  80.5 1.2 tie.4
  81.7 1.4 broadcast_select_fusion
  83.1 0.7 collective-permute-start.21
  83.8 0.2 select_reduce_fusion
  84.0 1.5 %collective-permute-start.19 = (f32[16,128,128]{2,1,0:T(8,128)}, f32[16,128,128]{2,1,0:T(8,128)S(1)}, u32[]{:S(2)}, u32[]{:S(2)}) collective-permute-start(f32[16,128,128]{2,1,0:T(8,128)} %get-tuple-element.42.refs_5_), channel_id=1, source_target_pairs={{0,2},{2,0},{1,3},{3,1},{4,6},{6,4},{5,7},{7,5},{8,10},{10,8},{9,1... | collective-permute-start | bytes 3145736 | tf_op jit(solution)/shard_map/ppermute | solution.py:186
  85.5 0.1 collective-permute-start.20
  85.7 6.8 %stage_0_2.1 = (f32[256,128,128]{2,1,0:T(8,128)S(1)}, bf16[128,128,256]{2,1,0:T(8,128)(2,1)S(1)}, f32[33,128,128]{2,1,0:T(8,128)S(1)}, s32[1]{0:T(128)}) custom-call(s32[1]{0:T(128)} %get-tuple-element.34.refs_0_, s32[24]{0:T(128)S(1)} %stack.99.refs_1_.refs_0_, s32[7]{0:T(128)S(1)} %select_reduce_fusion.2.refs_2_.refs_1_, ...), custom_call_target="tpu_custom_call" | custom-call | flops 8000000000 | tf_op jit(solution)/shard_map/stage_0_2/pallas_call | solution.py:103
  92.4 1.2 tie.5
  93.6 8.3 %collective-permute-done.2.refs_11_ = f32[16,128,128]{2,1,0:T(8,128)S(1)} collective-permute-done((f32[16,128,128]{2,1,0:T(8,128)}, f32[16,128,128]{2,1,0:T(8,128)S(1)}, u32[]{:S(2)}, u32[]{:S(2)}) %collective-permute-start.2) | collective-permute-done | bytes 1048608 | tf_op jit(solution)/shard_map/ppermute | solution.py:186
  101.9 0.5 collective-permute-start.22
  102.4 0.5 collective-permute-done.5.refs_12_
  102.9 0.1 broadcast_select_fusion.1
  103.1 3.6 %collective-permute-start.6 = (f32[16,128,128]{2,1,0:T(8,128)S(1)}, f32[16,128,128]{2,1,0:T(8,128)S(1)}, u32[]{:S(2)}, u32[]{:S(2)}) collective-permute-start(f32[16,128,128]{2,1,0:T(8,128)S(1)} %broadcast_select_fusion.1), channel_id=1, source_target_pairs={{0,32},{2,226},{32,64},{34,2},{64,96},{66,34},{96,128},{98,66},{12... | collective-permute-start | bytes 3145736 | tf_op jit(solution)/shard_map/ppermute | solution.py:192
  106.8 0.9 copy-done.5
  107.7 0.4 copy-done.3
  108.0 0.3 copy-done.4
  108.4 0.3 copy-done.6
  108.7 5.5 %stage_2_3.1 = (f32[256,128,128]{2,1,0:T(8,128)S(1)}, bf16[128,128,256]{2,1,0:T(8,128)(2,1)S(1)}, f32[33,128,128]{2,1,0:T(8,128)S(1)}, s32[1]{0:T(128)}) custom-call(s32[24]{0:T(128)S(1)} %stack.99.refs_1_.refs_0_, s32[7]{0:T(128)S(1)} %select_reduce_fusion.2.refs_2_.refs_1_, ...), custom_call_target="tpu_custom_call", output_to_operand_aliasing={{0}: (13, {}), {1}: (14, {}), {2}: (15, {})} | custom-call | flops 10000000 | tf_op jit(solution)/shard_map/stage_2_3/pallas_call | solution.py:103
  114.2 4.8 %collective-permute-done.6.refs_3_ = f32[16,128,128]{2,1,0:T(8,128)S(1)} collective-permute-done((f32[16,128,128]{2,1,0:T(8,128)S(1)}, f32[16,128,128]{2,1,0:T(8,128)S(1)}, u32[]{:S(2)}, u32[]{:S(2)}) %collective-permute-start.6) | collective-permute-done | bytes 1048608 | tf_op jit(solution)/shard_map/ppermute | solution.py:192
  119.0 2.0 %stage_3_4.1 = (f32[256,128,128]{2,1,0:T(8,128)S(1)}, bf16[128,128,256]{2,1,0:T(8,128)(2,1)S(1)}, f32[33,128,128]{2,1,0:T(8,128)S(1)}, s32[1]{0:T(128)}) custom-call(s32[24]{0:T(128)S(1)} %stack.99.refs_1_.refs_0_, s32[7]{0:T(128)S(1)} %select_reduce_fusion.2.refs_2_.refs_1_, ...), custom_call_target="tpu_custom_call", output_to_operand_aliasing={{0}: (4, {}), {1}: (5, {}), {2}: (6, {})} | custom-call | tf_op jit(solution)/shard_map/stage_3_4/pallas_call | solution.py:103
  121.0 2.2 %collective-permute-start.23 = (f32[8,128,128]{2,1,0:T(8,128)S(1)}, f32[8,128,128]{2,1,0:T(8,128)S(1)}, u32[]{:S(2)}, u32[]{:S(2)}) collective-permute-start(f32[8,128,128]{2,1,0:T(8,128)S(1)} %slice.29), channel_id=1, source_target_pairs={{0,1},{1,0},{2,3},{3,2},{4,5},{5,4},{6,7},{7,6},{8,9},{9,8},{10,11... | collective-permute-start | bytes 1572872 | tf_op jit(solution)/shard_map/ppermute | solution.py:186
  123.3 1.6 %stage_4_5.1 = (f32[256,128,128]{2,1,0:T(8,128)S(1)}, bf16[128,128,256]{2,1,0:T(8,128)(2,1)S(1)}, f32[33,128,128]{2,1,0:T(8,128)S(1)}, s32[1]{0:T(128)}) custom-call(s32[24]{0:T(128)S(1)} %stack.99.refs_1_.refs_0_, s32[7]{0:T(128)S(1)} %select_reduce_fusion.2.refs_2_.refs_1_, ...), custom_call_target="tpu_custom_call", output_to_operand_aliasing={{0}: (3, {}), {1}: (4, {}), {2}: (5, {})} | custom-call | tf_op jit(solution)/shard_map/stage_4_5/pallas_call | solution.py:103
  124.9 1.5 %collective-permute-start.24 = (f32[8,128,128]{2,1,0:T(8,128)S(1)}, f32[8,128,128]{2,1,0:T(8,128)S(1)}, u32[]{:S(2)}, u32[]{:S(2)}) collective-permute-start(f32[8,128,128]{2,1,0:T(8,128)S(1)} %slice.30), channel_id=1, source_target_pairs={{0,1},{1,0},{2,3},{3,2},{4,5},{5,4},{6,7},{7,6},{8,9},{9,8},{10,11... | collective-permute-start | bytes 1572872 | tf_op jit(solution)/shard_map/ppermute | solution.py:186
  126.4 2.1 %stage_5_6.1 = (f32[256,128,128]{2,1,0:T(8,128)S(1)}, bf16[128,128,256]{2,1,0:T(8,128)(2,1)S(1)}, f32[33,128,128]{2,1,0:T(8,128)S(1)}, s32[1]{0:T(128)}) custom-call(s32[24]{0:T(128)S(1)} %stack.99.refs_1_.refs_0_, s32[7]{0:T(128)S(1)} %select_reduce_fusion.2.refs_2_.refs_1_, ...), custom_call_target="tpu_custom_call", output_to_operand_aliasing={{0}: (3, {}), {1}: (4, {}), {2}: (5, {})} | custom-call | flops 10000000000 | tf_op jit(solution)/shard_map/stage_5_6/pallas_call | solution.py:103
  128.4 18.1 %collective-permute-done.24 = f32[8,128,128]{2,1,0:T(8,128)S(1)} collective-permute-done((f32[8,128,128]{2,1,0:T(8,128)S(1)}, f32[8,128,128]{2,1,0:T(8,128)S(1)}, u32[]{:S(2)}, u32[]{:S(2)}) %collective-permute-start.24) | collective-permute-done | bytes 524320 | tf_op jit(solution)/shard_map/ppermute | solution.py:186
  146.5 1.1 fusion
  (39 shorter events, 0.2 us)
Async XLA Ops:
  0.0 47.3 %copy-start.8 = (s32[1,1,1,512]{3,2,1,0:T(1,128)S(1)}, s32[1,1,1,512]{3,2,1,0:T(1,128)}, u32[]{:S(2)}) copy-start(s32[1,1,1,512]{3,2,1,0:T(1,128)} %param.9) | copy-start | bytes 6148
  0.0 47.3 %copy-start.9 = (s32[1,1,1,512]{3,2,1,0:T(1,128)S(1)}, s32[1,1,1,512]{3,2,1,0:T(1,128)}, u32[]{:S(2)}) copy-start(s32[1,1,1,512]{3,2,1,0:T(1,128)} %param.8) | copy-start | bytes 6148
  0.0 47.3 %copy-start.10 = (s32[1,1,1,512]{3,2,1,0:T(1,128)S(1)}, s32[1,1,1,512]{3,2,1,0:T(1,128)}, u32[]{:S(2)}) copy-start(s32[1,1,1,512]{3,2,1,0:T(1,128)} %param.10) | copy-start | bytes 6148
  0.0 21.5 %all-to-all-start = ((f32[16,128,128]{2,1,0:T(8,128)}), f32[16,128,128]{2,1,0:T(8,128)S(1)}, u32[]{:S(2)}, u32[]{:S(2)}) async-start(f32[16,128,128]{2,1,0:T(8,128)} %bitcast.39), calls=%async_computation | async-start | bytes 2097152 | tf_op jit(solution)/shard_map/all_to_all | solution.py:244
  6.9 1.3 collective-permute-start.7
  8.2 0.6 copy-start.7
  11.1 32.7 %collective-permute-start.8 = (f32[16,128,128]{2,1,0:T(8,128)}, f32[16,128,128]{2,1,0:T(8,128)}, u32[]{:S(2)}, u32[]{:S(2)}) collective-permute-start(f32[16,128,128]{2,1,0:T(8,128)} %pack.1), channel_id=1, source_target_pairs={{0,8},{8,16},{16,24},{24,0},{1,9},{9,17},{17,25},{25,1},{2,10},{10... | collective-permute-start | bytes 3145736 | tf_op jit(solution)/shard_map/ppermute | solution.py:186
  12.6 31.3 %collective-permute-start.9 = (f32[16,128,128]{2,1,0:T(8,128)}, f32[16,128,128]{2,1,0:T(8,128)}, u32[]{:S(2)}, u32[]{:S(2)}) collective-permute-start(f32[16,128,128]{2,1,0:T(8,128)} %pack.1), channel_id=1, source_target_pairs={{0,24},{8,0},{16,8},{24,16},{1,25},{9,1},{17,9},{25,17},{2,26},{10... | collective-permute-start | bytes 3145736 | tf_op jit(solution)/shard_map/ppermute | solution.py:186
  14.4 29.9 %collective-permute-start.10 = (f32[16,128,128]{2,1,0:T(8,128)}, f32[16,128,128]{2,1,0:T(8,128)}, u32[]{:S(2)}, u32[]{:S(2)}) collective-permute-start(f32[16,128,128]{2,1,0:T(8,128)} %pack.1), channel_id=1, source_target_pairs={{0,4},{4,0},{1,5},{5,1},{2,6},{6,2},{3,7},{7,3},{8,12},{12,8},{9,1... | collective-permute-start | bytes 3145736 | tf_op jit(solution)/shard_map/ppermute | solution.py:186
  21.5 30.6 %copy-start = (f32[16,128,128]{2,1,0:T(8,128)}, f32[16,128,128]{2,1,0:T(8,128)S(1)}, u32[]{:S(2)}) copy-start(f32[16,128,128]{2,1,0:T(8,128)S(1)} %all-to-all-done.refs_12_) | copy-start | bytes 3145732
  21.5 25.1 %collective-permute-start = (f32[16,128,128]{2,1,0:T(8,128)S(1)}, f32[16,128,128]{2,1,0:T(8,128)S(1)}, u32[]{:S(2)}, u32[]{:S(2)}) collective-permute-start(f32[16,128,128]{2,1,0:T(8,128)S(1)} %all-to-all-done.refs_12_), channel_id=1, source_target_pairs={{0,32},{32,64},{64,96},{96,128},{128,160},{160,192},{192,224},{224... | collective-permute-start | bytes 3145736 | tf_op jit(solution)/shard_map/ppermute | solution.py:186
  23.4 25.0 %collective-permute-start.3 = (f32[16,128,128]{2,1,0:T(8,128)S(1)}, f32[16,128,128]{2,1,0:T(8,128)S(1)}, u32[]{:S(2)}, u32[]{:S(2)}) collective-permute-start(f32[16,128,128]{2,1,0:T(8,128)S(1)} %all-to-all-done.refs_12_), channel_id=1, source_target_pairs={{0,224},{32,0},{64,32},{96,64},{128,96},{160,128},{192,160},{224,1... | collective-permute-start | bytes 3145736 | tf_op jit(solution)/shard_map/ppermute | solution.py:186
  43.8 8.3 %collective-permute-start.11 = (f32[16,128,128]{2,1,0:T(8,128)}, f32[16,128,128]{2,1,0:T(8,128)}, u32[]{:S(2)}, u32[]{:S(2)}) collective-permute-start(f32[16,128,128]{2,1,0:T(8,128)} %bitcast.37), channel_id=1, source_target_pairs={{0,2},{2,0},{1,3},{3,1},{4,6},{6,4},{5,7},{7,5},{8,10},{10,8},{9,1... | collective-permute-start | bytes 3145736 | tf_op jit(solution)/shard_map/ppermute | solution.py:186
  43.9 8.6 %collective-permute-start.12 = (f32[16,128,128]{2,1,0:T(8,128)}, f32[16,128,128]{2,1,0:T(8,128)}, u32[]{:S(2)}, u32[]{:S(2)}) collective-permute-start(f32[16,128,128]{2,1,0:T(8,128)} %collective-permute-done.8.refs_0_), channel_id=1, source_target_pairs={{0,2},{2,0},{1,3},{3,1},{4,6},{6,4},{5,7},{7,5},{8,10},{10,8},{9,1... | collective-permute-start | bytes 3145736 | tf_op jit(solution)/shard_map/ppermute | solution.py:186
  44.3 8.1 %collective-permute-start.13 = (f32[16,128,128]{2,1,0:T(8,128)}, f32[16,128,128]{2,1,0:T(8,128)}, u32[]{:S(2)}, u32[]{:S(2)}) collective-permute-start(f32[16,128,128]{2,1,0:T(8,128)} %collective-permute-done.9.refs_1_), channel_id=1, source_target_pairs={{0,2},{2,0},{1,3},{3,1},{4,6},{6,4},{5,7},{7,5},{8,10},{10,8},{9,1... | collective-permute-start | bytes 3145736 | tf_op jit(solution)/shard_map/ppermute | solution.py:186
  46.6 5.8 %collective-permute-start.14 = (f32[16,128,128]{2,1,0:T(8,128)}, f32[16,128,128]{2,1,0:T(8,128)}, u32[]{:S(2)}, u32[]{:S(2)}) collective-permute-start(f32[16,128,128]{2,1,0:T(8,128)} %collective-permute-done.10.refs_2_), channel_id=1, source_target_pairs={{0,2},{2,0},{1,3},{3,1},{4,6},{6,4},{5,7},{7,5},{8,10},{10,8},{9,1... | collective-permute-start | bytes 3145736 | tf_op jit(solution)/shard_map/ppermute | solution.py:186
  48.4 27.3 %collective-permute-start.1 = (f32[16,128,128]{2,1,0:T(8,128)S(1)}, f32[16,128,128]{2,1,0:T(8,128)}, u32[]{:S(2)}, u32[]{:S(2)}) collective-permute-start(f32[16,128,128]{2,1,0:T(8,128)S(1)} %collective-permute-done.refs_0_.refs_13_), channel_id=1, source_target_pairs={{0,32},{32,64},{64,96},{96,128},{128,160},{160,192},{192,224},{224... | collective-permute-start | bytes 3145736 | tf_op jit(solution)/shard_map/ppermute | solution.py:186
  52.1 25.0 %collective-permute-start.4 = (f32[16,128,128]{2,1,0:T(8,128)S(1)}, f32[16,128,128]{2,1,0:T(8,128)S(1)}, u32[]{:S(2)}, u32[]{:S(2)}) collective-permute-start(f32[16,128,128]{2,1,0:T(8,128)S(1)} %collective-permute-done.3.refs_1_.refs_14_), channel_id=1, source_target_pairs={{0,224},{32,0},{64,32},{96,64},{128,96},{160,128},{192,160},{224,1... | collective-permute-start | bytes 3145736 | tf_op jit(solution)/shard_map/ppermute | solution.py:186
  53.6 26.9 %collective-permute-start.15 = (f32[16,128,128]{2,1,0:T(8,128)}, f32[16,128,128]{2,1,0:T(8,128)}, u32[]{:S(2)}, u32[]{:S(2)}) collective-permute-start(f32[16,128,128]{2,1,0:T(8,128)} %get-tuple-element.31.refs_6_), channel_id=1, source_target_pairs={{0,8},{8,16},{16,24},{24,0},{1,9},{9,17},{17,25},{25,1},{2,10},{10... | collective-permute-start | bytes 3145736 | tf_op jit(solution)/shard_map/ppermute | solution.py:186
  53.9 26.7 %collective-permute-start.17 = (f32[16,128,128]{2,1,0:T(8,128)}, f32[16,128,128]{2,1,0:T(8,128)}, u32[]{:S(2)}, u32[]{:S(2)}) collective-permute-start(f32[16,128,128]{2,1,0:T(8,128)} %get-tuple-element.31.refs_6_), channel_id=1, source_target_pairs={{0,4},{4,0},{1,5},{5,1},{2,6},{6,2},{3,7},{7,3},{8,12},{12,8},{9,1... | collective-permute-start | bytes 3145736 | tf_op jit(solution)/shard_map/ppermute | solution.py:186
  54.8 25.7 %collective-permute-start.16 = (f32[16,128,128]{2,1,0:T(8,128)}, f32[16,128,128]{2,1,0:T(8,128)}, u32[]{:S(2)}, u32[]{:S(2)}) collective-permute-start(f32[16,128,128]{2,1,0:T(8,128)} %get-tuple-element.32.refs_8_), channel_id=1, source_target_pairs={{0,24},{8,0},{16,8},{24,16},{1,25},{9,1},{17,9},{25,17},{2,26},{10... | collective-permute-start | bytes 3145736 | tf_op jit(solution)/shard_map/ppermute | solution.py:186
  75.7 26.2 %collective-permute-start.2 = (f32[16,128,128]{2,1,0:T(8,128)}, f32[16,128,128]{2,1,0:T(8,128)S(1)}, u32[]{:S(2)}, u32[]{:S(2)}) collective-permute-start(f32[16,128,128]{2,1,0:T(8,128)} %collective-permute-done.1.refs_0_.refs_15_), channel_id=1, source_target_pairs={{0,32},{32,64},{64,96},{96,128},{128,160},{160,192},{192,224},{224... | collective-permute-start | bytes 3145736 | tf_op jit(solution)/shard_map/ppermute | solution.py:186
  77.6 25.3 %collective-permute-start.5 = (f32[16,128,128]{2,1,0:T(8,128)S(1)}, f32[16,128,128]{2,1,0:T(8,128)S(1)}, u32[]{:S(2)}, u32[]{:S(2)}) collective-permute-start(f32[16,128,128]{2,1,0:T(8,128)S(1)} %collective-permute-done.4.refs_1_.refs_16_), channel_id=1, source_target_pairs={{0,224},{32,0},{64,32},{96,64},{128,96},{160,128},{192,160},{224,1... | collective-permute-start | bytes 3145736 | tf_op jit(solution)/shard_map/ppermute | solution.py:186
  81.7 4.0 %copy-start.1 = (f32[16,128,128]{2,1,0:T(8,128)S(1)}, f32[16,128,128]{2,1,0:T(8,128)}, u32[]{:S(2)}) copy-start(f32[16,128,128]{2,1,0:T(8,128)} %copy-done) | copy-start | bytes 3145732
  83.1 18.8 %collective-permute-start.21 = (f32[16,128,128]{2,1,0:T(8,128)S(1)}, f32[16,128,128]{2,1,0:T(8,128)S(1)}, u32[]{:S(2)}, u32[]{:S(2)}) collective-permute-start(f32[16,128,128]{2,1,0:T(8,128)S(1)} %broadcast_select_fusion), channel_id=1, source_target_pairs={{0,8},{2,26},{8,16},{10,2},{16,24},{18,10},{24,0},{26,18},{1,9},{3... | collective-permute-start | bytes 3145736 | tf_op jit(solution)/shard_map/ppermute | solution.py:192
  84.0 22.7 %collective-permute-start.19 = (f32[16,128,128]{2,1,0:T(8,128)}, f32[16,128,128]{2,1,0:T(8,128)S(1)}, u32[]{:S(2)}, u32[]{:S(2)}) collective-permute-start(f32[16,128,128]{2,1,0:T(8,128)} %get-tuple-element.42.refs_5_), channel_id=1, source_target_pairs={{0,2},{2,0},{1,3},{3,1},{4,6},{6,4},{5,7},{7,5},{8,10},{10,8},{9,1... | collective-permute-start | bytes 3145736 | tf_op jit(solution)/shard_map/ppermute | solution.py:186
  85.5 21.2 %collective-permute-start.20 = (f32[16,128,128]{2,1,0:T(8,128)}, f32[16,128,128]{2,1,0:T(8,128)S(1)}, u32[]{:S(2)}, u32[]{:S(2)}) collective-permute-start(f32[16,128,128]{2,1,0:T(8,128)} %get-tuple-element.43.refs_7_), channel_id=1, source_target_pairs={{0,2},{2,0},{1,3},{3,1},{4,6},{6,4},{5,7},{7,5},{8,10},{10,8},{9,1... | collective-permute-start | bytes 3145736 | tf_op jit(solution)/shard_map/ppermute | solution.py:186
  101.9 4.8 %collective-permute-start.18 = (f32[16,128,128]{2,1,0:T(8,128)}, f32[16,128,128]{2,1,0:T(8,128)S(1)}, u32[]{:S(2)}, u32[]{:S(2)}) collective-permute-start(f32[16,128,128]{2,1,0:T(8,128)} %get-tuple-element.41.refs_3_), channel_id=1, source_target_pairs={{0,2},{2,0},{1,3},{3,1},{4,6},{6,4},{5,7},{7,5},{8,10},{10,8},{9,1... | collective-permute-start | bytes 3145736 | tf_op jit(solution)/shard_map/ppermute | solution.py:186
  101.9 4.8 %copy-start.2 = (f32[16,128,128]{2,1,0:T(8,128)}, f32[16,128,128]{2,1,0:T(8,128)S(1)}, u32[]{:S(2)}) copy-start(f32[16,128,128]{2,1,0:T(8,128)S(1)} %collective-permute-done.21.refs_9_) | copy-start | bytes 3145732
  101.9 4.8 %collective-permute-start.22 = (f32[16,128,128]{2,1,0:T(8,128)S(1)}, f32[16,128,128]{2,1,0:T(8,128)S(1)}, u32[]{:S(2)}, u32[]{:S(2)}) collective-permute-start(f32[16,128,128]{2,1,0:T(8,128)S(1)} %collective-permute-done.21.refs_9_), channel_id=1, source_target_pairs={{0,2},{2,0},{1,3},{3,1},{4,6},{6,4},{5,7},{7,5},{8,10},{10,8},{9,1... | collective-permute-start | bytes 3145736 | tf_op jit(solution)/shard_map/ppermute | solution.py:186
  103.1 16.0 %collective-permute-start.6 = (f32[16,128,128]{2,1,0:T(8,128)S(1)}, f32[16,128,128]{2,1,0:T(8,128)S(1)}, u32[]{:S(2)}, u32[]{:S(2)}) collective-permute-start(f32[16,128,128]{2,1,0:T(8,128)S(1)} %broadcast_select_fusion.1), channel_id=1, source_target_pairs={{0,32},{2,226},{32,64},{34,2},{64,96},{66,34},{96,128},{98,66},{12... | collective-permute-start | bytes 3145736 | tf_op jit(solution)/shard_map/ppermute | solution.py:192
  106.7 1.0 copy-start.5
  106.7 1.3 copy-start.3
  106.7 1.6 %copy-start.4 = (f32[16,128,128]{2,1,0:T(8,128)}, f32[16,128,128]{2,1,0:T(8,128)S(1)}, u32[]{:S(2)}) copy-start(f32[16,128,128]{2,1,0:T(8,128)S(1)} %collective-permute-done.20.refs_8_) | copy-start | bytes 3145732
  106.8 1.9 %copy-start.6 = (f32[16,128,128]{2,1,0:T(8,128)}, f32[16,128,128]{2,1,0:T(8,128)S(1)}, u32[]{:S(2)}) copy-start(f32[16,128,128]{2,1,0:T(8,128)S(1)} %collective-permute-done.22.refs_10_) | copy-start | bytes 3145732
  121.0 25.5 %collective-permute-start.23 = (f32[8,128,128]{2,1,0:T(8,128)S(1)}, f32[8,128,128]{2,1,0:T(8,128)S(1)}, u32[]{:S(2)}, u32[]{:S(2)}) collective-permute-start(f32[8,128,128]{2,1,0:T(8,128)S(1)} %slice.29), channel_id=1, source_target_pairs={{0,1},{1,0},{2,3},{3,2},{4,5},{5,4},{6,7},{7,6},{8,9},{9,8},{10,11... | collective-permute-start | bytes 1572872 | tf_op jit(solution)/shard_map/ppermute | solution.py:186
  124.9 21.6 %collective-permute-start.24 = (f32[8,128,128]{2,1,0:T(8,128)S(1)}, f32[8,128,128]{2,1,0:T(8,128)S(1)}, u32[]{:S(2)}, u32[]{:S(2)}) collective-permute-start(f32[8,128,128]{2,1,0:T(8,128)S(1)} %slice.30), channel_id=1, source_target_pairs={{0,1},{1,0},{2,3},{3,2},{4,5},{5,4},{6,7},{7,6},{8,9},{9,8},{10,11... | collective-permute-start | bytes 1572872 | tf_op jit(solution)/shard_map/ppermute | solution.py:186

commit v5 on v4

--- a/solution.py
+++ b/solution.py
@@ -120,7 +120,7 @@
     token[0] = 0
 
 
-def tie(arrays, tokens=(), place=ANYWHERE):
+def tie(arrays, tokens=(), place=ANYWHERE, flops=0):
     shape = jax.ShapeDtypeStruct if place is ANYWHERE else pltpu.HBM
     *arrays, token = pl.pallas_call(
         tie_kernel,
@@ -130,7 +130,7 @@
         input_output_aliases={i: i for i in range(len(arrays))},
         scratch_shapes=[pltpu.VMEM((8, BS), jnp.float32)],
         compiler_params=pltpu.CompilerParams(vmem_limit_bytes=1 << 20),
-        cost_estimate=pl.CostEstimate(flops=0, bytes_accessed=0, transcendentals=0),
+        cost_estimate=pl.CostEstimate(flops=flops, bytes_accessed=0, transcendentals=0),
         name="tie",
     )(*(arrays if place is ANYWHERE else hbm(*arrays)), *tokens)
     return arrays, token
@@ -252,14 +252,15 @@
     starts = jnp.stack(first_places + second_places + third_places)
     second, third = len(first_places), len(first_places) + len(second_places)
 
+    own_c = shift(own, "core", 1)
+    (mine,), _ = tie((mine,), (witness((own_c,)),), flops=10000000000)
     up1, down1 = shift(mine, "row", 1), shift(mine, "row", -1)
-    own_c = shift(own, "core", 1)
     sent = pack(own, later_than=(shift(own[:1], "core", 1),))
     own_up, own_down, across = shift(sent, "y", 1), shift(sent, "y", -1), shift(sent, "x", 1)
     own_up_c, own_down_c, across_c = shift(own_up, "core", 1), shift(own_down, "core", 1), shift(across, "core", 1)
     z1 = witness((up1, down1))
-    (own_up, own_down, across, own_c, own_up_c, own_down_c, across_c), _ = tie(
-        (own_up, own_down, across, own_c, own_up_c, own_down_c, across_c), (z1,), IN_HBM
+    (own_up, own_down, across, own_up_c, own_down_c, across_c), _ = tie(
+        (own_up, own_down, across, own_up_c, own_down_c, across_c), (z1,), IN_HBM
     )
 
     up2, down2 = shift(up1, "row", 1), shift(down1, "row", -1)

time: 150 us -> 148 us (0.987)
  waiting for transfers between devices: 82.7 us -> 70.4 us
  Pallas kernels: 24.6 us -> 34.2 us
    ppermute x23, waiting for transfers between devices: 70.9 us -> 61.4 us  [shift(): lax.ppermute(value, axis, [(i, (i + by) % size) for i in range(size)])]
    pallas_call x5, Pallas kernels: 17.9 us -> 25.8 us  [stage(): pl.pallas_call(lambda *refs: stage_kernel(bins, parts, len(rights), not a...]
    ppermute x2, waiting for transfers between devices: 4.81 us -> 2.51 us  [shift_apart(): return lax.ppermute(value, (axis, 'core'), pairs)]
    pallas_call x3 -> x4, Pallas kernels: 3.49 us -> 4.61 us  [tie(): pl.pallas_call(tie_kernel, out_shape=[shape(a.shape, a.dtype) for a in ar...]
    unnamed x22 -> x24, local copies, waits for them, and re-layouts: 2.59 us -> 3.58 us
  transfers between devices with their start and end apart: 26 -> 26, of which waited for: 12 -> 11; matrix products, arithmetic and copies ran while one was open for 2% -> 2% of each run, Pallas kernels for 15% -> 22%
where the time goes in v5:
time: 148 us; the launch traced here: 145 us
  waiting for transfers between devices  70.4 us (48%)
  Pallas kernels  34.2 us (23%)
  starting transfers between devices  31.5 us (21%)
  local copies, waits for them, and re-layouts  4.59 us (3%)
  other arithmetic  3.55 us (2%)
    ppermute x23, waiting for transfers between devices, shift(): lax.ppermute(value, axis, [(i, (i + by) % size) for i in range(size)])  61.4 us
    pallas_call x5, Pallas kernels, stage(): pl.pallas_call(lambda *refs: stage_kernel(bins, parts, len(rights), not a...  25.8 us
    ppermute x23, starting transfers between devices, shift(): lax.ppermute(value, axis, [(i, (i + by) % size) for i in range(size)])  21.9 us
    all_to_all x1, waiting for transfers between devices, body(): lax.all_to_all(factor_blocks.reshape(SA, BS, BS), ('y', 'x', 'core'), spl...  6.43 us
    all_to_all x1, starting transfers between devices, body(): lax.all_to_all(factor_blocks.reshape(SA, BS, BS), ('y', 'x', 'core'), spl...  6.06 us
    pallas_call x4, Pallas kernels, tie(): pl.pallas_call(tie_kernel, out_shape=[shape(a.shape, a.dtype) for a in ar...  4.61 us
    unnamed x24, local copies, waits for them, and re-layouts  3.58 us
    ppermute x2, starting transfers between devices, shift_apart(): return lax.ppermute(value, (axis, 'core'), pairs)  3.52 us
  transfers between devices with their start and end apart: 26, of which 11 were waited for; matrix products, arithmetic and copies ran while one was open for 2% of the time, Pallas kernels for 22%

profile of v5, /device:TPU:34, one launch (start us, length us, event | category | flops | bytes accessed | tf_op | source)
XLA Modules:
  0.0 145.2 jit_solution(13837945302838462008)
XLA Ops:
  0.0 6.1 %all-to-all-start = ((f32[16,128,128]{2,1,0:T(8,128)}), f32[16,128,128]{2,1,0:T(8,128)S(1)}, u32[]{:S(2)}, u32[]{:S(2)}) async-start(f32[16,128,128]{2,1,0:T(8,128)} %bitcast.39), calls=%async_computation | async-start | bytes 2097152 | tf_op jit(solution)/shard_map/all_to_all | solution.py:244
  6.1 0.8 slice_bitcast_fusion
  6.9 0.1 collective-permute-start.8
  7.1 1.1 collective-permute-done.8.refs_1_
  8.2 0.6 copy-done.8
  8.8 2.2 %pack.1 = f32[16,128,128]{2,1,0:T(8,128)} custom-call(f32[16,128,128]{2,1,0:T(8,128)} %bitcast.37, f32[1,128,128]{2,1,0:T(8,128)} %copy-done.8), custom_call_target="tpu_custom_call" | custom-call | tf_op jit(solution)/shard_map/pack/pallas_call | solution.py:168
  11.0 1.5 %collective-permute-start.9 = (f32[16,128,128]{2,1,0:T(8,128)}, f32[16,128,128]{2,1,0:T(8,128)}, u32[]{:S(2)}, u32[]{:S(2)}) collective-permute-start(f32[16,128,128]{2,1,0:T(8,128)} %pack.1), channel_id=1, source_target_pairs={{0,8},{8,16},{16,24},{24,0},{1,9},{9,17},{17,25},{25,1},{2,10},{10... | collective-permute-start | bytes 3145736 | tf_op jit(solution)/shard_map/ppermute | solution.py:186
  12.5 1.8 %collective-permute-start.10 = (f32[16,128,128]{2,1,0:T(8,128)}, f32[16,128,128]{2,1,0:T(8,128)}, u32[]{:S(2)}, u32[]{:S(2)}) collective-permute-start(f32[16,128,128]{2,1,0:T(8,128)} %pack.1), channel_id=1, source_target_pairs={{0,24},{8,0},{16,8},{24,16},{1,25},{9,1},{17,9},{25,17},{2,26},{10... | collective-permute-start | bytes 3145736 | tf_op jit(solution)/shard_map/ppermute | solution.py:186
  14.3 0.2 collective-permute-start.11
  14.5 0.5 witness.3.refs_1_
  15.0 0.0 copy-start.9
  15.0 6.4 %all-to-all-done.refs_0_ = f32[16,128,128]{2,1,0:T(8,128)S(1)} async-done(((f32[16,128,128]{2,1,0:T(8,128)}), f32[16,128,128]{2,1,0:T(8,128)S(1)}, u32[]{:S(2)}, u32[]{:S(2)}) %all-to-all-start) | async-done | bytes 1048608 | tf_op jit(solution)/shard_map/all_to_all | solution.py:244
  21.5 1.1 tie.4
  22.6 2.0 %collective-permute-start.1 = (f32[16,128,128]{2,1,0:T(8,128)S(1)}, f32[16,128,128]{2,1,0:T(8,128)S(1)}, u32[]{:S(2)}, u32[]{:S(2)}) collective-permute-start(f32[16,128,128]{2,1,0:T(8,128)S(1)} %get-tuple-element.31.refs_12_), channel_id=1, source_target_pairs={{0,32},{32,64},{64,96},{96,128},{128,160},{160,192},{192,224},{224... | collective-permute-start | bytes 3145736 | tf_op jit(solution)/shard_map/ppermute | solution.py:186
  24.6 0.1 collective-permute-start.4
  24.7 1.0 copy-done.1
  25.7 18.0 %collective-permute-done.9.refs_0_ = f32[16,128,128]{2,1,0:T(8,128)} collective-permute-done((f32[16,128,128]{2,1,0:T(8,128)}, f32[16,128,128]{2,1,0:T(8,128)}, u32[]{:S(2)}, u32[]{:S(2)}) %collective-permute-start.9) | collective-permute-done | bytes 1048608 | tf_op jit(solution)/shard_map/ppermute | solution.py:186
  43.8 0.1 collective-permute-start.12
  43.8 0.4 collective-permute-start.13
  44.3 0.1 collective-permute-start.14
  45.1 0.1 convert_reduce_fusion.1
  45.2 2.6 %collective-permute-done.1.refs_0_.refs_13_ = f32[16,128,128]{2,1,0:T(8,128)S(1)} collective-permute-done((f32[16,128,128]{2,1,0:T(8,128)S(1)}, f32[16,128,128]{2,1,0:T(8,128)S(1)}, u32[]{:S(2)}, u32[]{:S(2)}) %collective-permute-start.1) | collective-permute-done | bytes 1048608 | tf_op jit(solution)/shard_map/ppermute | solution.py:186
  47.8 1.9 %collective-permute-start.2 = (f32[16,128,128]{2,1,0:T(8,128)S(1)}, f32[16,128,128]{2,1,0:T(8,128)}, u32[]{:S(2)}, u32[]{:S(2)}) collective-permute-start(f32[16,128,128]{2,1,0:T(8,128)S(1)} %collective-permute-done.1.refs_0_.refs_13_), channel_id=1, source_target_pairs={{0,32},{32,64},{64,96},{96,128},{128,160},{160,192},{192,224},{224... | collective-permute-start | bytes 3145736 | tf_op jit(solution)/shard_map/ppermute | solution.py:186
  49.7 0.5 witness.4.refs_6_
  50.3 2.4 %collective-permute-start.5 = (f32[16,128,128]{2,1,0:T(8,128)S(1)}, f32[16,128,128]{2,1,0:T(8,128)S(1)}, u32[]{:S(2)}, u32[]{:S(2)}) collective-permute-start(f32[16,128,128]{2,1,0:T(8,128)S(1)} %collective-permute-done.4.refs_1_.refs_14_), channel_id=1, source_target_pairs={{0,224},{32,0},{64,32},{96,64},{128,96},{160,128},{192,160},{224,1... | collective-permute-start | bytes 3145736 | tf_op jit(solution)/shard_map/ppermute | solution.py:186
  52.7 1.2 tie.5
  53.8 0.1 collective-permute-start.15
  53.9 1.1 collective-permute-start.17
  55.1 3.0 %collective-permute-start.16 = (f32[16,128,128]{2,1,0:T(8,128)}, f32[16,128,128]{2,1,0:T(8,128)}, u32[]{:S(2)}, u32[]{:S(2)}) collective-permute-start(f32[16,128,128]{2,1,0:T(8,128)} %get-tuple-element.33.refs_8_), channel_id=1, source_target_pairs={{0,24},{8,0},{16,8},{24,16},{1,25},{9,1},{17,9},{25,17},{2,26},{10... | collective-permute-start | bytes 3145736 | tf_op jit(solution)/shard_map/ppermute | solution.py:186
  58.0 0.1 stack.99.refs_1_.refs_0_
  58.1 0.1 select_reduce_fusion.2.refs_2_.refs_1_
  58.3 0.1 select_reduce_fusion.1
  58.4 0.3 convert_reduce_fusion
  58.6 16.4 %collective-permute-done.2.refs_0_.refs_15_ = f32[16,128,128]{2,1,0:T(8,128)} collective-permute-done((f32[16,128,128]{2,1,0:T(8,128)S(1)}, f32[16,128,128]{2,1,0:T(8,128)}, u32[]{:S(2)}, u32[]{:S(2)}) %collective-permute-start.2) | collective-permute-done | bytes 1048608 | tf_op jit(solution)/shard_map/ppermute | solution.py:186
  75.0 0.9 collective-permute-done.5.refs_1_.refs_16_
  75.9 0.5 witness.5.refs_3_
  76.4 2.3 %collective-permute-start.6 = (f32[16,128,128]{2,1,0:T(8,128)S(1)}, f32[16,128,128]{2,1,0:T(8,128)S(1)}, u32[]{:S(2)}, u32[]{:S(2)}) collective-permute-start(f32[16,128,128]{2,1,0:T(8,128)S(1)} %collective-permute-done.5.refs_1_.refs_16_), channel_id=1, source_target_pairs={{0,224},{32,0},{64,32},{96,64},{128,96},{160,128},{192,160},{224,1... | collective-permute-start | bytes 3145736 | tf_op jit(solution)/shard_map/ppermute | solution.py:186
  78.8 1.0 collective-permute-done.15.refs_0_
  79.8 1.2 tie.6
  81.0 1.4 broadcast_select_fusion
  82.4 0.8 collective-permute-start.21
  83.2 0.2 select_reduce_fusion
  83.4 0.1 collective-permute-start.19
  83.5 0.5 collective-permute-start.20
  84.0 9.6 %stage_0_2.1 = (f32[256,128,128]{2,1,0:T(8,128)S(1)}, bf16[128,128,256]{2,1,0:T(8,128)(2,1)S(1)}, f32[33,128,128]{2,1,0:T(8,128)S(1)}, s32[1]{0:T(128)}) custom-call(s32[1]{0:T(128)} %get-tuple-element.35.refs_0_, s32[24]{0:T(128)S(1)} %stack.99.refs_1_.refs_0_, s32[7]{0:T(128)S(1)} %select_reduce_fusion.2.refs_2_.refs_1_, ...), custom_call_target="tpu_custom_call" | custom-call | flops 8000000000 | tf_op jit(solution)/shard_map/stage_0_2/pallas_call | solution.py:103
  93.6 1.2 tie.7
  94.8 5.4 %collective-permute-done.3.refs_11_ = f32[16,128,128]{2,1,0:T(8,128)S(1)} collective-permute-done((f32[16,128,128]{2,1,0:T(8,128)}, f32[16,128,128]{2,1,0:T(8,128)S(1)}, u32[]{:S(2)}, u32[]{:S(2)}) %collective-permute-start.3) | collective-permute-done | bytes 1048608 | tf_op jit(solution)/shard_map/ppermute | solution.py:186
  100.1 0.5 collective-permute-start.22
  100.6 0.7 collective-permute-done.6.refs_12_
  101.4 0.1 broadcast_select_fusion.1
  101.5 2.7 %collective-permute-start.7 = (f32[16,128,128]{2,1,0:T(8,128)S(1)}, f32[16,128,128]{2,1,0:T(8,128)S(1)}, u32[]{:S(2)}, u32[]{:S(2)}) collective-permute-start(f32[16,128,128]{2,1,0:T(8,128)S(1)} %broadcast_select_fusion.1), channel_id=1, source_target_pairs={{0,32},{2,226},{32,64},{34,2},{64,96},{66,34},{96,128},{98,66},{12... | collective-permute-start | bytes 3145736 | tf_op jit(solution)/shard_map/ppermute | solution.py:192
  104.3 0.9 copy-done.6
  105.2 0.4 copy-done.4
  105.6 0.3 copy-done.5
  105.9 0.3 copy-done.7
  106.3 7.8 %stage_2_3.1 = (f32[256,128,128]{2,1,0:T(8,128)S(1)}, bf16[128,128,256]{2,1,0:T(8,128)(2,1)S(1)}, f32[33,128,128]{2,1,0:T(8,128)S(1)}, s32[1]{0:T(128)}) custom-call(s32[24]{0:T(128)S(1)} %stack.99.refs_1_.refs_0_, s32[7]{0:T(128)S(1)} %select_reduce_fusion.2.refs_2_.refs_1_, ...), custom_call_target="tpu_custom_call", output_to_operand_aliasing={{0}: (13, {}), {1}: (14, {}), {2}: (15, {})} | custom-call | flops 10000000 | tf_op jit(solution)/shard_map/stage_2_3/pallas_call | solution.py:103
  114.1 2.5 %collective-permute-done.7.refs_3_ = f32[16,128,128]{2,1,0:T(8,128)S(1)} collective-permute-done((f32[16,128,128]{2,1,0:T(8,128)S(1)}, f32[16,128,128]{2,1,0:T(8,128)S(1)}, u32[]{:S(2)}, u32[]{:S(2)}) %collective-permute-start.7) | collective-permute-done | bytes 1048608 | tf_op jit(solution)/shard_map/ppermute | solution.py:192
  116.6 2.0 %stage_3_4.1 = (f32[256,128,128]{2,1,0:T(8,128)S(1)}, bf16[128,128,256]{2,1,0:T(8,128)(2,1)S(1)}, f32[33,128,128]{2,1,0:T(8,128)S(1)}, s32[1]{0:T(128)}) custom-call(s32[24]{0:T(128)S(1)} %stack.99.refs_1_.refs_0_, s32[7]{0:T(128)S(1)} %select_reduce_fusion.2.refs_2_.refs_1_, ...), custom_call_target="tpu_custom_call", output_to_operand_aliasing={{0}: (4, {}), {1}: (5, {}), {2}: (6, {})} | custom-call | tf_op jit(solution)/shard_map/stage_3_4/pallas_call | solution.py:103
  118.6 2.2 %collective-permute-start.23 = (f32[8,128,128]{2,1,0:T(8,128)S(1)}, f32[8,128,128]{2,1,0:T(8,128)S(1)}, u32[]{:S(2)}, u32[]{:S(2)}) collective-permute-start(f32[8,128,128]{2,1,0:T(8,128)S(1)} %slice.29), channel_id=1, source_target_pairs={{0,1},{1,0},{2,3},{3,2},{4,5},{5,4},{6,7},{7,6},{8,9},{9,8},{10,11... | collective-permute-start | bytes 1572872 | tf_op jit(solution)/shard_map/ppermute | solution.py:186
  120.8 1.6 %stage_4_5.1 = (f32[256,128,128]{2,1,0:T(8,128)S(1)}, bf16[128,128,256]{2,1,0:T(8,128)(2,1)S(1)}, f32[33,128,128]{2,1,0:T(8,128)S(1)}, s32[1]{0:T(128)}) custom-call(s32[24]{0:T(128)S(1)} %stack.99.refs_1_.refs_0_, s32[7]{0:T(128)S(1)} %select_reduce_fusion.2.refs_2_.refs_1_, ...), custom_call_target="tpu_custom_call", output_to_operand_aliasing={{0}: (3, {}), {1}: (4, {}), {2}: (5, {})} | custom-call | tf_op jit(solution)/shard_map/stage_4_5/pallas_call | solution.py:103
  122.5 1.5 %collective-permute-start.24 = (f32[8,128,128]{2,1,0:T(8,128)S(1)}, f32[8,128,128]{2,1,0:T(8,128)S(1)}, u32[]{:S(2)}, u32[]{:S(2)}) collective-permute-start(f32[8,128,128]{2,1,0:T(8,128)S(1)} %slice.30), channel_id=1, source_target_pairs={{0,1},{1,0},{2,3},{3,2},{4,5},{5,4},{6,7},{7,6},{8,9},{9,8},{10,11... | collective-permute-start | bytes 1572872 | tf_op jit(solution)/shard_map/ppermute | solution.py:186
  124.0 4.8 %stage_5_6.1 = (f32[256,128,128]{2,1,0:T(8,128)S(1)}, bf16[128,128,256]{2,1,0:T(8,128)(2,1)S(1)}, f32[33,128,128]{2,1,0:T(8,128)S(1)}, s32[1]{0:T(128)}) custom-call(s32[24]{0:T(128)S(1)} %stack.99.refs_1_.refs_0_, s32[7]{0:T(128)S(1)} %select_reduce_fusion.2.refs_2_.refs_1_, ...), custom_call_target="tpu_custom_call", output_to_operand_aliasing={{0}: (3, {}), {1}: (4, {}), {2}: (5, {})} | custom-call | flops 10000000000 | tf_op jit(solution)/shard_map/stage_5_6/pallas_call | solution.py:103
  128.8 15.3 %collective-permute-done.24 = f32[8,128,128]{2,1,0:T(8,128)S(1)} collective-permute-done((f32[8,128,128]{2,1,0:T(8,128)S(1)}, f32[8,128,128]{2,1,0:T(8,128)S(1)}, u32[]{:S(2)}, u32[]{:S(2)}) %collective-permute-start.24) | collective-permute-done | bytes 524320 | tf_op jit(solution)/shard_map/ppermute | solution.py:186
  144.1 1.1 fusion
  (43 shorter events, 0.2 us)
Async XLA Ops:
  0.0 14.5 %collective-permute-start = (f32[16,128,128]{2,1,0:T(8,128)}, f32[16,128,128]{2,1,0:T(8,128)S(1)}, u32[]{:S(2)}, u32[]{:S(2)}) collective-permute-start(f32[16,128,128]{2,1,0:T(8,128)} %bitcast.36), channel_id=1, source_target_pairs={{0,2},{2,0},{1,3},{3,1},{4,6},{6,4},{5,7},{7,5},{8,10},{10,8},{9,1... | collective-permute-start | bytes 3145736 | tf_op jit(solution)/shard_map/ppermute | solution.py:186
  0.0 21.5 %all-to-all-start = ((f32[16,128,128]{2,1,0:T(8,128)}), f32[16,128,128]{2,1,0:T(8,128)S(1)}, u32[]{:S(2)}, u32[]{:S(2)}) async-start(f32[16,128,128]{2,1,0:T(8,128)} %bitcast.39), calls=%async_computation | async-start | bytes 2097152 | tf_op jit(solution)/shard_map/all_to_all | solution.py:244
  6.9 1.3 collective-permute-start.8
  8.2 0.6 copy-start.8
  11.0 32.8 %collective-permute-start.9 = (f32[16,128,128]{2,1,0:T(8,128)}, f32[16,128,128]{2,1,0:T(8,128)}, u32[]{:S(2)}, u32[]{:S(2)}) collective-permute-start(f32[16,128,128]{2,1,0:T(8,128)} %pack.1), channel_id=1, source_target_pairs={{0,8},{8,16},{16,24},{24,0},{1,9},{9,17},{17,25},{25,1},{2,10},{10... | collective-permute-start | bytes 3145736 | tf_op jit(solution)/shard_map/ppermute | solution.py:186
  12.5 31.3 %collective-permute-start.10 = (f32[16,128,128]{2,1,0:T(8,128)}, f32[16,128,128]{2,1,0:T(8,128)}, u32[]{:S(2)}, u32[]{:S(2)}) collective-permute-start(f32[16,128,128]{2,1,0:T(8,128)} %pack.1), channel_id=1, source_target_pairs={{0,24},{8,0},{16,8},{24,16},{1,25},{9,1},{17,9},{25,17},{2,26},{10... | collective-permute-start | bytes 3145736 | tf_op jit(solution)/shard_map/ppermute | solution.py:186
  14.3 30.0 %collective-permute-start.11 = (f32[16,128,128]{2,1,0:T(8,128)}, f32[16,128,128]{2,1,0:T(8,128)}, u32[]{:S(2)}, u32[]{:S(2)}) collective-permute-start(f32[16,128,128]{2,1,0:T(8,128)} %pack.1), channel_id=1, source_target_pairs={{0,4},{4,0},{1,5},{5,1},{2,6},{6,2},{3,7},{7,3},{8,12},{12,8},{9,1... | collective-permute-start | bytes 3145736 | tf_op jit(solution)/shard_map/ppermute | solution.py:186
  14.5 8.1 %copy-start = (f32[16,128,128]{2,1,0:T(8,128)}, f32[16,128,128]{2,1,0:T(8,128)S(1)}, u32[]{:S(2)}) copy-start(f32[16,128,128]{2,1,0:T(8,128)S(1)} %collective-permute-done.refs_0_.refs_5_) | copy-start | bytes 3145732
  15.0 30.0 %copy-start.9 = (s32[1,1,1,512]{3,2,1,0:T(1,128)S(1)}, s32[1,1,1,512]{3,2,1,0:T(1,128)}, u32[]{:S(2)}) copy-start(s32[1,1,1,512]{3,2,1,0:T(1,128)} %param.9) | copy-start | bytes 6148
  15.0 30.0 %copy-start.10 = (s32[1,1,1,512]{3,2,1,0:T(1,128)S(1)}, s32[1,1,1,512]{3,2,1,0:T(1,128)}, u32[]{:S(2)}) copy-start(s32[1,1,1,512]{3,2,1,0:T(1,128)} %param.8) | copy-start | bytes 6148
  15.0 30.0 %copy-start.11 = (s32[1,1,1,512]{3,2,1,0:T(1,128)S(1)}, s32[1,1,1,512]{3,2,1,0:T(1,128)}, u32[]{:S(2)}) copy-start(s32[1,1,1,512]{3,2,1,0:T(1,128)} %param.10) | copy-start | bytes 6148
  22.6 25.2 %collective-permute-start.1 = (f32[16,128,128]{2,1,0:T(8,128)S(1)}, f32[16,128,128]{2,1,0:T(8,128)S(1)}, u32[]{:S(2)}, u32[]{:S(2)}) collective-permute-start(f32[16,128,128]{2,1,0:T(8,128)S(1)} %get-tuple-element.31.refs_12_), channel_id=1, source_target_pairs={{0,32},{32,64},{64,96},{96,128},{128,160},{160,192},{192,224},{224... | collective-permute-start | bytes 3145736 | tf_op jit(solution)/shard_map/ppermute | solution.py:186
  24.6 25.1 %collective-permute-start.4 = (f32[16,128,128]{2,1,0:T(8,128)S(1)}, f32[16,128,128]{2,1,0:T(8,128)S(1)}, u32[]{:S(2)}, u32[]{:S(2)}) collective-permute-start(f32[16,128,128]{2,1,0:T(8,128)S(1)} %get-tuple-element.31.refs_12_), channel_id=1, source_target_pairs={{0,224},{32,0},{64,32},{96,64},{128,96},{160,128},{192,160},{224,1... | collective-permute-start | bytes 3145736 | tf_op jit(solution)/shard_map/ppermute | solution.py:186
  24.7 1.0 copy-start.1
  43.8 8.9 %collective-permute-start.12 = (f32[16,128,128]{2,1,0:T(8,128)}, f32[16,128,128]{2,1,0:T(8,128)}, u32[]{:S(2)}, u32[]{:S(2)}) collective-permute-start(f32[16,128,128]{2,1,0:T(8,128)} %collective-permute-done.9.refs_0_), channel_id=1, source_target_pairs={{0,2},{2,0},{1,3},{3,1},{4,6},{6,4},{5,7},{7,5},{8,10},{10,8},{9,1... | collective-permute-start | bytes 3145736 | tf_op jit(solution)/shard_map/ppermute | solution.py:186
  43.8 8.8 %collective-permute-start.13 = (f32[16,128,128]{2,1,0:T(8,128)}, f32[16,128,128]{2,1,0:T(8,128)}, u32[]{:S(2)}, u32[]{:S(2)}) collective-permute-start(f32[16,128,128]{2,1,0:T(8,128)} %collective-permute-done.10.refs_1_), channel_id=1, source_target_pairs={{0,2},{2,0},{1,3},{3,1},{4,6},{6,4},{5,7},{7,5},{8,10},{10,8},{9,1... | collective-permute-start | bytes 3145736 | tf_op jit(solution)/shard_map/ppermute | solution.py:186
  44.3 8.4 %collective-permute-start.14 = (f32[16,128,128]{2,1,0:T(8,128)}, f32[16,128,128]{2,1,0:T(8,128)}, u32[]{:S(2)}, u32[]{:S(2)}) collective-permute-start(f32[16,128,128]{2,1,0:T(8,128)} %collective-permute-done.11.refs_2_), channel_id=1, source_target_pairs={{0,2},{2,0},{1,3},{3,1},{4,6},{6,4},{5,7},{7,5},{8,10},{10,8},{9,1... | collective-permute-start | bytes 3145736 | tf_op jit(solution)/shard_map/ppermute | solution.py:186
  47.8 27.2 %collective-permute-start.2 = (f32[16,128,128]{2,1,0:T(8,128)S(1)}, f32[16,128,128]{2,1,0:T(8,128)}, u32[]{:S(2)}, u32[]{:S(2)}) collective-permute-start(f32[16,128,128]{2,1,0:T(8,128)S(1)} %collective-permute-done.1.refs_0_.refs_13_), channel_id=1, source_target_pairs={{0,32},{32,64},{64,96},{96,128},{128,160},{160,192},{192,224},{224... | collective-permute-start | bytes 3145736 | tf_op jit(solution)/shard_map/ppermute | solution.py:186
  50.3 25.6 %collective-permute-start.5 = (f32[16,128,128]{2,1,0:T(8,128)S(1)}, f32[16,128,128]{2,1,0:T(8,128)S(1)}, u32[]{:S(2)}, u32[]{:S(2)}) collective-permute-start(f32[16,128,128]{2,1,0:T(8,128)S(1)} %collective-permute-done.4.refs_1_.refs_14_), channel_id=1, source_target_pairs={{0,224},{32,0},{64,32},{96,64},{128,96},{160,128},{192,160},{224,1... | collective-permute-start | bytes 3145736 | tf_op jit(solution)/shard_map/ppermute | solution.py:186
  53.8 25.9 %collective-permute-start.15 = (f32[16,128,128]{2,1,0:T(8,128)}, f32[16,128,128]{2,1,0:T(8,128)}, u32[]{:S(2)}, u32[]{:S(2)}) collective-permute-start(f32[16,128,128]{2,1,0:T(8,128)} %get-tuple-element.32.refs_6_), channel_id=1, source_target_pairs={{0,8},{8,16},{16,24},{24,0},{1,9},{9,17},{17,25},{25,1},{2,10},{10... | collective-permute-start | bytes 3145736 | tf_op jit(solution)/shard_map/ppermute | solution.py:186
  53.9 25.8 %collective-permute-start.17 = (f32[16,128,128]{2,1,0:T(8,128)}, f32[16,128,128]{2,1,0:T(8,128)}, u32[]{:S(2)}, u32[]{:S(2)}) collective-permute-start(f32[16,128,128]{2,1,0:T(8,128)} %get-tuple-element.32.refs_6_), channel_id=1, source_target_pairs={{0,4},{4,0},{1,5},{5,1},{2,6},{6,2},{3,7},{7,3},{8,12},{12,8},{9,1... | collective-permute-start | bytes 3145736 | tf_op jit(solution)/shard_map/ppermute | solution.py:186
  55.1 24.7 %collective-permute-start.16 = (f32[16,128,128]{2,1,0:T(8,128)}, f32[16,128,128]{2,1,0:T(8,128)}, u32[]{:S(2)}, u32[]{:S(2)}) collective-permute-start(f32[16,128,128]{2,1,0:T(8,128)} %get-tuple-element.33.refs_8_), channel_id=1, source_target_pairs={{0,24},{8,0},{16,8},{24,16},{1,25},{9,1},{17,9},{25,17},{2,26},{10... | collective-permute-start | bytes 3145736 | tf_op jit(solution)/shard_map/ppermute | solution.py:186
  75.0 25.1 %collective-permute-start.3 = (f32[16,128,128]{2,1,0:T(8,128)}, f32[16,128,128]{2,1,0:T(8,128)S(1)}, u32[]{:S(2)}, u32[]{:S(2)}) collective-permute-start(f32[16,128,128]{2,1,0:T(8,128)} %collective-permute-done.2.refs_0_.refs_15_), channel_id=1, source_target_pairs={{0,32},{32,64},{64,96},{96,128},{128,160},{160,192},{192,224},{224... | collective-permute-start | bytes 3145736 | tf_op jit(solution)/shard_map/ppermute | solution.py:186
  76.4 24.9 %collective-permute-start.6 = (f32[16,128,128]{2,1,0:T(8,128)S(1)}, f32[16,128,128]{2,1,0:T(8,128)S(1)}, u32[]{:S(2)}, u32[]{:S(2)}) collective-permute-start(f32[16,128,128]{2,1,0:T(8,128)S(1)} %collective-permute-done.5.refs_1_.refs_16_), channel_id=1, source_target_pairs={{0,224},{32,0},{64,32},{96,64},{128,96},{160,128},{192,160},{224,1... | collective-permute-start | bytes 3145736 | tf_op jit(solution)/shard_map/ppermute | solution.py:186
  80.9 3.0 %copy-start.2 = (f32[16,128,128]{2,1,0:T(8,128)S(1)}, f32[16,128,128]{2,1,0:T(8,128)}, u32[]{:S(2)}) copy-start(f32[16,128,128]{2,1,0:T(8,128)} %copy-done.1) | copy-start | bytes 3145732
  82.4 17.7 %collective-permute-start.21 = (f32[16,128,128]{2,1,0:T(8,128)S(1)}, f32[16,128,128]{2,1,0:T(8,128)S(1)}, u32[]{:S(2)}, u32[]{:S(2)}) collective-permute-start(f32[16,128,128]{2,1,0:T(8,128)S(1)} %broadcast_select_fusion), channel_id=1, source_target_pairs={{0,8},{2,26},{8,16},{10,2},{16,24},{18,10},{24,0},{26,18},{1,9},{3... | collective-permute-start | bytes 3145736 | tf_op jit(solution)/shard_map/ppermute | solution.py:192
  83.4 20.9 %collective-permute-start.19 = (f32[16,128,128]{2,1,0:T(8,128)}, f32[16,128,128]{2,1,0:T(8,128)S(1)}, u32[]{:S(2)}, u32[]{:S(2)}) collective-permute-start(f32[16,128,128]{2,1,0:T(8,128)} %get-tuple-element.42.refs_5_), channel_id=1, source_target_pairs={{0,2},{2,0},{1,3},{3,1},{4,6},{6,4},{5,7},{7,5},{8,10},{10,8},{9,1... | collective-permute-start | bytes 3145736 | tf_op jit(solution)/shard_map/ppermute | solution.py:186
  83.5 20.8 %collective-permute-start.20 = (f32[16,128,128]{2,1,0:T(8,128)}, f32[16,128,128]{2,1,0:T(8,128)S(1)}, u32[]{:S(2)}, u32[]{:S(2)}) collective-permute-start(f32[16,128,128]{2,1,0:T(8,128)} %get-tuple-element.43.refs_7_), channel_id=1, source_target_pairs={{0,2},{2,0},{1,3},{3,1},{4,6},{6,4},{5,7},{7,5},{8,10},{10,8},{9,1... | collective-permute-start | bytes 3145736 | tf_op jit(solution)/shard_map/ppermute | solution.py:186
  100.1 4.2 %collective-permute-start.18 = (f32[16,128,128]{2,1,0:T(8,128)}, f32[16,128,128]{2,1,0:T(8,128)S(1)}, u32[]{:S(2)}, u32[]{:S(2)}) collective-permute-start(f32[16,128,128]{2,1,0:T(8,128)} %get-tuple-element.41.refs_3_), channel_id=1, source_target_pairs={{0,2},{2,0},{1,3},{3,1},{4,6},{6,4},{5,7},{7,5},{8,10},{10,8},{9,1... | collective-permute-start | bytes 3145736 | tf_op jit(solution)/shard_map/ppermute | solution.py:186
  100.1 4.2 %copy-start.3 = (f32[16,128,128]{2,1,0:T(8,128)}, f32[16,128,128]{2,1,0:T(8,128)S(1)}, u32[]{:S(2)}) copy-start(f32[16,128,128]{2,1,0:T(8,128)S(1)} %collective-permute-done.21.refs_9_) | copy-start | bytes 3145732
  100.1 4.2 %collective-permute-start.22 = (f32[16,128,128]{2,1,0:T(8,128)S(1)}, f32[16,128,128]{2,1,0:T(8,128)S(1)}, u32[]{:S(2)}, u32[]{:S(2)}) collective-permute-start(f32[16,128,128]{2,1,0:T(8,128)S(1)} %collective-permute-done.21.refs_9_), channel_id=1, source_target_pairs={{0,2},{2,0},{1,3},{3,1},{4,6},{6,4},{5,7},{7,5},{8,10},{10,8},{9,1... | collective-permute-start | bytes 3145736 | tf_op jit(solution)/shard_map/ppermute | solution.py:186
  101.5 15.1 %collective-permute-start.7 = (f32[16,128,128]{2,1,0:T(8,128)S(1)}, f32[16,128,128]{2,1,0:T(8,128)S(1)}, u32[]{:S(2)}, u32[]{:S(2)}) collective-permute-start(f32[16,128,128]{2,1,0:T(8,128)S(1)} %broadcast_select_fusion.1), channel_id=1, source_target_pairs={{0,32},{2,226},{32,64},{34,2},{64,96},{66,34},{96,128},{98,66},{12... | collective-permute-start | bytes 3145736 | tf_op jit(solution)/shard_map/ppermute | solution.py:192
  104.3 1.0 copy-start.6
  104.3 1.3 copy-start.4
  104.3 1.6 %copy-start.5 = (f32[16,128,128]{2,1,0:T(8,128)}, f32[16,128,128]{2,1,0:T(8,128)S(1)}, u32[]{:S(2)}) copy-start(f32[16,128,128]{2,1,0:T(8,128)S(1)} %collective-permute-done.20.refs_8_) | copy-start | bytes 3145732
  104.3 1.9 %copy-start.7 = (f32[16,128,128]{2,1,0:T(8,128)}, f32[16,128,128]{2,1,0:T(8,128)S(1)}, u32[]{:S(2)}) copy-start(f32[16,128,128]{2,1,0:T(8,128)S(1)} %collective-permute-done.22.refs_10_) | copy-start | bytes 3145732
  118.6 25.4 %collective-permute-start.23 = (f32[8,128,128]{2,1,0:T(8,128)S(1)}, f32[8,128,128]{2,1,0:T(8,128)S(1)}, u32[]{:S(2)}, u32[]{:S(2)}) collective-permute-start(f32[8,128,128]{2,1,0:T(8,128)S(1)} %slice.29), channel_id=1, source_target_pairs={{0,1},{1,0},{2,3},{3,2},{4,5},{5,4},{6,7},{7,6},{8,9},{9,8},{10,11... | collective-permute-start | bytes 1572872 | tf_op jit(solution)/shard_map/ppermute | solution.py:186
  122.5 21.6 %collective-permute-start.24 = (f32[8,128,128]{2,1,0:T(8,128)S(1)}, f32[8,128,128]{2,1,0:T(8,128)S(1)}, u32[]{:S(2)}, u32[]{:S(2)}) collective-permute-start(f32[8,128,128]{2,1,0:T(8,128)S(1)} %slice.30), channel_id=1, source_target_pairs={{0,1},{1,0},{2,3},{3,2},{4,5},{5,4},{6,7},{7,6},{8,9},{9,8},{10,11... | collective-permute-start | bytes 1572872 | tf_op jit(solution)/shard_map/ppermute | solution.py:186

commit v6 on v5

--- a/solution.py
+++ b/solution.py
@@ -198,7 +198,8 @@
     kept = target_index // SCH == layer
     right_class = jnp.where((away <= 2) | (away >= 6), 0, jnp.where(away == 4, 2, 1))
     here = jnp.maximum(left_class, right_class)
-    bins = jnp.where(here == 0, jnp.where(kept, 1, 0), jnp.where(kept, 5, 1 + here + (here == 2) * (target_index % SCH // (SCH // 2))))
+    sent = jnp.where(here == 0, 0, 1 + here + (here == 2) * (target_index % SCH // (SCH // 2)))
+    bins = jnp.where(kept, 5, sent)
     bins = jnp.where(p < count, bins, BINS)
     target = jnp.where(kept, 0, SCH) + target_index % SCH
     code = (left_index << 16) | (right_index << 8) | target

time: 148 us -> 148 us (level)
  the two profiles are of different devices: /device:TPU:34 before, /device:TPU:6 now
where the time goes in v6:
time: 148 us
  waiting for transfers between devices  81.5 us (55%)
  starting transfers between devices  33.7 us (23%)
  Pallas kernels  24 us (16%)
  local copies, waits for them, and re-layouts  3.89 us (3%)
  other arithmetic  3.56 us (2%)
    ppermute x23, waiting for transfers between devices, shift(): lax.ppermute(value, axis, [(i, (i + by) % size) for i in range(size)])  68.6 us
    ppermute x23, starting transfers between devices, shift(): lax.ppermute(value, axis, [(i, (i + by) % size) for i in range(size)])  26.7 us
    pallas_call x5, Pallas kernels, stage(): pl.pallas_call(lambda *refs: stage_kernel(bins, parts, len(rights), not a...  15.6 us
    all_to_all x1, waiting for transfers between devices, body(): lax.all_to_all(factor_blocks.reshape(SA, BS, BS), ('y', 'x', 'core'), spl...  6.43 us
    ppermute x2, waiting for transfers between devices, shift_apart(): return lax.ppermute(value, (axis, 'core'), pairs)  6.43 us
    all_to_all x1, starting transfers between devices, body(): lax.all_to_all(factor_blocks.reshape(SA, BS, BS), ('y', 'x', 'core'), spl...  6.06 us
    pallas_call x4, Pallas kernels, tie(): pl.pallas_call(tie_kernel, out_shape=[shape(a.shape, a.dtype) for a in ar...  4.61 us
  transfers between devices with their start and end apart: 26, of which 11 were waited for; matrix products, arithmetic and copies ran while one was open for 2% of the time, Pallas kernels for 15%

profile of v6, /device:TPU:6, one launch (start us, length us, event | category | flops | bytes accessed | tf_op | source)
XLA Modules:
  0.0 147.5 jit_solution(11681184330498820252)
XLA Ops:
  0.0 6.1 %all-to-all-start = ((f32[16,128,128]{2,1,0:T(8,128)}), f32[16,128,128]{2,1,0:T(8,128)S(1)}, u32[]{:S(2)}, u32[]{:S(2)}) async-start(f32[16,128,128]{2,1,0:T(8,128)} %bitcast.39), calls=%async_computation | async-start | bytes 2097152 | tf_op jit(solution)/shard_map/all_to_all | solution.py:245
  6.1 0.8 slice_bitcast_fusion
  6.9 0.1 collective-permute-start.8
  7.1 1.1 collective-permute-done.8.refs_1_
  8.2 0.6 copy-done.8
  8.8 2.2 %pack.1 = f32[16,128,128]{2,1,0:T(8,128)} custom-call(f32[16,128,128]{2,1,0:T(8,128)} %bitcast.37, f32[1,128,128]{2,1,0:T(8,128)} %copy-done.8), custom_call_target="tpu_custom_call" | custom-call | tf_op jit(solution)/shard_map/pack/pallas_call | solution.py:168
  11.0 1.5 %collective-permute-start.9 = (f32[16,128,128]{2,1,0:T(8,128)}, f32[16,128,128]{2,1,0:T(8,128)}, u32[]{:S(2)}, u32[]{:S(2)}) collective-permute-start(f32[16,128,128]{2,1,0:T(8,128)} %pack.1), channel_id=1, source_target_pairs={{0,8},{8,16},{16,24},{24,0},{1,9},{9,17},{17,25},{25,1},{2,10},{10... | collective-permute-start | bytes 3145736 | tf_op jit(solution)/shard_map/ppermute | solution.py:186
  12.5 1.8 %collective-permute-start.10 = (f32[16,128,128]{2,1,0:T(8,128)}, f32[16,128,128]{2,1,0:T(8,128)}, u32[]{:S(2)}, u32[]{:S(2)}) collective-permute-start(f32[16,128,128]{2,1,0:T(8,128)} %pack.1), channel_id=1, source_target_pairs={{0,24},{8,0},{16,8},{24,16},{1,25},{9,1},{17,9},{25,17},{2,26},{10... | collective-permute-start | bytes 3145736 | tf_op jit(solution)/shard_map/ppermute | solution.py:186
  14.3 0.2 collective-permute-start.11
  14.5 0.5 witness.3.refs_1_
  15.0 0.0 copy-start.9
  15.0 0.0 copy-start.11
  15.0 6.4 %all-to-all-done.refs_0_ = f32[16,128,128]{2,1,0:T(8,128)S(1)} async-done(((f32[16,128,128]{2,1,0:T(8,128)}), f32[16,128,128]{2,1,0:T(8,128)S(1)}, u32[]{:S(2)}, u32[]{:S(2)}) %all-to-all-start) | async-done | bytes 1048608 | tf_op jit(solution)/shard_map/all_to_all | solution.py:245
  21.5 1.1 tie.4
  22.6 2.0 %collective-permute-start.1 = (f32[16,128,128]{2,1,0:T(8,128)S(1)}, f32[16,128,128]{2,1,0:T(8,128)S(1)}, u32[]{:S(2)}, u32[]{:S(2)}) collective-permute-start(f32[16,128,128]{2,1,0:T(8,128)S(1)} %get-tuple-element.31.refs_12_), channel_id=1, source_target_pairs={{0,32},{32,64},{64,96},{96,128},{128,160},{160,192},{192,224},{224... | collective-permute-start | bytes 3145736 | tf_op jit(solution)/shard_map/ppermute | solution.py:186
  24.6 4.0 %collective-permute-start.4 = (f32[16,128,128]{2,1,0:T(8,128)S(1)}, f32[16,128,128]{2,1,0:T(8,128)S(1)}, u32[]{:S(2)}, u32[]{:S(2)}) collective-permute-start(f32[16,128,128]{2,1,0:T(8,128)S(1)} %get-tuple-element.31.refs_12_), channel_id=1, source_target_pairs={{0,224},{32,0},{64,32},{96,64},{128,96},{160,128},{192,160},{224,1... | collective-permute-start | bytes 3145736 | tf_op jit(solution)/shard_map/ppermute | solution.py:186
  28.6 1.0 copy-done.1
  29.6 14.1 %collective-permute-done.9.refs_0_ = f32[16,128,128]{2,1,0:T(8,128)} collective-permute-done((f32[16,128,128]{2,1,0:T(8,128)}, f32[16,128,128]{2,1,0:T(8,128)}, u32[]{:S(2)}, u32[]{:S(2)}) %collective-permute-start.9) | collective-permute-done | bytes 1048608 | tf_op jit(solution)/shard_map/ppermute | solution.py:186
  43.8 0.1 collective-permute-start.12
  43.8 0.4 collective-permute-start.13
  44.3 0.1 collective-permute-start.14
  45.1 0.1 convert_reduce_fusion.1
  45.2 6.7 %collective-permute-done.1.refs_0_.refs_13_ = f32[16,128,128]{2,1,0:T(8,128)S(1)} collective-permute-done((f32[16,128,128]{2,1,0:T(8,128)S(1)}, f32[16,128,128]{2,1,0:T(8,128)S(1)}, u32[]{:S(2)}, u32[]{:S(2)}) %collective-permute-start.1) | collective-permute-done | bytes 1048608 | tf_op jit(solution)/shard_map/ppermute | solution.py:186
  51.9 0.5 witness.4.refs_6_
  52.5 3.3 %collective-permute-start.5 = (f32[16,128,128]{2,1,0:T(8,128)S(1)}, f32[16,128,128]{2,1,0:T(8,128)S(1)}, u32[]{:S(2)}, u32[]{:S(2)}) collective-permute-start(f32[16,128,128]{2,1,0:T(8,128)S(1)} %collective-permute-done.4.refs_1_.refs_14_), channel_id=1, source_target_pairs={{0,224},{32,0},{64,32},{96,64},{128,96},{160,128},{192,160},{224,1... | collective-permute-start | bytes 3145736 | tf_op jit(solution)/shard_map/ppermute | solution.py:186
  55.8 1.2 tie.5
  57.0 0.2 collective-permute-start.15
  57.2 1.0 collective-permute-start.17
  58.2 3.0 %collective-permute-start.16 = (f32[16,128,128]{2,1,0:T(8,128)}, f32[16,128,128]{2,1,0:T(8,128)}, u32[]{:S(2)}, u32[]{:S(2)}) collective-permute-start(f32[16,128,128]{2,1,0:T(8,128)} %get-tuple-element.33.refs_8_), channel_id=1, source_target_pairs={{0,24},{8,0},{16,8},{24,16},{1,25},{9,1},{17,9},{25,17},{2,26},{10... | collective-permute-start | bytes 3145736 | tf_op jit(solution)/shard_map/ppermute | solution.py:186
  61.1 0.1 stack.99.refs_1_.refs_0_
  61.3 0.1 select_reduce_fusion.2.refs_2_.refs_1_
  61.4 0.1 select_reduce_fusion.1
  61.5 0.3 convert_reduce_fusion
  61.7 16.1 %collective-permute-done.2.refs_0_.refs_15_ = f32[16,128,128]{2,1,0:T(8,128)} collective-permute-done((f32[16,128,128]{2,1,0:T(8,128)S(1)}, f32[16,128,128]{2,1,0:T(8,128)}, u32[]{:S(2)}, u32[]{:S(2)}) %collective-permute-start.2) | collective-permute-done | bytes 1048608 | tf_op jit(solution)/shard_map/ppermute | solution.py:186
  77.9 0.5 witness.5.refs_3_
  78.4 3.7 %collective-permute-start.6 = (f32[16,128,128]{2,1,0:T(8,128)S(1)}, f32[16,128,128]{2,1,0:T(8,128)S(1)}, u32[]{:S(2)}, u32[]{:S(2)}) collective-permute-start(f32[16,128,128]{2,1,0:T(8,128)S(1)} %collective-permute-done.5.refs_1_.refs_16_), channel_id=1, source_target_pairs={{0,224},{32,0},{64,32},{96,64},{128,96},{160,128},{192,160},{224,1... | collective-permute-start | bytes 3145736 | tf_op jit(solution)/shard_map/ppermute | solution.py:186
  82.1 0.5 collective-permute-done.15.refs_0_
  82.6 1.2 tie.6
  83.8 1.4 broadcast_select_fusion
  85.2 0.8 collective-permute-start.21
  86.1 0.2 select_reduce_fusion
  86.3 0.1 collective-permute-start.19
  86.4 0.5 collective-permute-start.20
  86.9 6.4 %stage_0_2.1 = (f32[256,128,128]{2,1,0:T(8,128)S(1)}, bf16[128,128,256]{2,1,0:T(8,128)(2,1)S(1)}, f32[33,128,128]{2,1,0:T(8,128)S(1)}, s32[1]{0:T(128)}) custom-call(s32[1]{0:T(128)} %get-tuple-element.35.refs_0_, s32[24]{0:T(128)S(1)} %stack.99.refs_1_.refs_0_, s32[7]{0:T(128)S(1)} %select_reduce_fusion.2.refs_2_.refs_1_, ...), custom_call_target="tpu_custom_call" | custom-call | flops 8000000000 | tf_op jit(solution)/shard_map/stage_0_2/pallas_call | solution.py:103
  93.2 1.2 tie.7
  94.4 8.5 %collective-permute-done.3.refs_11_ = f32[16,128,128]{2,1,0:T(8,128)S(1)} collective-permute-done((f32[16,128,128]{2,1,0:T(8,128)}, f32[16,128,128]{2,1,0:T(8,128)S(1)}, u32[]{:S(2)}, u32[]{:S(2)}) %collective-permute-start.3) | collective-permute-done | bytes 1048608 | tf_op jit(solution)/shard_map/ppermute | solution.py:186
  103.0 0.5 collective-permute-start.22
  103.5 0.1 broadcast_select_fusion.1
  103.6 0.1 collective-permute-start.7
  103.7 2.6 %collective-permute-done.18.refs_4_ = f32[16,128,128]{2,1,0:T(8,128)S(1)} collective-permute-done((f32[16,128,128]{2,1,0:T(8,128)}, f32[16,128,128]{2,1,0:T(8,128)S(1)}, u32[]{:S(2)}, u32[]{:S(2)}) %collective-permute-start.18) | collective-permute-done | bytes 1048608 | tf_op jit(solution)/shard_map/ppermute | solution.py:186
  106.4 0.7 collective-permute-done.22.refs_10_
  107.1 0.2 copy-done.6
  107.3 0.4 copy-done.4
  107.7 0.3 copy-done.5
  108.0 0.3 copy-done.7
  108.3 5.0 %stage_2_3.1 = (f32[256,128,128]{2,1,0:T(8,128)S(1)}, bf16[128,128,256]{2,1,0:T(8,128)(2,1)S(1)}, f32[33,128,128]{2,1,0:T(8,128)S(1)}, s32[1]{0:T(128)}) custom-call(s32[24]{0:T(128)S(1)} %stack.99.refs_1_.refs_0_, s32[7]{0:T(128)S(1)} %select_reduce_fusion.2.refs_2_.refs_1_, ...), custom_call_target="tpu_custom_call", output_to_operand_aliasing={{0}: (13, {}), {1}: (14, {}), {2}: (15, {})} | custom-call | flops 10000000 | tf_op jit(solution)/shard_map/stage_2_3/pallas_call | solution.py:103
  113.4 6.4 %collective-permute-done.7.refs_3_ = f32[16,128,128]{2,1,0:T(8,128)S(1)} collective-permute-done((f32[16,128,128]{2,1,0:T(8,128)S(1)}, f32[16,128,128]{2,1,0:T(8,128)S(1)}, u32[]{:S(2)}, u32[]{:S(2)}) %collective-permute-start.7) | collective-permute-done | bytes 1048608 | tf_op jit(solution)/shard_map/ppermute | solution.py:192
  119.8 1.5 %stage_3_4.1 = (f32[256,128,128]{2,1,0:T(8,128)S(1)}, bf16[128,128,256]{2,1,0:T(8,128)(2,1)S(1)}, f32[33,128,128]{2,1,0:T(8,128)S(1)}, s32[1]{0:T(128)}) custom-call(s32[24]{0:T(128)S(1)} %stack.99.refs_1_.refs_0_, s32[7]{0:T(128)S(1)} %select_reduce_fusion.2.refs_2_.refs_1_, ...), custom_call_target="tpu_custom_call", output_to_operand_aliasing={{0}: (4, {}), {1}: (5, {}), {2}: (6, {})} | custom-call | tf_op jit(solution)/shard_map/stage_3_4/pallas_call | solution.py:103
  121.4 1.9 %collective-permute-start.23 = (f32[8,128,128]{2,1,0:T(8,128)S(1)}, f32[8,128,128]{2,1,0:T(8,128)S(1)}, u32[]{:S(2)}, u32[]{:S(2)}) collective-permute-start(f32[8,128,128]{2,1,0:T(8,128)S(1)} %slice.29), channel_id=1, source_target_pairs={{0,1},{1,0},{2,3},{3,2},{4,5},{5,4},{6,7},{7,6},{8,9},{9,8},{10,11... | collective-permute-start | bytes 1572872 | tf_op jit(solution)/shard_map/ppermute | solution.py:186
  123.3 1.1 stage_4_5.1
  124.5 2.2 %collective-permute-start.24 = (f32[8,128,128]{2,1,0:T(8,128)S(1)}, f32[8,128,128]{2,1,0:T(8,128)S(1)}, u32[]{:S(2)}, u32[]{:S(2)}) collective-permute-start(f32[8,128,128]{2,1,0:T(8,128)S(1)} %slice.30), channel_id=1, source_target_pairs={{0,1},{1,0},{2,3},{3,2},{4,5},{5,4},{6,7},{7,6},{8,9},{9,8},{10,11... | collective-permute-start | bytes 1572872 | tf_op jit(solution)/shard_map/ppermute | solution.py:186
  126.7 1.6 %stage_5_6.1 = (f32[256,128,128]{2,1,0:T(8,128)S(1)}, bf16[128,128,256]{2,1,0:T(8,128)(2,1)S(1)}, f32[33,128,128]{2,1,0:T(8,128)S(1)}, s32[1]{0:T(128)}) custom-call(s32[24]{0:T(128)S(1)} %stack.99.refs_1_.refs_0_, s32[7]{0:T(128)S(1)} %select_reduce_fusion.2.refs_2_.refs_1_, ...), custom_call_target="tpu_custom_call", output_to_operand_aliasing={{0}: (3, {}), {1}: (4, {}), {2}: (5, {})} | custom-call | flops 10000000000 | tf_op jit(solution)/shard_map/stage_5_6/pallas_call | solution.py:103
  128.3 18.1 %collective-permute-done.24 = f32[8,128,128]{2,1,0:T(8,128)S(1)} collective-permute-done((f32[8,128,128]{2,1,0:T(8,128)S(1)}, f32[8,128,128]{2,1,0:T(8,128)S(1)}, u32[]{:S(2)}, u32[]{:S(2)}) %collective-permute-start.24) | collective-permute-done | bytes 524320 | tf_op jit(solution)/shard_map/ppermute | solution.py:186
  146.4 1.1 fusion
  (43 shorter events, 0.2 us)
Async XLA Ops:
  0.0 14.5 %collective-permute-start = (f32[16,128,128]{2,1,0:T(8,128)}, f32[16,128,128]{2,1,0:T(8,128)S(1)}, u32[]{:S(2)}, u32[]{:S(2)}) collective-permute-start(f32[16,128,128]{2,1,0:T(8,128)} %bitcast.36), channel_id=1, source_target_pairs={{0,2},{2,0},{1,3},{3,1},{4,6},{6,4},{5,7},{7,5},{8,10},{10,8},{9,1... | collective-permute-start | bytes 3145736 | tf_op jit(solution)/shard_map/ppermute | solution.py:186
  0.0 21.5 %all-to-all-start = ((f32[16,128,128]{2,1,0:T(8,128)}), f32[16,128,128]{2,1,0:T(8,128)S(1)}, u32[]{:S(2)}, u32[]{:S(2)}) async-start(f32[16,128,128]{2,1,0:T(8,128)} %bitcast.39), calls=%async_computation | async-start | bytes 2097152 | tf_op jit(solution)/shard_map/all_to_all | solution.py:245
  6.9 1.3 collective-permute-start.8
  8.2 0.6 copy-start.8
  11.0 32.8 %collective-permute-start.9 = (f32[16,128,128]{2,1,0:T(8,128)}, f32[16,128,128]{2,1,0:T(8,128)}, u32[]{:S(2)}, u32[]{:S(2)}) collective-permute-start(f32[16,128,128]{2,1,0:T(8,128)} %pack.1), channel_id=1, source_target_pairs={{0,8},{8,16},{16,24},{24,0},{1,9},{9,17},{17,25},{25,1},{2,10},{10... | collective-permute-start | bytes 3145736 | tf_op jit(solution)/shard_map/ppermute | solution.py:186
  12.5 31.3 %collective-permute-start.10 = (f32[16,128,128]{2,1,0:T(8,128)}, f32[16,128,128]{2,1,0:T(8,128)}, u32[]{:S(2)}, u32[]{:S(2)}) collective-permute-start(f32[16,128,128]{2,1,0:T(8,128)} %pack.1), channel_id=1, source_target_pairs={{0,24},{8,0},{16,8},{24,16},{1,25},{9,1},{17,9},{25,17},{2,26},{10... | collective-permute-start | bytes 3145736 | tf_op jit(solution)/shard_map/ppermute | solution.py:186
  14.3 30.0 %collective-permute-start.11 = (f32[16,128,128]{2,1,0:T(8,128)}, f32[16,128,128]{2,1,0:T(8,128)}, u32[]{:S(2)}, u32[]{:S(2)}) collective-permute-start(f32[16,128,128]{2,1,0:T(8,128)} %pack.1), channel_id=1, source_target_pairs={{0,4},{4,0},{1,5},{5,1},{2,6},{6,2},{3,7},{7,3},{8,12},{12,8},{9,1... | collective-permute-start | bytes 3145736 | tf_op jit(solution)/shard_map/ppermute | solution.py:186
  14.5 8.1 %copy-start = (f32[16,128,128]{2,1,0:T(8,128)}, f32[16,128,128]{2,1,0:T(8,128)S(1)}, u32[]{:S(2)}) copy-start(f32[16,128,128]{2,1,0:T(8,128)S(1)} %collective-permute-done.refs_0_.refs_5_) | copy-start | bytes 3145732
  15.0 30.0 %copy-start.9 = (s32[1,1,1,512]{3,2,1,0:T(1,128)S(1)}, s32[1,1,1,512]{3,2,1,0:T(1,128)}, u32[]{:S(2)}) copy-start(s32[1,1,1,512]{3,2,1,0:T(1,128)} %param.9) | copy-start | bytes 6148
  15.0 30.0 %copy-start.10 = (s32[1,1,1,512]{3,2,1,0:T(1,128)S(1)}, s32[1,1,1,512]{3,2,1,0:T(1,128)}, u32[]{:S(2)}) copy-start(s32[1,1,1,512]{3,2,1,0:T(1,128)} %param.8) | copy-start | bytes 6148
  15.0 30.0 %copy-start.11 = (s32[1,1,1,512]{3,2,1,0:T(1,128)S(1)}, s32[1,1,1,512]{3,2,1,0:T(1,128)}, u32[]{:S(2)}) copy-start(s32[1,1,1,512]{3,2,1,0:T(1,128)} %param.10) | copy-start | bytes 6148
  22.6 29.3 %collective-permute-start.1 = (f32[16,128,128]{2,1,0:T(8,128)S(1)}, f32[16,128,128]{2,1,0:T(8,128)S(1)}, u32[]{:S(2)}, u32[]{:S(2)}) collective-permute-start(f32[16,128,128]{2,1,0:T(8,128)S(1)} %get-tuple-element.31.refs_12_), channel_id=1, source_target_pairs={{0,32},{32,64},{64,96},{96,128},{128,160},{160,192},{192,224},{224... | collective-permute-start | bytes 3145736 | tf_op jit(solution)/shard_map/ppermute | solution.py:186
  24.6 27.3 %collective-permute-start.4 = (f32[16,128,128]{2,1,0:T(8,128)S(1)}, f32[16,128,128]{2,1,0:T(8,128)S(1)}, u32[]{:S(2)}, u32[]{:S(2)}) collective-permute-start(f32[16,128,128]{2,1,0:T(8,128)S(1)} %get-tuple-element.31.refs_12_), channel_id=1, source_target_pairs={{0,224},{32,0},{64,32},{96,64},{128,96},{160,128},{192,160},{224,1... | collective-permute-start | bytes 3145736 | tf_op jit(solution)/shard_map/ppermute | solution.py:186
  28.6 1.0 copy-start.1
  43.8 12.0 %collective-permute-start.12 = (f32[16,128,128]{2,1,0:T(8,128)}, f32[16,128,128]{2,1,0:T(8,128)}, u32[]{:S(2)}, u32[]{:S(2)}) collective-permute-start(f32[16,128,128]{2,1,0:T(8,128)} %collective-permute-done.9.refs_0_), channel_id=1, source_target_pairs={{0,2},{2,0},{1,3},{3,1},{4,6},{6,4},{5,7},{7,5},{8,10},{10,8},{9,1... | collective-permute-start | bytes 3145736 | tf_op jit(solution)/shard_map/ppermute | solution.py:186
  43.8 12.0 %collective-permute-start.13 = (f32[16,128,128]{2,1,0:T(8,128)}, f32[16,128,128]{2,1,0:T(8,128)}, u32[]{:S(2)}, u32[]{:S(2)}) collective-permute-start(f32[16,128,128]{2,1,0:T(8,128)} %collective-permute-done.10.refs_1_), channel_id=1, source_target_pairs={{0,2},{2,0},{1,3},{3,1},{4,6},{6,4},{5,7},{7,5},{8,10},{10,8},{9,1... | collective-permute-start | bytes 3145736 | tf_op jit(solution)/shard_map/ppermute | solution.py:186
  44.3 11.5 %collective-permute-start.14 = (f32[16,128,128]{2,1,0:T(8,128)}, f32[16,128,128]{2,1,0:T(8,128)}, u32[]{:S(2)}, u32[]{:S(2)}) collective-permute-start(f32[16,128,128]{2,1,0:T(8,128)} %collective-permute-done.11.refs_2_), channel_id=1, source_target_pairs={{0,2},{2,0},{1,3},{3,1},{4,6},{6,4},{5,7},{7,5},{8,10},{10,8},{9,1... | collective-permute-start | bytes 3145736 | tf_op jit(solution)/shard_map/ppermute | solution.py:186
  51.9 25.9 %collective-permute-start.2 = (f32[16,128,128]{2,1,0:T(8,128)S(1)}, f32[16,128,128]{2,1,0:T(8,128)}, u32[]{:S(2)}, u32[]{:S(2)}) collective-permute-start(f32[16,128,128]{2,1,0:T(8,128)S(1)} %collective-permute-done.1.refs_0_.refs_13_), channel_id=1, source_target_pairs={{0,32},{32,64},{64,96},{96,128},{128,160},{160,192},{192,224},{224... | collective-permute-start | bytes 3145736 | tf_op jit(solution)/shard_map/ppermute | solution.py:186
  52.5 25.4 %collective-permute-start.5 = (f32[16,128,128]{2,1,0:T(8,128)S(1)}, f32[16,128,128]{2,1,0:T(8,128)S(1)}, u32[]{:S(2)}, u32[]{:S(2)}) collective-permute-start(f32[16,128,128]{2,1,0:T(8,128)S(1)} %collective-permute-done.4.refs_1_.refs_14_), channel_id=1, source_target_pairs={{0,224},{32,0},{64,32},{96,64},{128,96},{160,128},{192,160},{224,1... | collective-permute-start | bytes 3145736 | tf_op jit(solution)/shard_map/ppermute | solution.py:186
  57.0 25.6 %collective-permute-start.15 = (f32[16,128,128]{2,1,0:T(8,128)}, f32[16,128,128]{2,1,0:T(8,128)}, u32[]{:S(2)}, u32[]{:S(2)}) collective-permute-start(f32[16,128,128]{2,1,0:T(8,128)} %get-tuple-element.32.refs_6_), channel_id=1, source_target_pairs={{0,8},{8,16},{16,24},{24,0},{1,9},{9,17},{17,25},{25,1},{2,10},{10... | collective-permute-start | bytes 3145736 | tf_op jit(solution)/shard_map/ppermute | solution.py:186
  57.2 25.4 %collective-permute-start.17 = (f32[16,128,128]{2,1,0:T(8,128)}, f32[16,128,128]{2,1,0:T(8,128)}, u32[]{:S(2)}, u32[]{:S(2)}) collective-permute-start(f32[16,128,128]{2,1,0:T(8,128)} %get-tuple-element.32.refs_6_), channel_id=1, source_target_pairs={{0,4},{4,0},{1,5},{5,1},{2,6},{6,2},{3,7},{7,3},{8,12},{12,8},{9,1... | collective-permute-start | bytes 3145736 | tf_op jit(solution)/shard_map/ppermute | solution.py:186
  58.2 24.4 %collective-permute-start.16 = (f32[16,128,128]{2,1,0:T(8,128)}, f32[16,128,128]{2,1,0:T(8,128)}, u32[]{:S(2)}, u32[]{:S(2)}) collective-permute-start(f32[16,128,128]{2,1,0:T(8,128)} %get-tuple-element.33.refs_8_), channel_id=1, source_target_pairs={{0,24},{8,0},{16,8},{24,16},{1,25},{9,1},{17,9},{25,17},{2,26},{10... | collective-permute-start | bytes 3145736 | tf_op jit(solution)/shard_map/ppermute | solution.py:186
  77.9 25.1 %collective-permute-start.3 = (f32[16,128,128]{2,1,0:T(8,128)}, f32[16,128,128]{2,1,0:T(8,128)S(1)}, u32[]{:S(2)}, u32[]{:S(2)}) collective-permute-start(f32[16,128,128]{2,1,0:T(8,128)} %collective-permute-done.2.refs_0_.refs_15_), channel_id=1, source_target_pairs={{0,32},{32,64},{64,96},{96,128},{128,160},{160,192},{192,224},{224... | collective-permute-start | bytes 3145736 | tf_op jit(solution)/shard_map/ppermute | solution.py:186
  78.4 25.1 %collective-permute-start.6 = (f32[16,128,128]{2,1,0:T(8,128)S(1)}, f32[16,128,128]{2,1,0:T(8,128)S(1)}, u32[]{:S(2)}, u32[]{:S(2)}) collective-permute-start(f32[16,128,128]{2,1,0:T(8,128)S(1)} %collective-permute-done.5.refs_1_.refs_16_), channel_id=1, source_target_pairs={{0,224},{32,0},{64,32},{96,64},{128,96},{160,128},{192,160},{224,1... | collective-permute-start | bytes 3145736 | tf_op jit(solution)/shard_map/ppermute | solution.py:186
  83.8 3.1 %copy-start.2 = (f32[16,128,128]{2,1,0:T(8,128)S(1)}, f32[16,128,128]{2,1,0:T(8,128)}, u32[]{:S(2)}) copy-start(f32[16,128,128]{2,1,0:T(8,128)} %copy-done.1) | copy-start | bytes 3145732
  85.2 17.7 %collective-permute-start.21 = (f32[16,128,128]{2,1,0:T(8,128)S(1)}, f32[16,128,128]{2,1,0:T(8,128)S(1)}, u32[]{:S(2)}, u32[]{:S(2)}) collective-permute-start(f32[16,128,128]{2,1,0:T(8,128)S(1)} %broadcast_select_fusion), channel_id=1, source_target_pairs={{0,8},{2,26},{8,16},{10,2},{16,24},{18,10},{24,0},{26,18},{1,9},{3... | collective-permute-start | bytes 3145736 | tf_op jit(solution)/shard_map/ppermute | solution.py:192
  86.3 20.1 %collective-permute-start.19 = (f32[16,128,128]{2,1,0:T(8,128)}, f32[16,128,128]{2,1,0:T(8,128)S(1)}, u32[]{:S(2)}, u32[]{:S(2)}) collective-permute-start(f32[16,128,128]{2,1,0:T(8,128)} %get-tuple-element.42.refs_5_), channel_id=1, source_target_pairs={{0,2},{2,0},{1,3},{3,1},{4,6},{6,4},{5,7},{7,5},{8,10},{10,8},{9,1... | collective-permute-start | bytes 3145736 | tf_op jit(solution)/shard_map/ppermute | solution.py:186
  86.4 20.0 %collective-permute-start.20 = (f32[16,128,128]{2,1,0:T(8,128)}, f32[16,128,128]{2,1,0:T(8,128)S(1)}, u32[]{:S(2)}, u32[]{:S(2)}) collective-permute-start(f32[16,128,128]{2,1,0:T(8,128)} %get-tuple-element.43.refs_7_), channel_id=1, source_target_pairs={{0,2},{2,0},{1,3},{3,1},{4,6},{6,4},{5,7},{7,5},{8,10},{10,8},{9,1... | collective-permute-start | bytes 3145736 | tf_op jit(solution)/shard_map/ppermute | solution.py:186
  103.0 3.4 %collective-permute-start.18 = (f32[16,128,128]{2,1,0:T(8,128)}, f32[16,128,128]{2,1,0:T(8,128)S(1)}, u32[]{:S(2)}, u32[]{:S(2)}) collective-permute-start(f32[16,128,128]{2,1,0:T(8,128)} %get-tuple-element.41.refs_3_), channel_id=1, source_target_pairs={{0,2},{2,0},{1,3},{3,1},{4,6},{6,4},{5,7},{7,5},{8,10},{10,8},{9,1... | collective-permute-start | bytes 3145736 | tf_op jit(solution)/shard_map/ppermute | solution.py:186
  103.0 4.2 %copy-start.3 = (f32[16,128,128]{2,1,0:T(8,128)}, f32[16,128,128]{2,1,0:T(8,128)S(1)}, u32[]{:S(2)}) copy-start(f32[16,128,128]{2,1,0:T(8,128)S(1)} %collective-permute-done.21.refs_9_) | copy-start | bytes 3145732
  103.0 4.1 %collective-permute-start.22 = (f32[16,128,128]{2,1,0:T(8,128)S(1)}, f32[16,128,128]{2,1,0:T(8,128)S(1)}, u32[]{:S(2)}, u32[]{:S(2)}) collective-permute-start(f32[16,128,128]{2,1,0:T(8,128)S(1)} %collective-permute-done.21.refs_9_), channel_id=1, source_target_pairs={{0,2},{2,0},{1,3},{3,1},{4,6},{6,4},{5,7},{7,5},{8,10},{10,8},{9,1... | collective-permute-start | bytes 3145736 | tf_op jit(solution)/shard_map/ppermute | solution.py:186
  103.6 16.2 %collective-permute-start.7 = (f32[16,128,128]{2,1,0:T(8,128)S(1)}, f32[16,128,128]{2,1,0:T(8,128)S(1)}, u32[]{:S(2)}, u32[]{:S(2)}) collective-permute-start(f32[16,128,128]{2,1,0:T(8,128)S(1)} %broadcast_select_fusion.1), channel_id=1, source_target_pairs={{0,32},{2,226},{32,64},{34,2},{64,96},{66,34},{96,128},{98,66},{12... | collective-permute-start | bytes 3145736 | tf_op jit(solution)/shard_map/ppermute | solution.py:192
  106.4 1.0 copy-start.6
  106.4 1.3 copy-start.4
  106.4 1.6 %copy-start.5 = (f32[16,128,128]{2,1,0:T(8,128)}, f32[16,128,128]{2,1,0:T(8,128)S(1)}, u32[]{:S(2)}) copy-start(f32[16,128,128]{2,1,0:T(8,128)S(1)} %collective-permute-done.20.refs_8_) | copy-start | bytes 3145732
  107.1 1.2 copy-start.7
  121.4 25.1 %collective-permute-start.23 = (f32[8,128,128]{2,1,0:T(8,128)S(1)}, f32[8,128,128]{2,1,0:T(8,128)S(1)}, u32[]{:S(2)}, u32[]{:S(2)}) collective-permute-start(f32[8,128,128]{2,1,0:T(8,128)S(1)} %slice.29), channel_id=1, source_target_pairs={{0,1},{1,0},{2,3},{3,2},{4,5},{5,4},{6,7},{7,6},{8,9},{9,8},{10,11... | collective-permute-start | bytes 1572872 | tf_op jit(solution)/shard_map/ppermute | solution.py:186
  124.5 21.9 %collective-permute-start.24 = (f32[8,128,128]{2,1,0:T(8,128)S(1)}, f32[8,128,128]{2,1,0:T(8,128)S(1)}, u32[]{:S(2)}, u32[]{:S(2)}) collective-permute-start(f32[8,128,128]{2,1,0:T(8,128)S(1)} %slice.30), channel_id=1, source_target_pairs={{0,1},{1,0},{2,3},{3,2},{4,5},{5,4},{6,7},{7,6},{8,9},{9,8},{10,11... | collective-permute-start | bytes 1572872 | tf_op jit(solution)/shard_map/ppermute | solution.py:186
